TPU v7x, 128 devices: a whole 4x4x4 slice. The times are simulated.
128 devices in a mesh: px: 8 (over y, core), py: 16 (over x, z).
Axes of the slice: x: 4, y: 4, z: 4, core: 2. Of those that a mesh axis runs over, the one named last changes fastest.
Arguments:
- checkpoint_field: float32 [32, 128, 1024], P('px', 'py'), may hold values from -6 to 6
- checkpoint_memory: float32 [4, 32, 128, 1024], P(None, 'px', 'py'), may hold values from -3 to 3
- stiffness: bfloat16 [32, 128, 64, 512], P('px', 'py'), may hold values from -0.25 to 0.25
- block_offsets: int32 [32, 128, 8], P('px', 'py'), may hold values from 0 to 8, as said below
- chargeability: float32 [32, 128, 64], P('px', 'py'), may hold values from 0.05 to 0.5
- relaxation: float32 [4, 32, 128, 64], P(None, 'px', 'py'), may hold values from 0.2 to 0.95
- observed: float32 [32768, 128], P(('px', 'py')), may hold values from -6 to 6
- receiver_part: int32 [32768, 1], P(('px', 'py')), may hold values from 0 to 127; in each aligned block of 256 rows (0 to 255, 256 to 511, ...) at most 8 rows name the same one
- receiver_node: int32 [32768], P(('px', 'py')), may hold values from 0 to 2047
- gate_step: int32 [8], replicated, may hold values from 1 to 4
Outputs:
- adjoint_field: float32 [32, 128, 1024], P('px', 'py')
- charge_gradient: float32 [32, 128, 64], P('px', 'py')
Inputs may be any that keep to these rules, and one draw needn't show every extreme that they name: `block_offsets`: each block row lists its own block (code 4) first and then 8 - 1 further distinct neighbour codes. `receiver_part`: within the 256 receivers of one owner (aligned blocks of rows) no partition is named more than 8 times, a bound that some block reaches.
All inputs are finite; a program needn't handle non-finite values.
Results may differ from a plain program's by a relative error of at most 0.0095.
Values may be sent and summed in bfloat16 or wider, within the bound.
No kernel may reach another device: no remote copies, remote signals or barrier semaphores. Data moves between devices by JAX's collectives and lax.ppermute only.
A program may use at most 128 MiB of HBM per device.

v0:
```python
import jax
import jax.numpy as jnp
from jax import lax
from jax.experimental import pallas as pl
from jax.experimental.pallas import tpu as pltpu
from jax.sharding import PartitionSpec as P

ROWS, COLS = 4, 8
OWN = ROWS * COLS
CAP = 8
WIDE = COLS + 4
PLACES = (ROWS + 4) * WIDE
F32, BF16 = jnp.float32, jnp.bfloat16
VMEM_BYTES = 24 * 1024 * 1024


def place(row, col):
    return (row + 2) * WIDE + col + 2


def low_lanes(rows):
    return lax.broadcasted_iota(jnp.int32, (rows, 128), 1) < 64


def doubled(plain):
    turned = pltpu.roll(plain, 64, 1)
    low = low_lanes(8)
    return jnp.concatenate([jnp.where(low, plain, turned), jnp.where(low, turned, plain)], 0)


def packed(plain):
    return jnp.concatenate([plain[:, :64], plain[:, 64:]], 0)


def unpacked(rows):
    return jnp.concatenate([rows[:8], rows[8:]], 1)


def halves(plain):
    high = plain.astype(BF16).astype(F32)
    return jnp.concatenate([high, plain - high], 0).astype(BF16)


def joined(pair):
    pair = pair.astype(F32)
    return pair[:8] + pair[8:]


def sides(par_ref, axis, near, far):
    even = par_ref[axis] == 0
    return jnp.where(even, near, far), jnp.where(even, far, near)


def call(kernel, out, inputs, scalars=0, scratch=(), flops=0):
    smem = pl.BlockSpec(memory_space=pltpu.SMEM)
    vmem = pl.BlockSpec(memory_space=pltpu.VMEM)
    moved = sum(a.size * a.dtype.itemsize for a in inputs)
    return pl.pallas_call(
        kernel,
        out_shape=[jax.ShapeDtypeStruct(s, d) for s, d in out],
        in_specs=[smem] * scalars + [vmem] * (len(inputs) - scalars),
        out_specs=[vmem] * len(out),
        scratch_shapes=list(scratch),
        compiler_params=pltpu.CompilerParams(vmem_limit_bytes=VMEM_BYTES),
        cost_estimate=pl.CostEstimate(flops=flops, bytes_accessed=moved, transcendentals=0),
    )(*inputs)


PLAIN = ((OWN, 8, 128), F32)


def to_plain(native, scratch, out):
    for x in range(ROWS):
        for r in range(8):
            scratch[pl.ds(x * 64 + r * 8, 8), :] = native(x, r)
    for x in range(ROWS):
        for y in range(COLS):
            out[x * COLS + y] = scratch[pl.ds(x * 64 + y, 8, stride=8), :]


def lanes(r):
    return pl.ds(r * 128, 128)


def twice(rows):
    return jnp.concatenate([rows, rows], 1)


def px_message(par_ref, plain, addend, outs):
    bases = sides(par_ref, 0, 2, 0)
    edges = sides(par_ref, 0, 3, 0)
    for out, base, edge in zip(outs, bases, edges):
        for k in range(2):
            for p in range(4):
                at = (base + k) * COLS + 2 * p
                out[k * 4 + p] = jnp.concatenate([plain[at], plain[at + 1]], 0).astype(BF16)
        for y in range(COLS):
            out[8 + y] = halves(addend[edge * COLS + y])


def start_kernel(par, field, memory, charge, plain, addend, summed, m_even, m_odd, scratch):
    terms = memory.shape[0]
    to_plain(lambda x, r: field[x, :, lanes(r)], scratch, plain)

    def total(x, r):
        acc = memory[0, x, :, lanes(r)]
        for q in range(1, terms):
            acc = acc + memory[q, x, :, lanes(r)]
        return acc

    to_plain(total, scratch, summed)
    wide = [twice(charge[x]) for x in range(ROWS)]
    for x in range(ROWS):
        for r in range(8):
            at = pl.ds(x * 64 + r * 8, 8)
            scratch[at, :] = scratch[at, :] * (-wide[x])
    for x in range(ROWS):
        for y in range(COLS):
            addend[x * COLS + y] = scratch[pl.ds(x * 64 + y, 8, stride=8), :]
    px_message(par, plain, addend, (m_even, m_odd))


def decay_kernel(field, memory, charge, relaxation, sum1, sum2, sum3, coef, scratch):
    terms = memory.shape[0]
    for x in range(ROWS):
        rates = [twice(relaxation[q, x]) for q in range(terms)]
        w0 = w1 = w2 = 0.0
        for rate in rates:
            w0 = w0 + (1.0 - rate)
            w1 = w1 + rate * (1.0 - rate)
            w2 = w2 + rate * rate * (1.0 - rate)
        for j, value in enumerate((twice(charge[x]), w0, w1, w2)):
            coef[j, pl.ds(x * COLS, COLS), :] = value
    for power, out in ((1, sum1), (2, sum2), (3, sum3)):
        scale = []
        for x in range(ROWS):
            row = []
            for q in range(terms):
                rate = twice(relaxation[q, x])
                row.append(rate if power == 1 else rate * rate if power == 2 else rate * rate * rate)
            scale.append(row)

        def part(x, r):
            acc = coef[power, pl.ds(x * COLS, COLS), :] * field[x, :, lanes(r)]
            for q in range(terms):
                acc = acc + scale[x][q] * memory[q, x, :, lanes(r)]
            return acc

        to_plain(part, scratch, out)


def py_kernel(par, plain, addend, r_even, r_odd, n_even, n_odd):
    pairs = sides(par, 1, 3, 0)
    edges = sides(par, 1, 7, 0)
    for out, pair, edge in zip((n_even, n_odd), pairs, edges):
        for x in range(ROWS):
            at = x * COLS + 2 * pair
            out[x] = jnp.concatenate([plain[at], plain[at + 1]], 0).astype(BF16)
            out[8 + x] = halves(addend[x * COLS + edge])
        for k in range(2):
            out[4 + k] = r_even[k * 4 + pair]
            out[6 + k] = r_odd[k * 4 + pair]
        out[12] = r_even[8 + edge]
        out[13] = r_odd[8 + edge]


def outer_places(par):
    row_even, row_odd = sides(par, 0, ROWS, -1)
    col_even, col_odd = sides(par, 1, COLS, -1)
    listed = []
    for array, row in ((0, row_even), (1, row_odd)):
        listed += [(array, y, place(row, y)) for y in range(COLS)]
    rows = [0, 1, 2, 3, row_even, row_odd]
    for array, col in ((2, col_even), (3, col_odd)):
        listed += [(array, j, place(row, col)) for j, row in enumerate(rows)]
    return listed


def weight_of(blocks, item):
    own, outer = blocks
    if item < OWN:
        return own[item // COLS, item % COLS]
    item -= OWN
    for array, count in zip(outer, (COLS, COLS, ROWS + 2, ROWS + 2)):
        if item < count:
            return array[item]
        item -= count


def forward_pair(par, table, blocks, plain, received, addend, field, middle, store_first, store_second):
    low = low_lanes(16)
    r_even, r_odd, n_even, n_odd = received
    for block in range(OWN):
        field[place(block // COLS, block % COLS)] = doubled(plain[block]).astype(BF16)

    def spread(pair, first, second):
        both = pair.astype(F32)
        field[first] = doubled(both[:8]).astype(BF16)
        field[second] = doubled(both[8:]).astype(BF16)

    row_bases = sides(par, 0, ROWS, -2)
    col_bases = sides(par, 1, COLS, -2)
    for msg, base in zip((r_even, r_odd), row_bases):
        for k in range(2):
            for p in range(4):
                at = place(base + k, 2 * p)
                spread(msg[k * 4 + p], at, at + 1)
    rows = [0, 1, 2, 3, row_bases[0], row_bases[0] + 1, row_bases[1], row_bases[1] + 1]
    for msg, base in zip((n_even, n_odd), col_bases):
        for j, row in enumerate(rows):
            at = place(row, base)
            spread(msg[j], at, at + 1)

    def product(source, item):
        parts = []
        for m in range(4):
            one = source[table[item * 8 + 2 * m]]
            two = source[table[item * 8 + 2 * m + 1]]
            parts.append(jnp.where(low, one, two))
        picked = jnp.concatenate(parts, 1)
        out = lax.dot_general(
            picked, weight_of(blocks, item), (((1,), (1,)), ((), ())), preferred_element_type=F32
        )
        return unpacked(out)

    outer = outer_places(par)
    for number, (array, index, at) in enumerate(outer):
        got = product(field, OWN + number) + joined(received[array][8 + index])
        middle[at] = doubled(got).astype(BF16)
    for block in range(OWN):
        got = store_first(block, product(field, block))
        middle[place(block // COLS, block % COLS)] = doubled(got).astype(BF16)
    for block in range(OWN):
        store_second(block, product(middle, block))


def forward_one(
    par, table, own, a_even, a_odd, b_even, b_odd, plain, addend, r_even, r_odd, n_even, n_odd, sum1, sum2, sum3, coef,
    field1, field2, addend2, full2, full3, m_even, m_odd, field, middle,
):
    def row(j, block):
        return coef[j, pl.ds(block, 1), :]

    def first(block, out):
        got = out + addend[block]
        field1[block] = got
        full = sum2[block] + row(1, block) * got
        full2[block] = full
        addend2[block] = -row(0, block) * full
        return got

    def second(block, out):
        got = out - row(0, block) * sum1[block]
        field2[block] = got

    forward_pair(
        par, table, (own, (a_even, a_odd, b_even, b_odd)), plain, (r_even, r_odd, n_even, n_odd), addend,
        field, middle, first, second,
    )
    px_message(par, field2, addend2, (m_even, m_odd))
    for block in range(OWN):
        full3[block] = sum3[block] + row(2, block) * field1[block] + row(1, block) * field2[block]


def forward_two(
    par, table, own, a_even, a_odd, b_even, b_odd, plain, addend, r_even, r_odd, n_even, n_odd, full3, coef,
    field3, field4, field, middle,
):
    def first(block, out):
        got = out + addend[block]
        field3[block] = got
        return got

    def second(block, out):
        field4[block] = out - coef[0, pl.ds(block, 1), :] * full3[block]

    forward_pair(
        par, table, (own, (a_even, a_odd, b_even, b_odd)), plain, (r_even, r_odd, n_even, n_odd), addend,
        field, middle, first, second,
    )


def adjoint_pair(par, table, blocks, start, add_first, add_second, outs, middle, last):
    first_out, second_out, m_even, m_odd = outs
    low = low_lanes(16)
    zero = jnp.zeros((16, 128), F32)
    for at in range(PLACES):
        middle[at] = zero
        last[at] = zero

    def push(target, item, rows):
        out = lax.dot_general(
            rows, weight_of(blocks, item), (((1,), (0,)), ((), ())), preferred_element_type=F32
        )
        spots = [table[item * 8 + k] for k in range(8)]
        sums = []
        for k in range(8):
            part = out[:, (k // 2) * 128 : (k // 2 + 1) * 128]
            part = jnp.where(low, part, 0.0) if k % 2 == 0 else jnp.where(low, 0.0, part)
            sums.append(target[spots[k]] + part)
        for k in range(8):
            target[spots[k]] = sums[k]

    def both(target, at):
        value = target[at]
        return value + pltpu.roll(value, 64, 1)

    def plain_of(value):
        return jnp.where(low_lanes(8), value[:8], value[8:])

    for block in range(OWN):
        push(middle, block, packed(start(block)).astype(BF16))
    rows_at = sides(par, 0, ROWS, -1)
    for number, (array, index, at) in enumerate(outer_places(par)):
        value = both(middle, at)
        push(last, OWN + number, value[:, :64].astype(BF16))
    for out, row in zip((m_even, m_odd), rows_at):
        for j in range(COLS + 2):
            out[j] = plain_of(both(middle, place(row, j - 1)))
    for x in range(ROWS):
        for j in range(COLS + 2):
            value = plain_of(both(middle, place(x, j - 1)))
            if 1 <= j <= COLS:
                block = x * COLS + j - 1
                value = value + add_first(block)
                push(last, block, packed(value).astype(BF16))
            first_out[x * (COLS + 2) + j] = value
    for out, base in zip((m_even, m_odd), sides(par, 0, ROWS, -2)):
        for k in range(2):
            for j in range(WIDE):
                out[COLS + 2 + k * WIDE + j] = plain_of(both(last, place(base + k, j - 2)))
    for x in range(ROWS):
        for j in range(WIDE):
            value = plain_of(both(last, place(x, j - 2)))
            if 2 <= j < COLS + 2:
                value = value + add_second(x * COLS + j - 2)
            second_out[x * WIDE + j] = value


def adjoint_py_kernel(par, first, second, r_even, r_odd, first_own, second_own, n_even, n_odd, one, two):
    one[...] = first[...]
    two[...] = second[...]
    for msg, row, base in zip((r_even, r_odd), sides(par, 0, 3, 0), sides(par, 0, 2, 0)):
        for j in range(COLS + 2):
            one[row * (COLS + 2) + j] += msg[j]
        for k in range(2):
            for j in range(WIDE):
                two[(base + k) * WIDE + j] += msg[COLS + 2 + k * WIDE + j]
    for out, col, base in zip((n_even, n_odd), sides(par, 1, COLS + 1, 0), sides(par, 1, COLS + 2, 0)):
        for x in range(ROWS):
            out[x] = one[x * (COLS + 2) + col]
            for k in range(2):
                out[ROWS + 2 * x + k] = two[x * WIDE + base + k]
    for x in range(ROWS):
        for y in range(COLS):
            first_own[x * COLS + y] = one[x * (COLS + 2) + 1 + y]
            second_own[x * COLS + y] = two[x * WIDE + 2 + y]


def settle(par, first_own, second_own, n_even, n_odd, first, second):
    first[...] = first_own[...]
    second[...] = second_own[...]
    for msg, col, base in zip((n_even, n_odd), sides(par, 1, 7, 0), sides(par, 1, 6, 0)):
        for x in range(ROWS):
            first[x * COLS + col] += msg[x]
            for k in range(2):
                second[x * COLS + base + k] += msg[ROWS + 2 * x + k]


def injected(tally, moment, counted, field, spread, block):
    return tally[moment] * counted[block] * field[block] - spread[moment - 1, block]


def adjoint_one(
    par, table, tally, own, a_even, a_odd, b_even, b_odd, field2, field3, field4, counted, spread, coef,
    adjoint4, first_out, second_out, m_even, m_odd, middle, last,
):
    def start(block):
        value = injected(tally, 4, counted, field4, spread, block)
        adjoint4[block] = value
        return value

    def add_first(block):
        return injected(tally, 3, counted, field3, spread, block)

    def add_second(block):
        memory = coef[0, pl.ds(block, 1), :] * coef[1, pl.ds(block, 1), :] * adjoint4[block]
        return injected(tally, 2, counted, field2, spread, block) - memory

    adjoint_pair(
        par, table, (own, (a_even, a_odd, b_even, b_odd)), start, add_first, add_second,
        (first_out, second_out, m_even, m_odd), middle, last,
    )


def adjoint_two(
    par, table, tally, own, a_even, a_odd, b_even, b_odd, first_own, second_own, n_even, n_odd, adjoint4, field1, counted,
    spread, coef, adjoint3, adjoint2, first_out, second_out, m_even, m_odd, middle, last,
):
    settle(par, first_own, second_own, n_even, n_odd, adjoint3, adjoint2)

    def row(j, block):
        return coef[j, pl.ds(block, 1), :]

    def add_first(block):
        memory = row(2, block) * adjoint4[block] + row(1, block) * adjoint3[block]
        return injected(tally, 1, counted, field1, spread, block) - row(0, block) * memory

    def add_second(block):
        memory = row(3, block) * adjoint4[block] + row(2, block) * adjoint3[block] + row(1, block) * adjoint2[block]
        return -row(0, block) * memory

    adjoint_pair(
        par, table, (own, (a_even, a_odd, b_even, b_odd)), lambda block: adjoint2[block], add_first, add_second,
        (first_out, second_out, m_even, m_odd), middle, last,
    )


def finish_kernel(
    par, first_own, second_own, n_even, n_odd, adjoint4, adjoint3, adjoint2, sum0, sum1, sum2, sum3,
    result, gradient, adjoint1, adjoint0, scratch,
):
    settle(par, first_own, second_own, n_even, n_odd, adjoint1, adjoint0)
    for x in range(ROWS):
        parts = []
        for y in range(COLS):
            block = x * COLS + y
            scratch[pl.ds(x * 64 + y * 8, 8), :] = adjoint0[block]
            value = (
                adjoint4[block] * sum3[block] + adjoint3[block] * sum2[block]
                + adjoint2[block] * sum1[block] + adjoint1[block] * sum0[block]
            )
            parts.append(jnp.sum(value, axis=0, keepdims=True))
        rows = jnp.concatenate(parts, 0)
        gradient[x] = -(rows[:, :64] + rows[:, 64:])
        for r in range(8):
            result[x, :, lanes(r)] = scratch[pl.ds(x * 64 + r, 8, stride=8), :]


def split(value):
    high = value.astype(BF16)
    return high, (value - high.astype(F32)).astype(BF16)


def owner_kernel(steps, observed, part, node, out):
    owned = observed.shape[0]
    slots = out.shape[0]
    devices = slots // CAP
    row = lax.broadcasted_iota(jnp.int32, (128, 128), 0)
    col = lax.broadcasted_iota(jnp.int32, (128, 128), 1)
    gate = row // 16
    source = row % 16
    step = jnp.zeros((128, 128), jnp.int32)
    for g in range(8):
        step = jnp.where(gate == g, steps[g], step)
    wanted = 2 * (col % 8) + (col // 8) % 2
    chosen = ((step == col // 16 + 1) & (source == wanted) & (col < 64)).astype(F32).astype(BF16)
    high, low = split(observed[...])
    dot = lambda a, b: lax.dot_general(a, b, (((1,), (0,)), ((), ())), preferred_element_type=F32)
    sums = dot(high, chosen) + dot(low, chosen)
    dest = part[...]
    member = (dest == lax.broadcasted_iota(jnp.int32, (owned, devices), 1)).astype(F32)
    earlier = (
        lax.broadcasted_iota(jnp.int32, (owned, owned), 0) > lax.broadcasted_iota(jnp.int32, (owned, owned), 1)
    ).astype(F32).astype(BF16)
    ahead = dot(earlier, member.astype(BF16))
    rank = jnp.sum(ahead * member, axis=1, keepdims=True).astype(jnp.int32)
    position = dest * CAP + rank
    where = (position == lax.broadcasted_iota(jnp.int32, (owned, slots), 1)).astype(F32).astype(BF16)
    lane = lax.broadcasted_iota(jnp.int32, (owned, 128), 1)
    which = node[...]
    block = (which // 64).astype(F32)
    inner = (which % 64).astype(F32)
    marks = jnp.where(lane == 64, block, jnp.where(lane == 65, inner, jnp.where(lane == 66, 1.0, 0.0)))
    high, low = split(jnp.where(lane < 64, sums, marks))
    turned = lambda a, b: lax.dot_general(a, b, (((0,), (0,)), ((), ())), preferred_element_type=F32)
    out[...] = turned(where, high) + turned(where, low)


def holder_kernel(slots, spread, counted):
    values = slots[...]
    count = values.shape[0]
    lane = lax.broadcasted_iota(jnp.int32, (count, 128), 1)
    pick = lambda at: jnp.sum(jnp.where(lane == at, values, 0.0), axis=1, keepdims=True)
    place_of = jnp.where(pick(66) > 0.5, pick(64) * 64.0 + pick(65), -1.0).astype(jnp.int32)
    high, low = split(values.T)
    both = jnp.concatenate([high, low], 0)
    low8 = low_lanes(8)
    for chunk in range(OWN * 64 // 256):
        spots = lax.broadcasted_iota(jnp.int32, (count, 256), 1) + chunk * 256
        hot = (place_of == spots).astype(F32).astype(BF16)
        out = lax.dot_general(both, hot, (((1,), (0,)), ((), ())), preferred_element_type=F32)
        out = out[:128] + out[128:]
        for j in range(2):
            first = chunk * 4 + 2 * j
            for n in range(4):
                even = out[n * 16 : n * 16 + 8, j * 128 : (j + 1) * 128]
                odd = out[n * 16 + 8 : n * 16 + 16, j * 128 : (j + 1) * 128]
                spread[n, first] = jnp.where(low8, even, pltpu.roll(odd, 64, 1))
                spread[n, first + 1] = jnp.where(low8, pltpu.roll(even, 64, 1), odd)
            many = jnp.broadcast_to(out[66:67, j * 128 : (j + 1) * 128], (8, 128))
            other = pltpu.roll(many, 64, 1)
            counted[first] = jnp.where(low8, many, other)
            counted[first + 1] = jnp.where(low8, other, many)


def swap_even(axis):
    return [(i, i ^ 1) for i in range(lax.axis_size(axis))]


def swap_odd(axis):
    inner = range(1, lax.axis_size(axis) - 1, 2)
    return [(i, i + 1) for i in inner] + [(i + 1, i) for i in inner]


def exchange(axis, for_even, for_odd):
    return lax.ppermute(for_even, axis, swap_even(axis)), lax.ppermute(for_odd, axis, swap_odd(axis))


def edge(array, par, dim, last):
    at = jnp.where(par == 0, last, 0)
    even = lax.dynamic_index_in_dim(array, at, dim, keepdims=False)
    return even, lax.dynamic_index_in_dim(array, last - at, dim, keepdims=False)


def with_corners(array, outer, par):
    sides_own = edge(array, par, 1, COLS - 1)
    ends = [edge(one, par, 0, COLS - 1) for one in outer]
    return tuple(
        jnp.concatenate([own, ends[0][k][None], ends[1][k][None]], 0) for k, own in enumerate(sides_own)
    )


def target_table(offsets, outer, par):
    row_even = jnp.where(par[0] == 0, ROWS, -1)
    row_odd = ROWS - 1 - row_even
    col_even = jnp.where(par[1] == 0, COLS, -1)
    col_odd = COLS - 1 - col_even
    along = jnp.arange(COLS, dtype=jnp.int32)
    down = jnp.concatenate([jnp.arange(ROWS, dtype=jnp.int32), jnp.stack([row_even, row_odd]).astype(jnp.int32)])
    own = place(jnp.arange(ROWS, dtype=jnp.int32)[:, None], along[None, :]).reshape(-1)
    spots = jnp.concatenate(
        [own, place(row_even, along), place(row_odd, along), place(down, col_even), place(down, col_odd)]
    )
    codes = jnp.concatenate([offsets.reshape(OWN, -1)] + list(outer), 0)
    shift = (codes // 3 - 1) * WIDE + codes % 3 - 1
    return (spots[:, None] + shift).reshape(-1).astype(jnp.int32)


def body(
    checkpoint_field,
    checkpoint_memory,
    stiffness,
    block_offsets,
    chargeability,
    relaxation,
    observed,
    receiver_part,
    receiver_node,
    gate_step,
):
    devices = lax.axis_size(("px", "py"))
    slots = devices * CAP
    par = jnp.stack([lax.axis_index("px") % 2, lax.axis_index("py") % 2]).astype(jnp.int32)
    column = ((256, 128), F32)
    places = pltpu.VMEM((PLACES, 16, 128), BF16)
    sums = pltpu.VMEM((PLACES, 16, 128), F32)
    px_shape = ((16, 16, 128), BF16)
    py_shape = ((14, 16, 128), BF16)
    plain, addend, sum0, m_even, m_odd = call(
        start_kernel, [PLAIN, PLAIN, PLAIN, px_shape, px_shape],
        [par, checkpoint_field, checkpoint_memory, chargeability], 1, [pltpu.VMEM(*column)],
    )
    r_even, r_odd = exchange("px", m_even, m_odd)
    a_even, a_odd = exchange("px", *edge(stiffness, par[0], 0, ROWS - 1))
    o_even, o_odd = exchange("px", *edge(block_offsets, par[0], 0, ROWS - 1))
    n_even, n_odd = call(
        py_kernel, [py_shape, py_shape], [par, plain, addend, r_even, r_odd], 1
    )
    n_even, n_odd = exchange("py", n_even, n_odd)
    b_even, b_odd = exchange("py", *with_corners(stiffness, (a_even, a_odd), par[1]))
    c_even, c_odd = exchange("py", *with_corners(block_offsets, (o_even, o_odd), par[1]))
    table = target_table(block_offsets, (o_even, o_odd, c_even, c_odd), par)
    (sent,) = call(
        owner_kernel, [((slots, 128), F32)],
        [gate_step, observed, receiver_part, receiver_node[:, None]], 1,
    )
    held = lax.all_to_all(
        sent.reshape(devices, CAP, 128), ("px", "py"), split_axis=0, concat_axis=0, tiled=True
    ).reshape(slots, 128)
    tally = jnp.sum(gate_step[None, :] == jnp.arange(5, dtype=jnp.int32)[:, None], axis=1).astype(F32)
    sum1, sum2, sum3, coef = call(
        decay_kernel, [PLAIN, PLAIN, PLAIN, ((4, OWN, 128), F32)],
        [checkpoint_field, checkpoint_memory, chargeability, relaxation], 0, [pltpu.VMEM(*column)],
    )
    spread, counted = call(holder_kernel, [((4, OWN, 8, 128), F32), PLAIN], [held])
    weights = [stiffness, a_even, a_odd, b_even, b_odd]
    field1, field2, addend2, sum2, sum3, m_even, m_odd = call(
        forward_one, [PLAIN] * 5 + [px_shape, px_shape],
        [par, table] + weights + [plain, addend, r_even, r_odd, n_even, n_odd, sum1, sum2, sum3, coef],
        2, [places, places],
    )
    r_even, r_odd = exchange("px", m_even, m_odd)
    n_even, n_odd = call(py_kernel, [py_shape, py_shape], [par, field2, addend2, r_even, r_odd], 1)
    n_even, n_odd = exchange("py", n_even, n_odd)
    field3, field4 = call(
        forward_two, [PLAIN, PLAIN],
        [par, table] + weights + [field2, addend2, r_even, r_odd, n_even, n_odd, sum3, coef],
        2, [places, places],
    )
    pair_out = [
        ((ROWS * (COLS + 2), 8, 128), F32), ((ROWS * WIDE, 8, 128), F32),
        ((COLS + 2 + 2 * WIDE, 8, 128), F32), ((COLS + 2 + 2 * WIDE, 8, 128), F32),
    ]

    def gathered(first, second, m_even, m_odd):
        r_even, r_odd = exchange("px", m_even, m_odd)
        own_first, own_second, n_even, n_odd = call(
            adjoint_py_kernel, [PLAIN, PLAIN, ((12, 8, 128), F32), ((12, 8, 128), F32)],
            [par, first, second, r_even, r_odd], 1,
            [pltpu.VMEM(first.shape, F32), pltpu.VMEM(second.shape, F32)],
        )
        n_even, n_odd = exchange("py", n_even, n_odd)
        return [own_first, own_second, n_even, n_odd]

    adjoint4, *rest = call(
        adjoint_one, [PLAIN] + pair_out,
        [par, table, tally] + weights + [field2, field3, field4, counted, spread, coef], 3, [sums, sums],
    )
    adjoint3, adjoint2, *rest = call(
        adjoint_two, [PLAIN, PLAIN] + pair_out,
        [par, table, tally] + weights + gathered(*rest) + [adjoint4, field1, counted, spread, coef], 3, [sums, sums],
    )
    field_out, gradient = call(
        finish_kernel, [(checkpoint_field.shape, F32), (chargeability.shape, F32)],
        [par] + gathered(*rest) + [adjoint4, adjoint3, adjoint2, sum0, sum1, sum2, sum3], 1,
        [pltpu.VMEM(*PLAIN), pltpu.VMEM(*PLAIN), pltpu.VMEM(*column)],
    )
    return field_out, gradient


def solution(mesh):
    in_specs = (
        P("px", "py", None),
        P(None, "px", "py", None),
        P("px", "py", None, None),
        P("px", "py", None),
        P("px", "py", None),
        P(None, "px", "py", None),
        P(("px", "py"), None),
        P(("px", "py"), None),
        P(("px", "py")),
        P(),
    )
    out_specs = (P("px", "py", None), P("px", "py", None))
    return jax.shard_map(body, mesh=mesh, in_specs=in_specs, out_specs=out_specs, check_vma=False)
```

profile of v0, /device:TPU:10, one launch (start us, length us, event | category | flops | bytes accessed | tf_op | source)
XLA Modules:
  0.0 141.2 jit_solution(9492347883642942833)
XLA Ops:
  8.4 2.3 %shard_map.119 = f32[1024,128]{1,0:T(8,128)} custom-call(s32[8]{0:T(128)S(1)} %copy-done.40, f32[256,128]{1,0:T(8,128)S(1)} %copy-done.26, s32[256,1]{1,0:T(8,128)S(1)} %copy.33.part, s32[256,1]{1,0:T(8,128)S(1)} %copy.34.node), custom_call_target="tpu_custom_call" | custom-call | bytes 133152 | tf_op jit(solution)/shard_map/pallas_call | solution.py:58
  10.7 10.6 %all-to-all-start = ((f32[128,8,128]{2,1,0:T(8,128)}), f32[128,8,128]{2,1,0:T(8,128)}, u32[]{:S(2)}, u32[]{:S(2)}) async-start(f32[128,8,128]{2,1,0:T(8,128)} %bitcast.14), calls=%async_computation | async-start | bytes 1048576 | tf_op jit(solution)/shard_map/all_to_all | solution.py:588
  24.7 2.4 %collective-permute-start.5 = (bf16[8,64,512]{2,1,0:T(8,128)(2,1)}, bf16[8,64,512]{2,1,0:T(8,128)(2,1)S(1)}, u32[]{:S(2)}, u32[]{:S(2)}) collective-permute-start(bf16[8,64,512]{2,1,0:T(8,128)(2,1)} %get-tuple-element.92), channel_id=1, source_target_pairs={{16,32},{48,64},{80,96},{32,16},{64,48},{96,80},{17,33},{49,65},{8... | collective-permute-start | bytes 1572872 | tf_op jit(solution)/shard_map/ppermute | solution.py:517
  36.2 4.2 %collective-permute-start.3 = (s32[6,8]{1,0:T(8,128)S(1)}, s32[6,8]{1,0:T(8,128)S(1)}, u32[]{:S(2)}, u32[]{:S(2)}) collective-permute-start(s32[6,8]{1,0:T(8,128)S(1)} %pad_add_fusion.1), channel_id=1, source_target_pairs={{1,2},{3,4},{5,6},{7,8},{9,10},{11,12},{13,14},{2,1},{4,3},{6,5},{... | collective-permute-start | bytes 584 | tf_op jit(solution)/shard_map/ppermute | solution.py:517
  48.1 4.2 %collective-permute-start.7 = (bf16[6,64,512]{2,1,0:T(8,128)(2,1)}, bf16[6,64,512]{2,1,0:T(8,128)(2,1)}, u32[]{:S(2)}, u32[]{:S(2)}) collective-permute-start(bf16[6,64,512]{2,1,0:T(8,128)(2,1)} %pad_maximum_fusion.1), channel_id=1, source_target_pairs={{1,2},{3,4},{5,6},{7,8},{9,10},{11,12},{13,14},{2,1},{4,3},{6,5},{... | collective-permute-start | bytes 1179656 | tf_op jit(solution)/shard_map/ppermute | solution.py:517
  62.4 2.5 %collective-permute-start.11 = (bf16[14,16,128]{2,1,0:T(8,128)(2,1)S(1)}, bf16[14,16,128]{2,1,0:T(8,128)(2,1)S(1)}, u32[]{:S(2)}, u32[]{:S(2)}) collective-permute-start(bf16[14,16,128]{2,1,0:T(8,128)(2,1)S(1)} %get-tuple-element.50), channel_id=1, source_target_pairs={{1,2},{3,4},{5,6},{7,8},{9,10},{11,12},{13,14},{2,1},{4,3},{6,5},{... | collective-permute-start | bytes 172040 | tf_op jit(solution)/shard_map/ppermute | solution.py:517
  65.6 5.0 %collective-permute-done.11.n_odd = bf16[14,16,128]{2,1,0:T(8,128)(2,1)S(1)} collective-permute-done((bf16[14,16,128]{2,1,0:T(8,128)(2,1)S(1)}, bf16[14,16,128]{2,1,0:T(8,128)(2,1)S(1)}, u32[]{:S(2)}, u32[]{:S(2)}) %collective-permute-start.11) | collective-permute-done | bytes 57376 | tf_op jit(solution)/shard_map/ppermute | solution.py:517
  74.1 3.2 %shard_map.116 = (f32[32,8,128]{2,1,0:T(8,128)S(1)}, f32[32,8,128]{2,1,0:T(8,128)S(1)}, f32[32,8,128]{2,1,0:T(8,128)S(1)}, f32[32,8,128]{2,1,0:T(8,128)S(1)}, f3...) custom-call(s32[2]{0:T(128)S(1)} %pad_add_fusion.2.par, ...), custom_call_target="tpu_custom_call" | custom-call | bytes 4900744 | tf_op jit(solution)/shard_map/pallas_call | solution.py:58
  78.7 2.5 %collective-permute-start.13 = (bf16[16,16,128]{2,1,0:T(8,128)(2,1)S(1)}, bf16[16,16,128]{2,1,0:T(8,128)(2,1)S(1)}, u32[]{:S(2)}, u32[]{:S(2)}) collective-permute-start(bf16[16,16,128]{2,1,0:T(8,128)(2,1)S(1)} %get-tuple-element.58), channel_id=1, source_target_pairs={{16,32},{48,64},{80,96},{32,16},{64,48},{96,80},{17,33},{49,65},{8... | collective-permute-start | bytes 196616 | tf_op jit(solution)/shard_map/ppermute | solution.py:517
  81.2 3.0 %collective-permute-done.13.r_odd = bf16[16,16,128]{2,1,0:T(8,128)(2,1)S(1)} collective-permute-done((bf16[16,16,128]{2,1,0:T(8,128)(2,1)S(1)}, bf16[16,16,128]{2,1,0:T(8,128)(2,1)S(1)}, u32[]{:S(2)}, u32[]{:S(2)}) %collective-permute-start.13) | collective-permute-done | bytes 65568 | tf_op jit(solution)/shard_map/ppermute | solution.py:517
  86.2 2.7 %collective-permute-start.15 = (bf16[14,16,128]{2,1,0:T(8,128)(2,1)}, bf16[14,16,128]{2,1,0:T(8,128)(2,1)}, u32[]{:S(2)}, u32[]{:S(2)}) collective-permute-start(bf16[14,16,128]{2,1,0:T(8,128)(2,1)} %get-tuple-element.60), channel_id=1, source_target_pairs={{1,2},{3,4},{5,6},{7,8},{9,10},{11,12},{13,14},{2,1},{4,3},{6,5},{... | collective-permute-start | bytes 172040 | tf_op jit(solution)/shard_map/ppermute | solution.py:517
  89.0 2.8 %shard_map.120 = (f32[4,32,8,128]{3,2,1,0:T(8,128)S(1)}, f32[32,8,128]{2,1,0:T(8,128)S(1)}) custom-call(f32[1024,128]{1,0:T(8,128)} %bitcast.15.slots), custom_call_target="tpu_custom_call" | custom-call | bytes 524288 | tf_op jit(solution)/shard_map/pallas_call | solution.py:58
  91.9 3.0 %collective-permute-done.15.n_odd = bf16[14,16,128]{2,1,0:T(8,128)(2,1)} collective-permute-done((bf16[14,16,128]{2,1,0:T(8,128)(2,1)}, bf16[14,16,128]{2,1,0:T(8,128)(2,1)}, u32[]{:S(2)}, u32[]{:S(2)}) %collective-permute-start.15) | collective-permute-done | bytes 57376 | tf_op jit(solution)/shard_map/ppermute | solution.py:517
  100.1 3.1 %shard_map.118 = (f32[32,8,128]{2,1,0:T(8,128)S(1)}, f32[32,8,128]{2,1,0:T(8,128)S(1)}) custom-call(s32[2]{0:T(128)S(1)} %pad_add_fusion.2.par, s32[480]{0:T(512)S(1)} %fusion.4.table, bf16[4,8,64,512]{3,2,1,0:T(8,128)(2,1)S(1)} %copy-done, bf16[8,64,512]{2,1,0:T(8,128)(2,1)S(1)} %collective-permute-done.4.a_even, ...), custom_call_target="tpu_custom_call" | custom-call | bytes 4638600 | tf_op jit(solution)/shard_map/pallas_call | solution.py:58
  103.2 3.0 %shard_map.121 = (f32[32,8,128]{2,1,0:T(8,128)S(1)}, f32[40,8,128]{2,1,0:T(8,128)S(1)}, f32[48,8,128]{2,1,0:T(8,128)S(1)}, f32[34,8,128]{2,1,0:T(8,128)S(1)}, f32[34,8,128]{2,1,0:T(8,128)S(1)}) custom-call(s32[2]{0:T(128)S(1)} %pad_add_fusion.2.par, s32[480]{0:T(512)S(1)} %fusion.4.table, f32[5]{0:T(128)S(1)} %convert_element_type.7.tally, ...), custom_call_target="tpu_custom_call" | custom-call | bytes 5048220 | tf_op jit(solution)/shard_map/pallas_call | solution.py:58
  106.3 1.9 %collective-permute-start.17 = (f32[34,8,128]{2,1,0:T(8,128)S(1)}, f32[34,8,128]{2,1,0:T(8,128)S(1)}, u32[]{:S(2)}, u32[]{:S(2)}) collective-permute-start(f32[34,8,128]{2,1,0:T(8,128)S(1)} %get-tuple-element.69), channel_id=1, source_target_pairs={{16,32},{48,64},{80,96},{32,16},{64,48},{96,80},{17,33},{49,65},{8... | collective-permute-start | bytes 417800 | tf_op jit(solution)/shard_map/ppermute | solution.py:517
  108.2 4.4 %collective-permute-done.17.r_odd = f32[34,8,128]{2,1,0:T(8,128)S(1)} collective-permute-done((f32[34,8,128]{2,1,0:T(8,128)S(1)}, f32[34,8,128]{2,1,0:T(8,128)S(1)}, u32[]{:S(2)}, u32[]{:S(2)}) %collective-permute-start.17) | collective-permute-done | bytes 139296 | tf_op jit(solution)/shard_map/ppermute | solution.py:517
  113.4 2.7 %collective-permute-start.19 = (f32[12,8,128]{2,1,0:T(8,128)S(1)}, f32[12,8,128]{2,1,0:T(8,128)S(1)}, u32[]{:S(2)}, u32[]{:S(2)}) collective-permute-start(f32[12,8,128]{2,1,0:T(8,128)S(1)} %get-tuple-element.73), channel_id=1, source_target_pairs={{1,2},{3,4},{5,6},{7,8},{9,10},{11,12},{13,14},{2,1},{4,3},{6,5},{... | collective-permute-start | bytes 147464 | tf_op jit(solution)/shard_map/ppermute | solution.py:517
  117.5 4.0 %collective-permute-done.19.n_odd = f32[12,8,128]{2,1,0:T(8,128)S(1)} collective-permute-done((f32[12,8,128]{2,1,0:T(8,128)S(1)}, f32[12,8,128]{2,1,0:T(8,128)S(1)}, u32[]{:S(2)}, u32[]{:S(2)}) %collective-permute-start.19) | collective-permute-done | bytes 49184 | tf_op jit(solution)/shard_map/ppermute | solution.py:517
  121.5 3.0 %shard_map.123 = (f32[32,8,128]{2,1,0:T(8,128)S(1)}, f32[32,8,128]{2,1,0:T(8,128)S(1)}, f32[40,8,128]{2,1,0:T(8,128)S(1)}, f32[48,8,128]{2,1,0:T(8,128)S(1)}, f3...) custom-call(s32[2]{0:T(128)S(1)} %pad_add_fusion.2.par, s32[480]{0:T(512)S(1)} %fusion.4.table, ...), custom_call_target="tpu_custom_call" | custom-call | bytes 5277596 | tf_op jit(solution)/shard_map/pallas_call | solution.py:58
  124.7 1.9 %collective-permute-start.21 = (f32[34,8,128]{2,1,0:T(8,128)S(1)}, f32[34,8,128]{2,1,0:T(8,128)S(1)}, u32[]{:S(2)}, u32[]{:S(2)}) collective-permute-start(f32[34,8,128]{2,1,0:T(8,128)S(1)} %get-tuple-element.79), channel_id=1, source_target_pairs={{16,32},{48,64},{80,96},{32,16},{64,48},{96,80},{17,33},{49,65},{8... | collective-permute-start | bytes 417800 | tf_op jit(solution)/shard_map/ppermute | solution.py:517
  126.6 4.4 %collective-permute-done.21.r_odd = f32[34,8,128]{2,1,0:T(8,128)S(1)} collective-permute-done((f32[34,8,128]{2,1,0:T(8,128)S(1)}, f32[34,8,128]{2,1,0:T(8,128)S(1)}, u32[]{:S(2)}, u32[]{:S(2)}) %collective-permute-start.21) | collective-permute-done | bytes 139296 | tf_op jit(solution)/shard_map/ppermute | solution.py:517
  131.8 2.7 %collective-permute-start.23 = (f32[12,8,128]{2,1,0:T(8,128)S(1)}, f32[12,8,128]{2,1,0:T(8,128)S(1)}, u32[]{:S(2)}, u32[]{:S(2)}) collective-permute-start(f32[12,8,128]{2,1,0:T(8,128)S(1)} %get-tuple-element.83), channel_id=1, source_target_pairs={{1,2},{3,4},{5,6},{7,8},{9,10},{11,12},{13,14},{2,1},{4,3},{6,5},{... | collective-permute-start | bytes 147464 | tf_op jit(solution)/shard_map/ppermute | solution.py:517
  135.9 4.0 %collective-permute-done.23.n_odd = f32[12,8,128]{2,1,0:T(8,128)S(1)} collective-permute-done((f32[12,8,128]{2,1,0:T(8,128)S(1)}, f32[12,8,128]{2,1,0:T(8,128)S(1)}, u32[]{:S(2)}, u32[]{:S(2)}) %collective-permute-start.23) | collective-permute-done | bytes 49184 | tf_op jit(solution)/shard_map/ppermute | solution.py:517
  (167 shorter events, 56.3 us)
Async XLA Ops:
  1.5 32.8 %collective-permute-start.1 = (s32[8,8]{1,0:T(8,128)S(1)}, s32[8,8]{1,0:T(8,128)S(1)}, u32[]{:S(2)}, u32[]{:S(2)}) collective-permute-start(s32[8,8]{1,0:T(8,128)S(1)} %get-tuple-element.100), channel_id=1, source_target_pairs={{16,32},{48,64},{80,96},{32,16},{64,48},{96,80},{17,33},{49,65},{8... | collective-permute-start | bytes 776 | tf_op jit(solution)/shard_map/ppermute | solution.py:517
  3.5 30.9 %collective-permute-start = (s32[8,8]{1,0:T(8,128)S(1)}, s32[8,8]{1,0:T(8,128)S(1)}, u32[]{:S(2)}, u32[]{:S(2)}) collective-permute-start(s32[8,8]{1,0:T(8,128)S(1)} %get-tuple-element.101), channel_id=1, source_target_pairs={{0,16},{16,0},{32,48},{48,32},{64,80},{80,64},{96,112},{112,96},{1... | collective-permute-start | bytes 776 | tf_op jit(solution)/shard_map/ppermute | solution.py:517
  10.7 78.3 %all-to-all-start = ((f32[128,8,128]{2,1,0:T(8,128)}), f32[128,8,128]{2,1,0:T(8,128)}, u32[]{:S(2)}, u32[]{:S(2)}) async-start(f32[128,8,128]{2,1,0:T(8,128)} %bitcast.14), calls=%async_computation | async-start | bytes 1048576 | tf_op jit(solution)/shard_map/all_to_all | solution.py:588
  23.4 34.7 %collective-permute-start.8 = (bf16[16,16,128]{2,1,0:T(8,128)(2,1)}, bf16[16,16,128]{2,1,0:T(8,128)(2,1)}, u32[]{:S(2)}, u32[]{:S(2)}) collective-permute-start(bf16[16,16,128]{2,1,0:T(8,128)(2,1)} %get-tuple-element.47), channel_id=1, source_target_pairs={{0,16},{16,0},{32,48},{48,32},{64,80},{80,64},{96,112},{112,96},{1... | collective-permute-start | bytes 196616 | tf_op jit(solution)/shard_map/ppermute | solution.py:517
  24.7 19.8 %collective-permute-start.5 = (bf16[8,64,512]{2,1,0:T(8,128)(2,1)}, bf16[8,64,512]{2,1,0:T(8,128)(2,1)S(1)}, u32[]{:S(2)}, u32[]{:S(2)}) collective-permute-start(bf16[8,64,512]{2,1,0:T(8,128)(2,1)} %get-tuple-element.92), channel_id=1, source_target_pairs={{16,32},{48,64},{80,96},{32,16},{64,48},{96,80},{17,33},{49,65},{8... | collective-permute-start | bytes 1572872 | tf_op jit(solution)/shard_map/ppermute | solution.py:517
  27.2 17.4 %collective-permute-start.4 = (bf16[8,64,512]{2,1,0:T(8,128)(2,1)}, bf16[8,64,512]{2,1,0:T(8,128)(2,1)S(1)}, u32[]{:S(2)}, u32[]{:S(2)}) collective-permute-start(bf16[8,64,512]{2,1,0:T(8,128)(2,1)} %get-tuple-element.93), channel_id=1, source_target_pairs={{0,16},{16,0},{32,48},{48,32},{64,80},{80,64},{96,112},{112,96},{1... | collective-permute-start | bytes 1572872 | tf_op jit(solution)/shard_map/ppermute | solution.py:517
  34.4 6.2 %collective-permute-start.2 = (s32[6,8]{1,0:T(8,128)S(1)}, s32[6,8]{1,0:T(8,128)S(1)}, u32[]{:S(2)}, u32[]{:S(2)}) collective-permute-start(s32[6,8]{1,0:T(8,128)S(1)} %pad_add_fusion), channel_id=1, source_target_pairs={{0,1},{1,0},{2,3},{3,2},{4,5},{5,4},{6,7},{7,6},{8,9},{9,8},{10,11... | collective-permute-start | bytes 584 | tf_op jit(solution)/shard_map/ppermute | solution.py:517
  36.2 7.6 %collective-permute-start.3 = (s32[6,8]{1,0:T(8,128)S(1)}, s32[6,8]{1,0:T(8,128)S(1)}, u32[]{:S(2)}, u32[]{:S(2)}) collective-permute-start(s32[6,8]{1,0:T(8,128)S(1)} %pad_add_fusion.1), channel_id=1, source_target_pairs={{1,2},{3,4},{5,6},{7,8},{9,10},{11,12},{13,14},{2,1},{4,3},{6,5},{... | collective-permute-start | bytes 584 | tf_op jit(solution)/shard_map/ppermute | solution.py:517
  40.6 17.6 %collective-permute-start.9 = (bf16[16,16,128]{2,1,0:T(8,128)(2,1)}, bf16[16,16,128]{2,1,0:T(8,128)(2,1)}, u32[]{:S(2)}, u32[]{:S(2)}) collective-permute-start(bf16[16,16,128]{2,1,0:T(8,128)(2,1)} %get-tuple-element.48), channel_id=1, source_target_pairs={{16,32},{48,64},{80,96},{32,16},{64,48},{96,80},{17,33},{49,65},{8... | collective-permute-start | bytes 196616 | tf_op jit(solution)/shard_map/ppermute | solution.py:517
  46.4 24.2 %collective-permute-start.6 = (bf16[6,64,512]{2,1,0:T(8,128)(2,1)}, bf16[6,64,512]{2,1,0:T(8,128)(2,1)S(1)}, u32[]{:S(2)}, u32[]{:S(2)}) collective-permute-start(bf16[6,64,512]{2,1,0:T(8,128)(2,1)} %pad_maximum_fusion), channel_id=1, source_target_pairs={{0,1},{1,0},{2,3},{3,2},{4,5},{5,4},{6,7},{7,6},{8,9},{9,8},{10,11... | collective-permute-start | bytes 1179656 | tf_op jit(solution)/shard_map/ppermute | solution.py:517
  48.1 22.5 %collective-permute-start.7 = (bf16[6,64,512]{2,1,0:T(8,128)(2,1)}, bf16[6,64,512]{2,1,0:T(8,128)(2,1)}, u32[]{:S(2)}, u32[]{:S(2)}) collective-permute-start(bf16[6,64,512]{2,1,0:T(8,128)(2,1)} %pad_maximum_fusion.1), channel_id=1, source_target_pairs={{1,2},{3,4},{5,6},{7,8},{9,10},{11,12},{13,14},{2,1},{4,3},{6,5},{... | collective-permute-start | bytes 1179656 | tf_op jit(solution)/shard_map/ppermute | solution.py:517
  60.9 4.7 %collective-permute-start.10 = (bf16[14,16,128]{2,1,0:T(8,128)(2,1)S(1)}, bf16[14,16,128]{2,1,0:T(8,128)(2,1)S(1)}, u32[]{:S(2)}, u32[]{:S(2)}) collective-permute-start(bf16[14,16,128]{2,1,0:T(8,128)(2,1)S(1)} %get-tuple-element.49), channel_id=1, source_target_pairs={{0,1},{1,0},{2,3},{3,2},{4,5},{5,4},{6,7},{7,6},{8,9},{9,8},{10,11... | collective-permute-start | bytes 172040 | tf_op jit(solution)/shard_map/ppermute | solution.py:517
  62.4 8.2 %collective-permute-start.11 = (bf16[14,16,128]{2,1,0:T(8,128)(2,1)S(1)}, bf16[14,16,128]{2,1,0:T(8,128)(2,1)S(1)}, u32[]{:S(2)}, u32[]{:S(2)}) collective-permute-start(bf16[14,16,128]{2,1,0:T(8,128)(2,1)S(1)} %get-tuple-element.50), channel_id=1, source_target_pairs={{1,2},{3,4},{5,6},{7,8},{9,10},{11,12},{13,14},{2,1},{4,3},{6,5},{... | collective-permute-start | bytes 172040 | tf_op jit(solution)/shard_map/ppermute | solution.py:517
  78.7 2.5 %collective-permute-start.12 = (bf16[16,16,128]{2,1,0:T(8,128)(2,1)S(1)}, bf16[16,16,128]{2,1,0:T(8,128)(2,1)S(1)}, u32[]{:S(2)}, u32[]{:S(2)}) collective-permute-start(bf16[16,16,128]{2,1,0:T(8,128)(2,1)S(1)} %get-tuple-element.57), channel_id=1, source_target_pairs={{0,16},{16,0},{32,48},{48,32},{64,80},{80,64},{96,112},{112,96},{1... | collective-permute-start | bytes 196616 | tf_op jit(solution)/shard_map/ppermute | solution.py:517
  78.7 5.6 %collective-permute-start.13 = (bf16[16,16,128]{2,1,0:T(8,128)(2,1)S(1)}, bf16[16,16,128]{2,1,0:T(8,128)(2,1)S(1)}, u32[]{:S(2)}, u32[]{:S(2)}) collective-permute-start(bf16[16,16,128]{2,1,0:T(8,128)(2,1)S(1)} %get-tuple-element.58), channel_id=1, source_target_pairs={{16,32},{48,64},{80,96},{32,16},{64,48},{96,80},{17,33},{49,65},{8... | collective-permute-start | bytes 196616 | tf_op jit(solution)/shard_map/ppermute | solution.py:517
  86.1 5.7 %collective-permute-start.14 = (bf16[14,16,128]{2,1,0:T(8,128)(2,1)}, bf16[14,16,128]{2,1,0:T(8,128)(2,1)}, u32[]{:S(2)}, u32[]{:S(2)}) collective-permute-start(bf16[14,16,128]{2,1,0:T(8,128)(2,1)} %get-tuple-element.59), channel_id=1, source_target_pairs={{0,1},{1,0},{2,3},{3,2},{4,5},{5,4},{6,7},{7,6},{8,9},{9,8},{10,11... | collective-permute-start | bytes 172040 | tf_op jit(solution)/shard_map/ppermute | solution.py:517
  86.2 8.6 %collective-permute-start.15 = (bf16[14,16,128]{2,1,0:T(8,128)(2,1)}, bf16[14,16,128]{2,1,0:T(8,128)(2,1)}, u32[]{:S(2)}, u32[]{:S(2)}) collective-permute-start(bf16[14,16,128]{2,1,0:T(8,128)(2,1)} %get-tuple-element.60), channel_id=1, source_target_pairs={{1,2},{3,4},{5,6},{7,8},{9,10},{11,12},{13,14},{2,1},{4,3},{6,5},{... | collective-permute-start | bytes 172040 | tf_op jit(solution)/shard_map/ppermute | solution.py:517
  106.2 2.0 %collective-permute-start.16 = (f32[34,8,128]{2,1,0:T(8,128)S(1)}, f32[34,8,128]{2,1,0:T(8,128)S(1)}, u32[]{:S(2)}, u32[]{:S(2)}) collective-permute-start(f32[34,8,128]{2,1,0:T(8,128)S(1)} %get-tuple-element.68), channel_id=1, source_target_pairs={{0,16},{16,0},{32,48},{48,32},{64,80},{80,64},{96,112},{112,96},{1... | collective-permute-start | bytes 417800 | tf_op jit(solution)/shard_map/ppermute | solution.py:517
  106.3 6.4 %collective-permute-start.17 = (f32[34,8,128]{2,1,0:T(8,128)S(1)}, f32[34,8,128]{2,1,0:T(8,128)S(1)}, u32[]{:S(2)}, u32[]{:S(2)}) collective-permute-start(f32[34,8,128]{2,1,0:T(8,128)S(1)} %get-tuple-element.69), channel_id=1, source_target_pairs={{16,32},{48,64},{80,96},{32,16},{64,48},{96,80},{17,33},{49,65},{8... | collective-permute-start | bytes 417800 | tf_op jit(solution)/shard_map/ppermute | solution.py:517
  113.3 4.2 %collective-permute-start.18 = (f32[12,8,128]{2,1,0:T(8,128)S(1)}, f32[12,8,128]{2,1,0:T(8,128)S(1)}, u32[]{:S(2)}, u32[]{:S(2)}) collective-permute-start(f32[12,8,128]{2,1,0:T(8,128)S(1)} %get-tuple-element.72), channel_id=1, source_target_pairs={{0,1},{1,0},{2,3},{3,2},{4,5},{5,4},{6,7},{7,6},{8,9},{9,8},{10,11... | collective-permute-start | bytes 147464 | tf_op jit(solution)/shard_map/ppermute | solution.py:517
  113.4 8.1 %collective-permute-start.19 = (f32[12,8,128]{2,1,0:T(8,128)S(1)}, f32[12,8,128]{2,1,0:T(8,128)S(1)}, u32[]{:S(2)}, u32[]{:S(2)}) collective-permute-start(f32[12,8,128]{2,1,0:T(8,128)S(1)} %get-tuple-element.73), channel_id=1, source_target_pairs={{1,2},{3,4},{5,6},{7,8},{9,10},{11,12},{13,14},{2,1},{4,3},{6,5},{... | collective-permute-start | bytes 147464 | tf_op jit(solution)/shard_map/ppermute | solution.py:517
  124.7 6.4 %collective-permute-start.21 = (f32[34,8,128]{2,1,0:T(8,128)S(1)}, f32[34,8,128]{2,1,0:T(8,128)S(1)}, u32[]{:S(2)}, u32[]{:S(2)}) collective-permute-start(f32[34,8,128]{2,1,0:T(8,128)S(1)} %get-tuple-element.79), channel_id=1, source_target_pairs={{16,32},{48,64},{80,96},{32,16},{64,48},{96,80},{17,33},{49,65},{8... | collective-permute-start | bytes 417800 | tf_op jit(solution)/shard_map/ppermute | solution.py:517
  131.7 4.2 %collective-permute-start.22 = (f32[12,8,128]{2,1,0:T(8,128)S(1)}, f32[12,8,128]{2,1,0:T(8,128)S(1)}, u32[]{:S(2)}, u32[]{:S(2)}) collective-permute-start(f32[12,8,128]{2,1,0:T(8,128)S(1)} %get-tuple-element.82), channel_id=1, source_target_pairs={{0,1},{1,0},{2,3},{3,2},{4,5},{5,4},{6,7},{7,6},{8,9},{9,8},{10,11... | collective-permute-start | bytes 147464 | tf_op jit(solution)/shard_map/ppermute | solution.py:517
  131.8 8.1 %collective-permute-start.23 = (f32[12,8,128]{2,1,0:T(8,128)S(1)}, f32[12,8,128]{2,1,0:T(8,128)S(1)}, u32[]{:S(2)}, u32[]{:S(2)}) collective-permute-start(f32[12,8,128]{2,1,0:T(8,128)S(1)} %get-tuple-element.83), channel_id=1, source_target_pairs={{1,2},{3,4},{5,6},{7,8},{9,10},{11,12},{13,14},{2,1},{4,3},{6,5},{... | collective-permute-start | bytes 147464 | tf_op jit(solution)/shard_map/ppermute | solution.py:517
  (44 other events, 265.9 us)
where the time goes:
time: 143 us; the launch traced here: 141 us
  starting transfers between devices  49 us (34%)
  waiting for transfers between devices  32 us (22%)
  local copies, waits for them, and re-layouts  29.6 us (21%)
  Pallas kernels  23.8 us (17%)
  other arithmetic  5.77 us (4%)
    ppermute x12, starting transfers between devices, exchange(): lax.ppermute(for_odd, axis, swap_odd(axis))  31.6 us
    ppermute x12, waiting for transfers between devices, exchange(): lax.ppermute(for_odd, axis, swap_odd(axis))  29.1 us
    pallas_call x13, Pallas kernels, call(): pl.pallas_call(kernel, out_shape=[jax.ShapeDtypeStruct(s, d) for s, d in...  23.8 us
    unnamed x87, local copies, waits for them, and re-layouts  19.3 us
    all_to_all x1, starting transfers between devices, body(): lax.all_to_all(sent.reshape(devices, CAP, 128), ('px', 'py'), split_axis=...  10.6 us
    ppermute x12, starting transfers between devices, exchange(): lax.ppermute(for_even, axis, swap_even(axis))  6.79 us
    concatenate x4, other arithmetic, with_corners(): jnp.concatenate([own, ends[0][k][None], ends[1][k][None]], 0)  3.51 us
  transfers between devices with their start and end apart: 25, of which 10 were waited for; matrix products, arithmetic and copies ran while one was open for 11% of the time, Pallas kernels for 9%

commit v1 on v0

v1 whole, which is shorter than its diff:
```python
import jax
import jax.numpy as jnp
from jax import lax
from jax.experimental import pallas as pl
from jax.experimental.pallas import tpu as pltpu
from jax.sharding import PartitionSpec as P

ROWS, COLS = 4, 8
OWN = ROWS * COLS
CAP = 8
WIDE = COLS + 4
PLACES = (ROWS + 4) * WIDE
F32, BF16 = jnp.float32, jnp.bfloat16
VMEM_BYTES = 16 * 1024 * 1024
NODE, WIDTH = 64, 512
FIELD, ADDEND, SUM0, SUM1, SUM2, SUM3, COEF = (i * OWN for i in range(7))
PX_BASE, PY_BASE = COLS * NODE, (ROWS + 2) * NODE


def place(row, col):
    return (row + 2) * WIDE + col + 2


def low_lanes(rows):
    return lax.broadcasted_iota(jnp.int32, (rows, 128), 1) < 64


def doubled(plain):
    turned = pltpu.roll(plain, 64, 1)
    low = low_lanes(8)
    return jnp.concatenate([jnp.where(low, plain, turned), jnp.where(low, turned, plain)], 0)


def packed(plain):
    return jnp.concatenate([plain[:, :64], plain[:, 64:]], 0)


def unpacked(rows):
    return jnp.concatenate([rows[:8], rows[8:]], 1)


def halves(plain):
    high = plain.astype(BF16).astype(F32)
    return jnp.concatenate([high, plain - high], 0).astype(BF16)


def joined(pair):
    pair = pair.astype(F32)
    return pair[:8] + pair[8:]


def sides(par_ref, axis, near, far):
    even = par_ref[axis] == 0
    return jnp.where(even, near, far), jnp.where(even, far, near)


class Flow:
    def __init__(self, sems):
        self.sems, self.used, self.coming, self.going = sems, 0, {}, []

    def copy(self, source, target):
        made = pltpu.make_async_copy(source, target, self.sems.at[self.used])
        self.used += 1
        made.start()
        return made

    def wait(self, *refs):
        for ref in refs:
            for made in self.coming.pop(id(ref), ()):
                made.wait()

    def send(self, source, target):
        self.going.append(self.copy(source, target))

    def finish(self):
        for key in list(self.coming):
            for made in self.coming.pop(key):
                made.wait()
        for made in self.going:
            made.wait()


def call(kernel, outs, inputs, scratch=(), copies=0):
    spaces = {"s": pltpu.SMEM, "v": pltpu.VMEM, "h": pltpu.HBM, "b": pltpu.HBM}
    arrays = [array for array, _ in inputs]
    fetched = [i for i, (_, kind) in enumerate(inputs) if kind == "h"]
    total = len(fetched) + copies

    def wrapped(*refs):
        refs = list(refs)
        buffers = refs[len(inputs) + len(outs) + len(scratch) :]
        flow = Flow(buffers[-1])
        for buffer, i in zip(buffers, fetched):
            flow.coming[id(buffer)] = [flow.copy(refs[i], buffer)]
            refs[i] = buffer
        kernel(flow, *refs[: len(inputs) + len(outs) + len(scratch)])
        flow.finish()

    buffers = [pltpu.VMEM(arrays[i].shape, arrays[i].dtype) for i in fetched]
    return pl.pallas_call(
        wrapped,
        out_shape=[jax.ShapeDtypeStruct(shape, dtype) for shape, dtype, _ in outs],
        in_specs=[pl.BlockSpec(memory_space=spaces[kind]) for _, kind in inputs],
        out_specs=[pl.BlockSpec(memory_space=spaces[kind]) for _, _, kind in outs],
        scratch_shapes=list(scratch) + buffers + [pltpu.SemaphoreType.DMA((max(total, 1),))],
        compiler_params=pltpu.CompilerParams(vmem_limit_bytes=VMEM_BYTES),
    )(*arrays)


PLAIN = ((OWN, 8, 128), F32, "v")


class Tiles:
    def __init__(self, ref, base=None):
        self.ref, self.base = ref, base

    def at(self, t):
        if self.base is None:
            return (t,)
        return pl.ds(self.base + 16 * (t // 4), 16), pl.ds(128 * (t % 4), 128)

    def __getitem__(self, t):
        return self.ref[self.at(t)]

    def __setitem__(self, t, value):
        self.ref[self.at(t)] = value


def to_plain(native, scratch, out):
    for x in range(ROWS):
        for r in range(8):
            scratch[pl.ds(x * 64 + r * 8, 8), :] = native(x, r)
    for x in range(ROWS):
        for y in range(COLS):
            out[x * COLS + y] = scratch[pl.ds(x * 64 + y, 8, stride=8), :]


def lanes(r):
    return pl.ds(r * 128, 128)


def twice(rows):
    return jnp.concatenate([rows, rows], 1)


def px_message(par, plain, addend, outs):
    bases = sides(par, 0, 2, 0)
    edges = sides(par, 0, 3, 0)
    for out, base, edge in zip(outs, bases, edges):
        for k in range(2):
            for p in range(4):
                at = (base + k) * COLS + 2 * p
                out[k * 4 + p] = jnp.concatenate([plain(at), plain(at + 1)], 0).astype(BF16)
        for y in range(COLS):
            out[8 + y] = halves(addend(edge * COLS + y))


def py_message(par, plain, addend, outs):
    pairs = sides(par, 1, 3, 0)
    edges = sides(par, 1, 7, 0)
    for out, pair, edge in zip(outs, pairs, edges):
        for x in range(ROWS):
            at = x * COLS + 2 * pair
            out[x] = jnp.concatenate([plain(at), plain(at + 1)], 0).astype(BF16)
            out[8 + x] = halves(addend(x * COLS + edge))


def picked_tile(tiles, choice, low, high):
    return jnp.where(choice == 0, tiles[low].astype(F32), tiles[high].astype(F32)).astype(BF16)


def py_fill(par, r_even, r_odd, outs):
    edges = sides(par, 1, 7, 0)
    for out, edge in zip(outs, edges):
        for k in range(2):
            out[4 + k] = picked_tile(r_even, edge, k * 4, k * 4 + 3)
            out[6 + k] = picked_tile(r_odd, edge, k * 4, k * 4 + 3)
        out[12] = picked_tile(r_even, edge, 8, 15)
        out[13] = picked_tile(r_odd, edge, 8, 15)


def shift_lines(offsets):
    row = lax.broadcasted_iota(jnp.int32, (8, 128), 0)
    lane = lax.broadcasted_iota(jnp.int32, (8, 128), 1)
    repeat = ((lane % 8 == row) & (lane < 64)).astype(F32).astype(BF16)
    lines = jnp.zeros((8, 128), F32)
    for x in range(ROWS):
        codes = offsets[x].astype(F32).astype(BF16)
        wide = lax.dot_general(codes, repeat, (((1,), (0,)), ((), ())), preferred_element_type=F32)
        line = jnp.sum(jnp.where(lane // 8 == row, wide, 0.0), axis=0, keepdims=True)
        lines = jnp.where(row == x, line, lines)
    above = (lines > 2.5).astype(F32) + (lines > 5.5).astype(F32)
    return 9.0 * above + lines - 13.0


def start_kernel(
    flow, par, field, memory, charge, offsets, stiffness, m_even, m_odd, n_even, n_odd, lines, plain, addend, scratch
):
    for out, edge in zip((m_even, m_odd), sides(par, 0, ROWS - 1, 0)):
        for y in range(COLS):
            flow.send(stiffness.at[edge, y], out.at[pl.ds(y * NODE, NODE), :])
    for out, edge in zip((n_even, n_odd), sides(par, 1, COLS - 1, 0)):
        for x in range(ROWS):
            flow.send(stiffness.at[x, edge], out.at[pl.ds(x * NODE, NODE), :])
    flow.wait(offsets)
    found = shift_lines(offsets)
    lines[...] = found
    px_tiles = [Tiles(m_even, PX_BASE), Tiles(m_odd, PX_BASE)]
    py_tiles = [Tiles(n_even, PY_BASE), Tiles(n_odd, PY_BASE)]
    for out, edge in zip(px_tiles, sides(par, 0, ROWS - 1, 0)):
        line = jnp.where(edge == 0, found[0:1], found[ROWS - 1 : ROWS])
        out[16] = jnp.broadcast_to(line, (16, 128)).astype(BF16)
    for out in py_tiles:
        out[14] = jnp.concatenate([found, jnp.zeros((8, 128), F32)], 0).astype(BF16)
    flow.wait(field, memory, charge)
    terms = memory.shape[0]
    to_plain(lambda x, r: field[x, :, lanes(r)], scratch, plain)

    def total(x, r):
        acc = memory[0, x, :, lanes(r)]
        for q in range(1, terms):
            acc = acc + memory[q, x, :, lanes(r)]
        return acc * -twice(charge[x])

    to_plain(total, scratch, addend)
    get, add = (lambda at: plain[at]), (lambda at: addend[at])
    px_message(par, get, add, px_tiles)
    py_message(par, get, add, py_tiles)


def first_py_kernel(flow, par, r_even, r_odd, in_even, in_odd, n_even, n_odd):
    n_even[...] = in_even[...]
    n_odd[...] = in_odd[...]
    tiles = [Tiles(r_even, PX_BASE), Tiles(r_odd, PX_BASE)]
    outs = [Tiles(n_even, PY_BASE), Tiles(n_odd, PY_BASE)]
    py_fill(par, tiles[0], tiles[1], outs)
    row = lax.broadcasted_iota(jnp.int32, (16, 128), 0)
    for out, source, edge in zip((n_even, n_odd), (in_even, in_odd), sides(par, 1, COLS - 1, 0)):
        for k, got in enumerate((r_even, r_odd)):
            out[pl.ds((ROWS + k) * NODE, NODE), :] = got[pl.ds(edge * NODE, NODE), :]
    for out, source in zip(outs, (Tiles(in_even, PY_BASE), Tiles(in_odd, PY_BASE))):
        even, odd = tiles[0][16].astype(F32), tiles[1][16].astype(F32)
        own = source[14].astype(F32)
        out[14] = jnp.where(row == ROWS, even, jnp.where(row == ROWS + 1, odd, own)).astype(BF16)


def second_py_kernel(flow, par, r_even, r_odd, in_even, in_odd, n_even, n_odd):
    n_even[...] = in_even[...]
    n_odd[...] = in_odd[...]
    py_fill(par, Tiles(r_even), Tiles(r_odd), (Tiles(n_even), Tiles(n_odd)))


def decay_kernel(flow, after, field, memory, charge, relaxation, out, full, scratch):
    terms = memory.shape[0]
    flow.wait(field, memory, charge, relaxation)
    wide = [twice(charge[x]) for x in range(ROWS)]
    rates = [[twice(relaxation[q, x]) for q in range(terms)] for x in range(ROWS)]
    coefs = []
    for x in range(ROWS):
        w0 = w1 = w2 = 0.0
        for rate in rates[x]:
            w0 = w0 + (1.0 - rate)
            w1 = w1 + rate * (1.0 - rate)
            w2 = w2 + rate * rate * (1.0 - rate)
        coefs.append((wide[x], w0, w1, w2))
        for j in range(4):
            full[COEF + j * ROWS + x] = coefs[x][j]

    def region(base):
        return full.at[pl.ds(base, OWN)]

    def total(x, r):
        acc = memory[0, x, :, lanes(r)]
        for q in range(1, terms):
            acc = acc + memory[q, x, :, lanes(r)]
        return acc

    to_plain(lambda x, r: field[x, :, lanes(r)], scratch, region(FIELD))
    to_plain(total, scratch, region(SUM0))
    to_plain(lambda x, r: total(x, r) * -wide[x], scratch, region(ADDEND))
    for power, base in ((1, SUM1), (2, SUM2), (3, SUM3)):
        scale = [[rate if power == 1 else rate * rate if power == 2 else rate * rate * rate for rate in row] for row in rates]

        def part(x, r):
            acc = coefs[x][power] * field[x, :, lanes(r)]
            for q in range(terms):
                acc = acc + scale[x][q] * memory[q, x, :, lanes(r)]
            return acc

        to_plain(part, scratch, region(base))
    flow.send(full, out)


class Coefs:
    def __init__(self, ref):
        self.ref = ref

    def __call__(self, j, block):
        return self.ref[j * ROWS + block // COLS, pl.ds(block % COLS, 1), :]


def outer_places(par):
    row_even, row_odd = sides(par, 0, ROWS, -1)
    col_even, col_odd = sides(par, 1, COLS, -1)
    listed = []
    for array, row in ((0, row_even), (1, row_odd)):
        listed += [(array, y, place(row, y)) for y in range(COLS)]
    rows = [0, 1, 2, 3, row_even, row_odd]
    for array, col in ((2, col_even), (3, col_odd)):
        listed += [(array, j, place(row, col)) for j, row in enumerate(rows)]
    return listed


def weight_of(blocks, item):
    own, r_even, r_odd, n_even, n_odd = blocks
    if item < OWN:
        return own[item // COLS, item % COLS]
    item -= OWN
    for array, count in ((r_even, COLS), (r_odd, COLS), (n_even, ROWS + 2), (n_odd, ROWS + 2)):
        if item < count:
            return array[pl.ds(item * NODE, NODE), :]
        item -= count


def targets_of(table, par):
    columns = sides(par, 1, 0, COLS - 1)

    def target(item, k):
        if item < OWN + 2 * COLS:
            return table[item // COLS, (item % COLS) * 8 + k]
        item -= OWN + 2 * COLS
        side, j = item // (ROWS + 2), item % (ROWS + 2)
        return table[8 * (side + 1) + j, columns[side] * 8 + k]

    return target


def table_lines(par, lines, r_even, r_odd, n_even, n_odd):
    row = lax.broadcasted_iota(jnp.int32, (8, 128), 0)
    lane = lax.broadcasted_iota(jnp.int32, (8, 128), 1)
    row_even, row_odd = sides(par, 0, ROWS, -1)
    line = jnp.where(row == ROWS, row_even, jnp.where(row == ROWS + 1, row_odd, row))
    even = Tiles(r_even, PX_BASE)[16].astype(F32)[:8]
    odd = Tiles(r_odd, PX_BASE)[16].astype(F32)[:8]
    first = jnp.where(row == ROWS, even, jnp.where(row == ROWS + 1, odd, lines))
    parts = [first.astype(jnp.int32) + place(line, lane // 8)]
    for msg, col in zip((n_even, n_odd), sides(par, 1, COLS, -1)):
        parts.append(Tiles(msg, PY_BASE)[14].astype(F32)[:8].astype(jnp.int32) + place(line, col))
    return jnp.concatenate(parts, 0)


def forward_pair(par, target, ready, blocks, plain, received, field, middle, store_first, store_second):
    low = low_lanes(16)
    r_even, r_odd, n_even, n_odd = received

    def spread(pair, first, second):
        both = pair.astype(F32)
        field[first] = doubled(both[:8]).astype(BF16)
        field[second] = doubled(both[8:]).astype(BF16)

    row_bases = sides(par, 0, ROWS, -2)
    col_bases = sides(par, 1, COLS, -2)
    for msg, base in zip((r_even, r_odd), row_bases):
        for k in range(2):
            for p in range(4):
                at = place(base + k, 2 * p)
                spread(msg[k * 4 + p], at, at + 1)
    rows = [0, 1, 2, 3, row_bases[0], row_bases[0] + 1, row_bases[1], row_bases[1] + 1]
    for msg, base in zip((n_even, n_odd), col_bases):
        for j, row in enumerate(rows):
            at = place(row, base)
            spread(msg[j], at, at + 1)
    ready()
    for block in range(OWN):
        field[place(block // COLS, block % COLS)] = doubled(plain(block)).astype(BF16)

    def product(source, item):
        parts = []
        for m in range(4):
            one = source[target(item, 2 * m)]
            two = source[target(item, 2 * m + 1)]
            parts.append(jnp.where(low, one, two))
        picked = jnp.concatenate(parts, 1)
        out = lax.dot_general(
            picked, weight_of(blocks, item), (((1,), (1,)), ((), ())), preferred_element_type=F32
        )
        return unpacked(out)

    for number, (array, index, at) in enumerate(outer_places(par)):
        got = product(field, OWN + number) + joined(received[array][8 + index])
        middle[at] = doubled(got).astype(BF16)
    for block in range(OWN):
        got = store_first(block, product(field, block))
        middle[place(block // COLS, block % COLS)] = doubled(got).astype(BF16)
    for block in range(OWN):
        store_second(block, product(middle, block))


def forward_one(
    flow, par, lines, own, r_even, r_odd, n_even, n_odd, known, past, now, m_even, m_odd, p_even, p_odd, table_out,
    field, middle, table, codes, older,
):
    table_out[...] = table_lines(par, lines[...], r_even, r_odd, n_even, n_odd)
    looked = flow.copy(table_out, table)
    coef = Coefs(known.at[pl.ds(COEF, 4 * ROWS)])

    def ready():
        looked.wait()
        flow.wait(known)

    def first(block, out):
        got = out + known[ADDEND + block]
        older[block] = got
        full = known[SUM2 + block] + coef(1, block) * got
        older[OWN + block] = full
        now[OWN + block] = -coef(0, block) * full
        if block == OWN - 1:
            flow.send(older, past)
        return got

    def second(block, out):
        now[block] = out - coef(0, block) * known[SUM1 + block]

    received = (Tiles(r_even, PX_BASE), Tiles(r_odd, PX_BASE), Tiles(n_even, PY_BASE), Tiles(n_odd, PY_BASE))
    forward_pair(
        par, targets_of(table, par), ready, (own, r_even, r_odd, n_even, n_odd), lambda block: known[FIELD + block],
        received, field, middle, first, second,
    )
    get, add = (lambda at: now[at]), (lambda at: now[OWN + at])
    px_message(par, get, add, (Tiles(m_even), Tiles(m_odd)))
    py_message(par, get, add, (Tiles(p_even), Tiles(p_odd)))
    for block in range(OWN):
        now[2 * OWN + block] = known[SUM3 + block] + coef(2, block) * older[block] + coef(1, block) * now[block]


def turn_kernel(
    flow, par, table, tally, own, r_even, r_odd, n_even, n_odd, e_even, e_odd, s_even, s_odd, now, coefs, spread, counted,
    adjoint4, first_out, second_out, m_even, m_odd, field, middle, sums_one, sums_two, field3, field4, start_out,
):
    blocks = (own, r_even, r_odd, n_even, n_odd)
    target = targets_of(table, par)
    coef = Coefs(coefs)

    def first(block, out):
        got = out + now[OWN + block]
        field3[block] = got
        return got

    def second(block, out):
        field4[block] = out - coef(0, block) * now[2 * OWN + block]

    received = (Tiles(e_even), Tiles(e_odd), Tiles(s_even), Tiles(s_odd))
    clear(sums_one, sums_two)
    forward_pair(
        par, target, lambda: flow.wait(coefs), blocks, lambda block: now[block], received, field, middle, first, second
    )
    flow.wait(spread, counted)

    def start(block):
        value = injected(tally, 4, counted, field4[block], spread, block)
        start_out[block] = value
        if block == OWN - 1:
            flow.send(start_out, adjoint4)
        return value

    def add_first(block):
        return injected(tally, 3, counted, field3[block], spread, block)

    def add_second(block):
        memory = coef(0, block) * coef(1, block) * start_out[block]
        return injected(tally, 2, counted, now[block], spread, block) - memory

    adjoint_pair(
        par, target, blocks, start, add_first, add_second, (first_out, second_out, m_even, m_odd), sums_one, sums_two
    )


def clear(*refs):
    for ref in refs:
        zero = jnp.zeros(ref.shape[1:], F32)
        for at in range(ref.shape[0]):
            ref[at] = zero


def adjoint_pair(par, target, blocks, start, add_first, add_second, outs, middle, last):
    first_out, second_out, m_even, m_odd = outs
    low = low_lanes(16)

    def push(sums_ref, item, rows):
        out = lax.dot_general(
            rows, weight_of(blocks, item), (((1,), (0,)), ((), ())), preferred_element_type=F32
        )
        spots = [target(item, k) for k in range(8)]
        sums = []
        for k in range(8):
            part = out[:, (k // 2) * 128 : (k // 2 + 1) * 128]
            part = jnp.where(low, part, 0.0) if k % 2 == 0 else jnp.where(low, 0.0, part)
            sums.append(sums_ref[spots[k]] + part)
        for k in range(8):
            sums_ref[spots[k]] = sums[k]

    def both(sums_ref, at):
        value = sums_ref[at]
        return value + pltpu.roll(value, 64, 1)

    def plain_of(value):
        return jnp.where(low_lanes(8), value[:8], value[8:])

    for block in range(OWN):
        push(middle, block, packed(start(block)).astype(BF16))
    rows_at = sides(par, 0, ROWS, -1)
    for number, (array, index, at) in enumerate(outer_places(par)):
        value = both(middle, at)
        push(last, OWN + number, value[:, :64].astype(BF16))
    for out, row in zip((m_even, m_odd), rows_at):
        for j in range(COLS + 2):
            out[j] = plain_of(both(middle, place(row, j - 1)))
    for x in range(ROWS):
        for j in range(COLS + 2):
            value = plain_of(both(middle, place(x, j - 1)))
            if 1 <= j <= COLS:
                block = x * COLS + j - 1
                value = value + add_first(block)
                push(last, block, packed(value).astype(BF16))
            first_out[x * (COLS + 2) + j] = value
    for out, base in zip((m_even, m_odd), sides(par, 0, ROWS, -2)):
        for k in range(2):
            for j in range(WIDE):
                out[COLS + 2 + k * WIDE + j] = plain_of(both(last, place(base + k, j - 2)))
    for x in range(ROWS):
        for j in range(WIDE):
            value = plain_of(both(last, place(x, j - 2)))
            if 2 <= j < COLS + 2:
                value = value + add_second(x * COLS + j - 2)
            second_out[x * WIDE + j] = value


def adjoint_py_kernel(flow, par, first, second, r_even, r_odd, first_own, second_own, n_even, n_odd, one, two):
    one[...] = first[...]
    two[...] = second[...]
    for msg, row, base in zip((r_even, r_odd), sides(par, 0, 3, 0), sides(par, 0, 2, 0)):
        for j in range(COLS + 2):
            one[row * (COLS + 2) + j] += msg[j]
        for k in range(2):
            for j in range(WIDE):
                two[(base + k) * WIDE + j] += msg[COLS + 2 + k * WIDE + j]
    for out, col, base in zip((n_even, n_odd), sides(par, 1, COLS + 1, 0), sides(par, 1, COLS + 2, 0)):
        for x in range(ROWS):
            out[x] = one[x * (COLS + 2) + col]
            for k in range(2):
                out[ROWS + 2 * x + k] = two[x * WIDE + base + k]
    for x in range(ROWS):
        for y in range(COLS):
            first_own[x * COLS + y] = one[x * (COLS + 2) + 1 + y]
            second_own[x * COLS + y] = two[x * WIDE + 2 + y]


def settle(par, first_own, second_own, n_even, n_odd, first, second):
    first[...] = first_own[...]
    second[...] = second_own[...]
    for msg, col, base in zip((n_even, n_odd), sides(par, 1, 7, 0), sides(par, 1, 6, 0)):
        for x in range(ROWS):
            first[x * COLS + col] += msg[x]
            for k in range(2):
                second[x * COLS + base + k] += msg[ROWS + 2 * x + k]


def injected(tally, moment, counted, field, spread, block):
    return tally[moment] * counted[block] * field - spread[moment - 1, block]


def adjoint_two(
    flow, par, table, tally, own, r_even, r_odd, n_even, n_odd, first_own, second_own, e_even, e_odd, adjoint4, past, coefs,
    spread, counted, later, first_out, second_out, m_even, m_odd, sums_one, sums_two, adjoint3, adjoint2,
):
    clear(sums_one, sums_two)
    settle(par, first_own, second_own, e_even, e_odd, adjoint3, adjoint2)
    flow.send(adjoint3, later.at[pl.ds(0, OWN)])
    flow.send(adjoint2, later.at[pl.ds(OWN, OWN)])
    coef = Coefs(coefs)

    def add_first(block):
        if block == 0:
            flow.wait(adjoint4, past, coefs, spread, counted)
        memory = coef(2, block) * adjoint4[block] + coef(1, block) * adjoint3[block]
        return injected(tally, 1, counted, past[block], spread, block) - coef(0, block) * memory

    def add_second(block):
        memory = coef(3, block) * adjoint4[block] + coef(2, block) * adjoint3[block] + coef(1, block) * adjoint2[block]
        return -coef(0, block) * memory

    adjoint_pair(
        par, targets_of(table, par), (own, r_even, r_odd, n_even, n_odd), lambda block: adjoint2[block], add_first,
        add_second, (first_out, second_out, m_even, m_odd), sums_one, sums_two,
    )


def gradient_kernel(flow, after, adjoint4, later, known, past, now, out):
    flow.wait(adjoint4, later, known, past, now)
    for block in range(OWN):
        out[block] = (
            adjoint4[block] * now[2 * OWN + block] + later[block] * past[OWN + block]
            + later[OWN + block] * known[SUM1 + block]
        )
        out[OWN + block] = known[SUM0 + block]


def finish_kernel(
    flow, par, first_own, second_own, n_even, n_odd, before, result, gradient, adjoint1, adjoint0, scratch
):
    settle(par, first_own, second_own, n_even, n_odd, adjoint1, adjoint0)
    for x in range(ROWS):
        parts = []
        for y in range(COLS):
            block = x * COLS + y
            scratch[pl.ds(x * 64 + y * 8, 8), :] = adjoint0[block]
            value = before[block] + adjoint1[block] * before[OWN + block]
            parts.append(jnp.sum(value, axis=0, keepdims=True))
        rows = jnp.concatenate(parts, 0)
        gradient[x] = -(rows[:, :64] + rows[:, 64:])
        for r in range(8):
            result[x, :, lanes(r)] = scratch[pl.ds(x * 64 + r, 8, stride=8), :]


def split(value):
    high = value.astype(BF16)
    return high, (value - high.astype(F32)).astype(BF16)


def owner_kernel(flow, steps, after, observed, part, node, out, slots_of):
    flow.wait(observed, part, node)
    owned = observed.shape[0]
    slots = out.shape[0]
    devices = slots // CAP
    row = lax.broadcasted_iota(jnp.int32, (128, 128), 0)
    col = lax.broadcasted_iota(jnp.int32, (128, 128), 1)
    gate = row // 16
    source = row % 16
    step = jnp.zeros((128, 128), jnp.int32)
    for g in range(8):
        step = jnp.where(gate == g, steps[g], step)
    wanted = 2 * (col % 8) + (col // 8) % 2
    chosen = ((step == col // 16 + 1) & (source == wanted) & (col < 64)).astype(F32).astype(BF16)
    high, low = split(observed[...])
    dot = lambda a, b: lax.dot_general(a, b, (((1,), (0,)), ((), ())), preferred_element_type=F32)
    sums = dot(high, chosen) + dot(low, chosen)
    dest = part[...]
    member = (dest == lax.broadcasted_iota(jnp.int32, (devices, owned), 0)).astype(F32)
    earlier = (
        lax.broadcasted_iota(jnp.int32, (owned, owned), 0) < lax.broadcasted_iota(jnp.int32, (owned, owned), 1)
    ).astype(F32).astype(BF16)
    ahead = dot(member.astype(BF16), earlier)
    rank = jnp.sum(ahead * member, axis=0, keepdims=True).astype(jnp.int32)
    position = dest * CAP + rank
    where = (position == lax.broadcasted_iota(jnp.int32, (slots, owned), 0)).astype(F32).astype(BF16)
    line = lax.broadcasted_iota(jnp.int32, (128, owned), 0)
    which = node[...]
    block = lax.shift_right_logical(which, 6)
    inner = which - block * 64
    marks = jnp.where(line == 64, block, jnp.where(line == 65, inner, jnp.where(line == 66, 1, 0)))
    high, low = split(sums)
    turned = lambda a, b: lax.dot_general(a, b, (((1,), (1,)), ((), ())), preferred_element_type=F32)
    slots_of[...] = dot(where, high) + dot(where, low) + turned(where, marks.astype(F32).astype(BF16))
    flow.send(slots_of, out)


def holder_kernel(flow, slots, spread_out, counted_out, spread, counted):
    flow.wait(slots)
    values = slots[...]
    count = values.shape[0]
    lane = lax.broadcasted_iota(jnp.int32, (count, 128), 1)
    pick = lambda at: jnp.sum(jnp.where(lane == at, values, 0.0), axis=1, keepdims=True)
    place_of = jnp.where(pick(66) > 0.5, pick(64) * 64.0 + pick(65), -1.0).astype(jnp.int32)
    high, low = split(values.T)
    both = jnp.concatenate([high, low], 0)
    low8 = low_lanes(8)
    for chunk in range(OWN * 64 // 256):
        spots = lax.broadcasted_iota(jnp.int32, (count, 256), 1) + chunk * 256
        hot = (place_of == spots).astype(F32).astype(BF16)
        out = lax.dot_general(both, hot, (((1,), (0,)), ((), ())), preferred_element_type=F32)
        out = out[:128] + out[128:]
        for j in range(2):
            first = chunk * 4 + 2 * j
            for n in range(4):
                even = out[n * 16 : n * 16 + 8, j * 128 : (j + 1) * 128]
                odd = out[n * 16 + 8 : n * 16 + 16, j * 128 : (j + 1) * 128]
                spread[n, first] = jnp.where(low8, even, pltpu.roll(odd, 64, 1))
                spread[n, first + 1] = jnp.where(low8, pltpu.roll(even, 64, 1), odd)
            many = jnp.broadcast_to(out[66:67, j * 128 : (j + 1) * 128], (8, 128))
            other = pltpu.roll(many, 64, 1)
            counted[first] = jnp.where(low8, many, other)
            counted[first + 1] = jnp.where(low8, other, many)
    flow.send(spread, spread_out)
    flow.send(counted, counted_out)


def swap_even(axis):
    return [(i, i ^ 1) for i in range(lax.axis_size(axis))]


def swap_odd(axis):
    inner = range(1, lax.axis_size(axis) - 1, 2)
    return [(i, i + 1) for i in inner] + [(i + 1, i) for i in inner]


def exchange(axis, for_even, for_odd):
    return lax.ppermute(for_even, axis, swap_even(axis)), lax.ppermute(for_odd, axis, swap_odd(axis))


def body(
    checkpoint_field,
    checkpoint_memory,
    stiffness,
    block_offsets,
    chargeability,
    relaxation,
    observed,
    receiver_part,
    receiver_node,
    gate_step,
):
    devices = lax.axis_size(("px", "py"))
    slots = devices * CAP
    par = jnp.stack([lax.axis_index("px") % 2, lax.axis_index("py") % 2]).astype(jnp.int32)
    turn = pltpu.VMEM((256, 128), F32)
    places = pltpu.VMEM((PLACES, 16, 128), BF16)
    sums = pltpu.VMEM((PLACES, 16, 128), F32)
    blocks = pltpu.VMEM((OWN, 8, 128), F32)
    px_first = ((PX_BASE + 80, WIDTH), BF16, "v")
    py_first = ((PY_BASE + 64, WIDTH), BF16, "v")
    px_shape = ((16, 16, 128), BF16, "v")
    py_shape = ((14, 16, 128), BF16, "v")
    m_even, m_odd, p_even, p_odd, lines = call(
        start_kernel, [px_first, px_first, py_first, py_first, ((8, 128), F32, "v")],
        [
            (par, "s"), (checkpoint_field, "h"), (checkpoint_memory, "h"), (chargeability, "h"), (block_offsets, "h"),
            (stiffness, "b"),
        ],
        [blocks, blocks, turn], copies=2 * COLS + 2 * ROWS,
    )
    r_even, r_odd = exchange("px", m_even, m_odd)
    (known,) = call(
        decay_kernel, [((COEF + 4 * ROWS, 8, 128), F32, "h")],
        [(lines, "v"), (checkpoint_field, "h"), (checkpoint_memory, "h"), (chargeability, "h"), (relaxation, "h")],
        [pltpu.VMEM((COEF + 4 * ROWS, 8, 128), F32), turn], copies=1,
    )
    (sent,) = call(
        owner_kernel, [((slots, 128), F32, "h")],
        [
            (gate_step, "s"), (r_even, "v"), (observed, "h"), (receiver_part.reshape(1, -1), "h"),
            (receiver_node.reshape(1, -1), "h"),
        ],
        [pltpu.VMEM((slots, 128), F32)], copies=1,
    )
    held = lax.all_to_all(
        sent.reshape(devices, CAP, 128), ("px", "py"), split_axis=0, concat_axis=0, tiled=True
    ).reshape(slots, 128)
    n_even, n_odd = call(
        first_py_kernel, [py_first, py_first],
        [(par, "s"), (r_even, "v"), (r_odd, "v"), (p_even, "v"), (p_odd, "v")],
    )
    n_even, n_odd = exchange("py", n_even, n_odd)
    tally = jnp.sum(gate_step[None, :] == jnp.arange(5, dtype=jnp.int32)[:, None], axis=1).astype(F32)
    weights = [(a, "v") for a in (stiffness, r_even, r_odd, n_even, n_odd)]
    past, now, m_even, m_odd, p_even, p_odd, table = call(
        forward_one,
        [
            ((2 * OWN, 8, 128), F32, "h"), ((3 * OWN, 8, 128), F32, "v"), px_shape, px_shape, py_shape, py_shape,
            ((24, 128), jnp.int32, "v"),
        ],
        [(par, "s"), (lines, "v")] + weights + [(known, "h")],
        [places, places, pltpu.SMEM((24, 128), jnp.int32), pltpu.VMEM((8, 128), F32), pltpu.VMEM((2 * OWN, 8, 128), F32)],
        copies=2,
    )
    r_even, r_odd = exchange("px", m_even, m_odd)
    n_even, n_odd = call(
        second_py_kernel, [py_shape, py_shape],
        [(par, "s"), (r_even, "v"), (r_odd, "v"), (p_even, "v"), (p_odd, "v")],
    )
    n_even, n_odd = exchange("py", n_even, n_odd)
    spread, counted = call(
        holder_kernel, [((4, OWN, 8, 128), F32, "h"), ((OWN, 8, 128), F32, "h")], [(held, "h")],
        [pltpu.VMEM((4, OWN, 8, 128), F32), blocks], copies=2,
    )
    coefs = known[COEF:]
    pair_out = [
        ((ROWS * (COLS + 2), 8, 128), F32, "v"), ((ROWS * WIDE, 8, 128), F32, "v"),
        ((COLS + 2 + 2 * WIDE, 8, 128), F32, "v"), ((COLS + 2 + 2 * WIDE, 8, 128), F32, "v"),
    ]
    adjoint4, *rest = call(
        turn_kernel, [((OWN, 8, 128), F32, "h")] + pair_out,
        [(par, "s"), (table, "s"), (tally, "s")] + weights
        + [(r_even, "v"), (r_odd, "v"), (n_even, "v"), (n_odd, "v"), (now, "v"), (coefs, "h"), (spread, "h"), (counted, "h")],
        [places, places, sums, sums, blocks, blocks, blocks], copies=1,
    )

    def gathered(first, second, m_even, m_odd):
        r_even, r_odd = exchange("px", m_even, m_odd)
        own_first, own_second, n_even, n_odd = call(
            adjoint_py_kernel, [PLAIN, PLAIN, ((12, 8, 128), F32, "v"), ((12, 8, 128), F32, "v")],
            [(par, "s"), (first, "v"), (second, "v"), (r_even, "v"), (r_odd, "v")],
            [pltpu.VMEM(first.shape, F32), pltpu.VMEM(second.shape, F32)],
        )
        n_even, n_odd = exchange("py", n_even, n_odd)
        return [(a, "v") for a in (own_first, own_second, n_even, n_odd)]

    later, *rest = call(
        adjoint_two, [((2 * OWN, 8, 128), F32, "h")] + pair_out,
        [(par, "s"), (table, "s"), (tally, "s")] + weights + gathered(*rest)
        + [(adjoint4, "h"), (past, "h"), (coefs, "h"), (spread, "h"), (counted, "h")],
        [sums, sums, blocks, blocks], copies=2,
    )
    (before,) = call(
        gradient_kernel, [((2 * OWN, 8, 128), F32, "v")],
        [(rest[2], "v"), (adjoint4, "h"), (later, "h"), (known, "h"), (past, "h"), (now, "h")],
    )
    field_out, gradient = call(
        finish_kernel, [(checkpoint_field.shape, F32, "v"), (chargeability.shape, F32, "v")],
        [(par, "s")] + gathered(*rest) + [(before, "v")], [blocks, blocks, turn],
    )
    return field_out, gradient


def solution(mesh):
    in_specs = (
        P("px", "py", None),
        P(None, "px", "py", None),
        P("px", "py", None, None),
        P("px", "py", None),
        P("px", "py", None),
        P(None, "px", "py", None),
        P(("px", "py"), None),
        P(("px", "py"), None),
        P(("px", "py")),
        P(),
    )
    out_specs = (P("px", "py", None), P("px", "py", None))
    return jax.shard_map(body, mesh=mesh, in_specs=in_specs, out_specs=out_specs, check_vma=False)
```

time: 143 us -> 109 us (0.76)
  local copies, waits for them, and re-layouts: 29.6 us -> 9.28 us
  starting transfers between devices: 49 us -> 40.2 us
  Pallas kernels: 23.8 us -> 29.9 us
  other arithmetic: 5.77 us -> 0.2 us
  waiting for transfers between devices: 32 us -> 27.1 us
    unnamed x87 -> x44, local copies, waits for them, and re-layouts: 19.3 us -> 9.28 us
    pallas_call x13, Pallas kernels: 23.8 us -> 29.9 us  [call(): pl.pallas_call(wrapped, out_shape=[jax.ShapeDtypeStruct(shape, dtype) for...]
    ppermute x12 -> x8, starting transfers between devices: 31.6 us -> 26.1 us  [exchange(): lax.ppermute(for_odd, axis, swap_odd(axis))]
    concatenate x4 -> x0, other arithmetic: 3.51 us -> none  [with_corners(): jnp.concatenate([own, ends[0][k][None], ends[1][k][None]], 0)]
    ppermute x12 -> x8, waiting for transfers between devices: 2.84 us -> 0.02 us  [exchange(): lax.ppermute(for_even, axis, swap_even(axis))]
    squeeze x3 -> x0, local copies, waits for them, and re-layouts: 2.8 us -> none  [edge(): lax.dynamic_index_in_dim(array, last - at, dim, keepdims=False)]
    all_to_all x1, starting transfers between devices: 10.6 us -> 8.08 us  [body(): lax.all_to_all(sent.reshape(devices, CAP, 128), ('px', 'py'), split_axis=...]
    rem x2 -> x0, local copies, waits for them, and re-layouts: 2.24 us -> none  [target_table(): shift = (codes // 3 - 1) * WIDE + codes % 3 - 1]
  transfers between devices with their start and end apart: 25 -> 17, of which waited for: 10 -> 7; matrix products, arithmetic and copies ran while one was open for 11% -> 0% of each run, Pallas kernels for 9% -> 11%
where the time goes in v1:
time: 109 us; the launch traced here: 108 us
  starting transfers between devices  40.2 us (37%)
  Pallas kernels  29.9 us (27%)
  waiting for transfers between devices  27.1 us (25%)
  local copies, waits for them, and re-layouts  9.28 us (9%)
  between operations  1.22 us (1%)
    pallas_call x13, Pallas kernels, call(): pl.pallas_call(wrapped, out_shape=[jax.ShapeDtypeStruct(shape, dtype) for...  29.9 us
    ppermute x8, waiting for transfers between devices, exchange(): lax.ppermute(for_odd, axis, swap_odd(axis))  27.1 us
    ppermute x8, starting transfers between devices, exchange(): lax.ppermute(for_odd, axis, swap_odd(axis))  26.1 us
    unnamed x44, local copies, waits for them, and re-layouts  9.28 us
    all_to_all x1, starting transfers between devices, body(): lax.all_to_all(sent.reshape(devices, CAP, 128), ('px', 'py'), split_axis=...  8.08 us
    ppermute x8, starting transfers between devices, exchange(): lax.ppermute(for_even, axis, swap_even(axis))  5.98 us
  transfers between devices with their start and end apart: 17, of which 7 were waited for; matrix products, arithmetic and copies ran while one was open for 0% of the time, Pallas kernels for 11%

profile of v1, /device:TPU:10, one launch (start us, length us, event | category | flops | bytes accessed | tf_op | source)
XLA Modules:
  0.0 107.9 jit_solution(18328750039354463969)
XLA Ops:
  0.7 1.6 %copy-done = bf16[4,8,64,512]{3,2,1,0:T(8,128)(2,1)S(1)} copy-done((bf16[4,8,64,512]{3,2,1,0:T(8,128)(2,1)S(1)}, bf16[4,8,64,512]{3,2,1,0:T(8,128)(2,1)}, u32[]{:S(2)}) %copy-start) | copy-done | bytes 2097176
  5.7 3.4 %shard_map.113 = (bf16[592,512]{1,0:T(8,128)(2,1)S(1)}, bf16[592,512]{1,0:T(8,128)(2,1)S(1)}, bf16[448,512]{1,0:T(8,128)(2,1)S(1)}, bf16[448,512]{1,0:T(8,128)(2,1)S(1)}, f32[8,128]{1,0:T(8,128)S(1)}) custom-call(s32[2]{0:T(128)S(1)} %pad_add_fusion.refs_0_, f32[4,8,1024]{2,1,0:T(8,128)S(1)} %copy-done.12, f32[4,4,8,1024]{3,2,1,0:T(8,128)S(1)} %copy-done.4, ...), custom_call_target="tpu_custom_call" | custom-call | tf_op jit(solution)/shard_map/pallas_call | solution.py:100
  9.2 2.4 %collective-permute-start.1 = (bf16[592,512]{1,0:T(8,128)(2,1)S(1)}, bf16[592,512]{1,0:T(8,128)(2,1)S(1)}, u32[]{:S(2)}, u32[]{:S(2)}) collective-permute-start(bf16[592,512]{1,0:T(8,128)(2,1)S(1)} %get-tuple-element.40), channel_id=1, source_target_pairs={{16,32},{48,64},{80,96},{32,16},{64,48},{96,80},{17,33},{49,65},{8... | collective-permute-start | bytes 1818632 | tf_op jit(solution)/shard_map/ppermute | solution.py:707
  11.7 8.9 %collective-permute-done.1.refs_2_.refs_4_.refs_5_ = bf16[592,512]{1,0:T(8,128)(2,1)S(1)} collective-permute-done((bf16[592,512]{1,0:T(8,128)(2,1)S(1)}, bf16[592,512]{1,0:T(8,128)(2,1)S(1)}, u32[]{:S(2)}, u32[]{:S(2)}) %collective-permute-start.1) | collective-permute-done | bytes 606240 | tf_op jit(solution)/shard_map/ppermute | solution.py:707
  22.2 2.0 %collective-permute-start.2 = (bf16[448,512]{1,0:T(8,128)(2,1)}, bf16[448,512]{1,0:T(8,128)(2,1)}, u32[]{:S(2)}, u32[]{:S(2)}) collective-permute-start(bf16[448,512]{1,0:T(8,128)(2,1)} %get-tuple-element.43), channel_id=1, source_target_pairs={{0,1},{1,0},{2,3},{3,2},{4,5},{5,4},{6,7},{7,6},{8,9},{9,8},{10,11... | collective-permute-start | bytes 1376264 | tf_op jit(solution)/shard_map/ppermute | solution.py:707
  24.2 4.5 %collective-permute-start.3 = (bf16[448,512]{1,0:T(8,128)(2,1)}, bf16[448,512]{1,0:T(8,128)(2,1)}, u32[]{:S(2)}, u32[]{:S(2)}) collective-permute-start(bf16[448,512]{1,0:T(8,128)(2,1)} %get-tuple-element.44), channel_id=1, source_target_pairs={{1,2},{3,4},{5,6},{7,8},{9,10},{11,12},{13,14},{2,1},{4,3},{6,5},{... | collective-permute-start | bytes 1376264 | tf_op jit(solution)/shard_map/ppermute | solution.py:707
  31.1 8.1 %all-to-all-start = ((f32[128,8,128]{2,1,0:T(8,128)}), f32[128,8,128]{2,1,0:T(8,128)}, u32[]{:S(2)}, u32[]{:S(2)}) async-start(f32[128,8,128]{2,1,0:T(8,128)} %bitcast.6), calls=%async_computation | async-start | bytes 1048576 | tf_op jit(solution)/shard_map/all_to_all | solution.py:755
  41.1 4.6 %shard_map.116 = (f32[64,8,128]{2,1,0:T(8,128)S(1)}, f32[96,8,128]{2,1,0:T(8,128)S(1)}, bf16[16,16,128]{2,1,0:T(8,128)(2,1)S(1)}, bf16[16,16,128]{2,1,0:T(8,128)...) custom-call(s32[2]{0:T(128)S(1)} %pad_add_fusion.refs_0_, ...), custom_call_target="tpu_custom_call" | custom-call | tf_op jit(solution)/shard_map/pallas_call | solution.py:100
  47.3 2.4 %collective-permute-start.5 = (bf16[16,16,128]{2,1,0:T(8,128)(2,1)S(1)}, bf16[16,16,128]{2,1,0:T(8,128)(2,1)S(1)}, u32[]{:S(2)}, u32[]{:S(2)}) collective-permute-start(bf16[16,16,128]{2,1,0:T(8,128)(2,1)S(1)} %get-tuple-element.47), channel_id=1, source_target_pairs={{16,32},{48,64},{80,96},{32,16},{64,48},{96,80},{17,33},{49,65},{8... | collective-permute-start | bytes 196616 | tf_op jit(solution)/shard_map/ppermute | solution.py:707
  49.8 3.1 %collective-permute-done.5.refs_2_.refs_9_ = bf16[16,16,128]{2,1,0:T(8,128)(2,1)S(1)} collective-permute-done((bf16[16,16,128]{2,1,0:T(8,128)(2,1)S(1)}, bf16[16,16,128]{2,1,0:T(8,128)(2,1)S(1)}, u32[]{:S(2)}, u32[]{:S(2)}) %collective-permute-start.5) | collective-permute-done | bytes 65568 | tf_op jit(solution)/shard_map/ppermute | solution.py:707
  54.1 1.8 %collective-permute-start.6 = (bf16[14,16,128]{2,1,0:T(8,128)(2,1)}, bf16[14,16,128]{2,1,0:T(8,128)(2,1)}, u32[]{:S(2)}, u32[]{:S(2)}) collective-permute-start(bf16[14,16,128]{2,1,0:T(8,128)(2,1)} %get-tuple-element.50), channel_id=1, source_target_pairs={{0,1},{1,0},{2,3},{3,2},{4,5},{5,4},{6,7},{7,6},{8,9},{9,8},{10,11... | collective-permute-start | bytes 172040 | tf_op jit(solution)/shard_map/ppermute | solution.py:707
  55.8 4.2 %collective-permute-start.7 = (bf16[14,16,128]{2,1,0:T(8,128)(2,1)}, bf16[14,16,128]{2,1,0:T(8,128)(2,1)}, u32[]{:S(2)}, u32[]{:S(2)}) collective-permute-start(bf16[14,16,128]{2,1,0:T(8,128)(2,1)} %get-tuple-element.51), channel_id=1, source_target_pairs={{1,2},{3,4},{5,6},{7,8},{9,10},{11,12},{13,14},{2,1},{4,3},{6,5},{... | collective-permute-start | bytes 172040 | tf_op jit(solution)/shard_map/ppermute | solution.py:707
  60.2 3.1 %shard_map.119 = (f32[4,32,8,128]{3,2,1,0:T(8,128)S(1)}, f32[32,8,128]{2,1,0:T(8,128)S(1)}) custom-call(f32[1024,128]{1,0:T(8,128)} %bitcast.5.refs_0_), custom_call_target="tpu_custom_call" | custom-call | tf_op jit(solution)/shard_map/pallas_call | solution.py:100
  65.3 6.0 %shard_map.120 = (f32[32,8,128]{2,1,0:T(8,128)S(1)}, f32[40,8,128]{2,1,0:T(8,128)S(1)}, f32[48,8,128]{2,1,0:T(8,128)S(1)}, f32[34,8,128]{2,1,0:T(8,128)S(1)}, f32[34,8,128]{2,1,0:T(8,128)S(1)}) custom-call(s32[2]{0:T(128)S(1)} %pad_add_fusion.refs_0_, s32[24,128]{1,0:T(8,128)S(1)} %get-tuple-element.45.refs_1_, f32[5]{0:T(128)S(1)} %convert_element_type.7.refs_2_, ...), custom_call_target="tpu_custom_call" | custom-call | tf_op jit(solution)/shard_map/pallas_call | solution.py:100
  71.5 1.9 %collective-permute-start.9 = (f32[34,8,128]{2,1,0:T(8,128)S(1)}, f32[34,8,128]{2,1,0:T(8,128)S(1)}, u32[]{:S(2)}, u32[]{:S(2)}) collective-permute-start(f32[34,8,128]{2,1,0:T(8,128)S(1)} %get-tuple-element.58), channel_id=1, source_target_pairs={{16,32},{48,64},{80,96},{32,16},{64,48},{96,80},{17,33},{49,65},{8... | collective-permute-start | bytes 417800 | tf_op jit(solution)/shard_map/ppermute | solution.py:707
  73.4 4.4 %collective-permute-done.9.refs_4_ = f32[34,8,128]{2,1,0:T(8,128)S(1)} collective-permute-done((f32[34,8,128]{2,1,0:T(8,128)S(1)}, f32[34,8,128]{2,1,0:T(8,128)S(1)}, u32[]{:S(2)}, u32[]{:S(2)}) %collective-permute-start.9) | collective-permute-done | bytes 139296 | tf_op jit(solution)/shard_map/ppermute | solution.py:707
  78.6 4.4 %collective-permute-start.11 = (f32[12,8,128]{2,1,0:T(8,128)S(1)}, f32[12,8,128]{2,1,0:T(8,128)S(1)}, u32[]{:S(2)}, u32[]{:S(2)}) collective-permute-start(f32[12,8,128]{2,1,0:T(8,128)S(1)} %get-tuple-element.62), channel_id=1, source_target_pairs={{1,2},{3,4},{5,6},{7,8},{9,10},{11,12},{13,14},{2,1},{4,3},{6,5},{... | collective-permute-start | bytes 147464 | tf_op jit(solution)/shard_map/ppermute | solution.py:707
  83.0 3.7 %collective-permute-done.11.refs_11_ = f32[12,8,128]{2,1,0:T(8,128)S(1)} collective-permute-done((f32[12,8,128]{2,1,0:T(8,128)S(1)}, f32[12,8,128]{2,1,0:T(8,128)S(1)}, u32[]{:S(2)}, u32[]{:S(2)}) %collective-permute-start.11) | collective-permute-done | bytes 49184 | tf_op jit(solution)/shard_map/ppermute | solution.py:707
  86.7 4.5 %shard_map.122 = (f32[64,8,128]{2,1,0:T(8,128)S(1)}, f32[40,8,128]{2,1,0:T(8,128)S(1)}, f32[48,8,128]{2,1,0:T(8,128)S(1)}, f32[34,8,128]{2,1,0:T(8,128)S(1)}, f32[34,8,128]{2,1,0:T(8,128)S(1)}) custom-call(s32[2]{0:T(128)S(1)} %pad_add_fusion.refs_0_, s32[24,128]{1,0:T(8,128)S(1)} %get-tuple-element.45.refs_1_, f32[5]{0:T(128)S(1)} %convert_element_type.7.refs_2_, ...), custom_call_target="tpu_custom_call" | custom-call | tf_op jit(solution)/shard_map/pallas_call | solution.py:100
  91.2 1.9 %collective-permute-start.13 = (f32[34,8,128]{2,1,0:T(8,128)S(1)}, f32[34,8,128]{2,1,0:T(8,128)S(1)}, u32[]{:S(2)}, u32[]{:S(2)}) collective-permute-start(f32[34,8,128]{2,1,0:T(8,128)S(1)} %get-tuple-element.68), channel_id=1, source_target_pairs={{16,32},{48,64},{80,96},{32,16},{64,48},{96,80},{17,33},{49,65},{8... | collective-permute-start | bytes 417800 | tf_op jit(solution)/shard_map/ppermute | solution.py:707
  93.1 1.7 %collective-permute-start.12 = (f32[34,8,128]{2,1,0:T(8,128)S(1)}, f32[34,8,128]{2,1,0:T(8,128)S(1)}, u32[]{:S(2)}, u32[]{:S(2)}) collective-permute-start(f32[34,8,128]{2,1,0:T(8,128)S(1)} %get-tuple-element.67.refs_0_), channel_id=1, source_target_pairs={{0,16},{16,0},{32,48},{48,32},{64,80},{80,64},{96,112},{112,96},{1... | collective-permute-start | bytes 417800 | tf_op jit(solution)/shard_map/ppermute | solution.py:707
  94.9 2.7 %collective-permute-done.13.refs_4_ = f32[34,8,128]{2,1,0:T(8,128)S(1)} collective-permute-done((f32[34,8,128]{2,1,0:T(8,128)S(1)}, f32[34,8,128]{2,1,0:T(8,128)S(1)}, u32[]{:S(2)}, u32[]{:S(2)}) %collective-permute-start.13) | collective-permute-done | bytes 139296 | tf_op jit(solution)/shard_map/ppermute | solution.py:707
  98.3 4.2 %collective-permute-start.15 = (f32[12,8,128]{2,1,0:T(8,128)S(1)}, f32[12,8,128]{2,1,0:T(8,128)S(1)}, u32[]{:S(2)}, u32[]{:S(2)}) collective-permute-start(f32[12,8,128]{2,1,0:T(8,128)S(1)} %get-tuple-element.72), channel_id=1, source_target_pairs={{1,2},{3,4},{5,6},{7,8},{9,10},{11,12},{13,14},{2,1},{4,3},{6,5},{... | collective-permute-start | bytes 147464 | tf_op jit(solution)/shard_map/ppermute | solution.py:707
  103.2 3.2 %collective-permute-done.15.refs_4_ = f32[12,8,128]{2,1,0:T(8,128)S(1)} collective-permute-done((f32[12,8,128]{2,1,0:T(8,128)S(1)}, f32[12,8,128]{2,1,0:T(8,128)S(1)}, u32[]{:S(2)}, u32[]{:S(2)}) %collective-permute-start.15) | collective-permute-done | bytes 49184 | tf_op jit(solution)/shard_map/ppermute | solution.py:707
  (71 shorter events, 17.8 us)
Async XLA Ops:
  5.7 23.0 %copy-start.14 = (f32[256,128]{1,0:T(8,128)S(1)}, f32[256,128]{1,0:T(8,128)}, u32[]{:S(2)}) copy-start(f32[256,128]{1,0:T(8,128)} %refs_2_.7) | copy-start | bytes 393220
  5.7 23.0 %copy-start.19 = (s32[256,1]{0,1:T(1,128)S(1)}, s32[256,1]{0,1:T(1,128)}, u32[]{:S(2)}) copy-start(s32[256,1]{0,1:T(1,128)} %param.17) | copy-start | bytes 3076
  5.7 23.0 %copy-start.20 = (s32[256]{0:T(256)S(1)}, s32[256]{0:T(256)}, u32[]{:S(2)}) copy-start(s32[256]{0:T(256)} %param.18) | copy-start | bytes 3076
  5.7 23.0 %copy-start.21 = (s32[8]{0:T(128)S(1)}, s32[8]{0:T(128)}, u32[]{:S(2)}) copy-start(s32[8]{0:T(128)} %refs_0_.1) | copy-start | bytes 100
  9.1 2.6 %collective-permute-start = (bf16[592,512]{1,0:T(8,128)(2,1)S(1)}, bf16[592,512]{1,0:T(8,128)(2,1)S(1)}, u32[]{:S(2)}, u32[]{:S(2)}) collective-permute-start(bf16[592,512]{1,0:T(8,128)(2,1)S(1)} %get-tuple-element.39), channel_id=1, source_target_pairs={{0,16},{16,0},{32,48},{48,32},{64,80},{80,64},{96,112},{112,96},{1... | collective-permute-start | bytes 1818632 | tf_op jit(solution)/shard_map/ppermute | solution.py:707
  9.2 11.4 %collective-permute-start.1 = (bf16[592,512]{1,0:T(8,128)(2,1)S(1)}, bf16[592,512]{1,0:T(8,128)(2,1)S(1)}, u32[]{:S(2)}, u32[]{:S(2)}) collective-permute-start(bf16[592,512]{1,0:T(8,128)(2,1)S(1)} %get-tuple-element.40), channel_id=1, source_target_pairs={{16,32},{48,64},{80,96},{32,16},{64,48},{96,80},{17,33},{49,65},{8... | collective-permute-start | bytes 1818632 | tf_op jit(solution)/shard_map/ppermute | solution.py:707
  20.6 18.6 %copy-start.17 = (f32[4,4,8,64]{3,2,1,0:T(8,128)S(1)}, f32[4,4,8,64]{3,2,1,0:T(8,128)}, u32[]{:S(2)}) copy-start(f32[4,4,8,64]{3,2,1,0:T(8,128)} %refs_4_.3) | copy-start | bytes 98308
  22.2 18.9 %copy-start.1 = (bf16[4,8,64,512]{3,2,1,0:T(8,128)(2,1)S(1)}, bf16[4,8,64,512]{3,2,1,0:T(8,128)(2,1)}, u32[]{:S(2)}) copy-start(bf16[4,8,64,512]{3,2,1,0:T(8,128)(2,1)} %refs_3_.7) | copy-start | bytes 6291460
  22.2 18.9 %collective-permute-start.2 = (bf16[448,512]{1,0:T(8,128)(2,1)}, bf16[448,512]{1,0:T(8,128)(2,1)}, u32[]{:S(2)}, u32[]{:S(2)}) collective-permute-start(bf16[448,512]{1,0:T(8,128)(2,1)} %get-tuple-element.43), channel_id=1, source_target_pairs={{0,1},{1,0},{2,3},{3,2},{4,5},{5,4},{6,7},{7,6},{8,9},{9,8},{10,11... | collective-permute-start | bytes 1376264 | tf_op jit(solution)/shard_map/ppermute | solution.py:707
  24.2 16.9 %collective-permute-start.3 = (bf16[448,512]{1,0:T(8,128)(2,1)}, bf16[448,512]{1,0:T(8,128)(2,1)}, u32[]{:S(2)}, u32[]{:S(2)}) collective-permute-start(bf16[448,512]{1,0:T(8,128)(2,1)} %get-tuple-element.44), channel_id=1, source_target_pairs={{1,2},{3,4},{5,6},{7,8},{9,10},{11,12},{13,14},{2,1},{4,3},{6,5},{... | collective-permute-start | bytes 1376264 | tf_op jit(solution)/shard_map/ppermute | solution.py:707
  31.1 29.1 %all-to-all-start = ((f32[128,8,128]{2,1,0:T(8,128)}), f32[128,8,128]{2,1,0:T(8,128)}, u32[]{:S(2)}, u32[]{:S(2)}) async-start(f32[128,8,128]{2,1,0:T(8,128)} %bitcast.6), calls=%async_computation | async-start | bytes 1048576 | tf_op jit(solution)/shard_map/all_to_all | solution.py:755
  47.2 2.6 %collective-permute-start.4 = (bf16[16,16,128]{2,1,0:T(8,128)(2,1)S(1)}, bf16[16,16,128]{2,1,0:T(8,128)(2,1)S(1)}, u32[]{:S(2)}, u32[]{:S(2)}) collective-permute-start(bf16[16,16,128]{2,1,0:T(8,128)(2,1)S(1)} %get-tuple-element.46), channel_id=1, source_target_pairs={{0,16},{16,0},{32,48},{48,32},{64,80},{80,64},{96,112},{112,96},{1... | collective-permute-start | bytes 196616 | tf_op jit(solution)/shard_map/ppermute | solution.py:707
  47.3 5.6 %collective-permute-start.5 = (bf16[16,16,128]{2,1,0:T(8,128)(2,1)S(1)}, bf16[16,16,128]{2,1,0:T(8,128)(2,1)S(1)}, u32[]{:S(2)}, u32[]{:S(2)}) collective-permute-start(bf16[16,16,128]{2,1,0:T(8,128)(2,1)S(1)} %get-tuple-element.47), channel_id=1, source_target_pairs={{16,32},{48,64},{80,96},{32,16},{64,48},{96,80},{17,33},{49,65},{8... | collective-permute-start | bytes 196616 | tf_op jit(solution)/shard_map/ppermute | solution.py:707
  54.1 9.2 %collective-permute-start.6 = (bf16[14,16,128]{2,1,0:T(8,128)(2,1)}, bf16[14,16,128]{2,1,0:T(8,128)(2,1)}, u32[]{:S(2)}, u32[]{:S(2)}) collective-permute-start(bf16[14,16,128]{2,1,0:T(8,128)(2,1)} %get-tuple-element.50), channel_id=1, source_target_pairs={{0,1},{1,0},{2,3},{3,2},{4,5},{5,4},{6,7},{7,6},{8,9},{9,8},{10,11... | collective-permute-start | bytes 172040 | tf_op jit(solution)/shard_map/ppermute | solution.py:707
  55.8 8.5 %collective-permute-start.7 = (bf16[14,16,128]{2,1,0:T(8,128)(2,1)}, bf16[14,16,128]{2,1,0:T(8,128)(2,1)}, u32[]{:S(2)}, u32[]{:S(2)}) collective-permute-start(bf16[14,16,128]{2,1,0:T(8,128)(2,1)} %get-tuple-element.51), channel_id=1, source_target_pairs={{1,2},{3,4},{5,6},{7,8},{9,10},{11,12},{13,14},{2,1},{4,3},{6,5},{... | collective-permute-start | bytes 172040 | tf_op jit(solution)/shard_map/ppermute | solution.py:707
  65.3 21.4 %copy-start.11 = (f32[64,8,128]{2,1,0:T(8,128)S(1)}, f32[64,8,128]{2,1,0:T(8,128)}, u32[]{:S(2)}) copy-start(f32[64,8,128]{2,1,0:T(8,128)} %copy-done.10) | copy-start | bytes 786436
  71.4 2.0 %collective-permute-start.8 = (f32[34,8,128]{2,1,0:T(8,128)S(1)}, f32[34,8,128]{2,1,0:T(8,128)S(1)}, u32[]{:S(2)}, u32[]{:S(2)}) collective-permute-start(f32[34,8,128]{2,1,0:T(8,128)S(1)} %get-tuple-element.57), channel_id=1, source_target_pairs={{0,16},{16,0},{32,48},{48,32},{64,80},{80,64},{96,112},{112,96},{1... | collective-permute-start | bytes 417800 | tf_op jit(solution)/shard_map/ppermute | solution.py:707
  71.5 6.4 %collective-permute-start.9 = (f32[34,8,128]{2,1,0:T(8,128)S(1)}, f32[34,8,128]{2,1,0:T(8,128)S(1)}, u32[]{:S(2)}, u32[]{:S(2)}) collective-permute-start(f32[34,8,128]{2,1,0:T(8,128)S(1)} %get-tuple-element.58), channel_id=1, source_target_pairs={{16,32},{48,64},{80,96},{32,16},{64,48},{96,80},{17,33},{49,65},{8... | collective-permute-start | bytes 417800 | tf_op jit(solution)/shard_map/ppermute | solution.py:707
  78.5 4.5 %collective-permute-start.10 = (f32[12,8,128]{2,1,0:T(8,128)S(1)}, f32[12,8,128]{2,1,0:T(8,128)S(1)}, u32[]{:S(2)}, u32[]{:S(2)}) collective-permute-start(f32[12,8,128]{2,1,0:T(8,128)S(1)} %get-tuple-element.61), channel_id=1, source_target_pairs={{0,1},{1,0},{2,3},{3,2},{4,5},{5,4},{6,7},{7,6},{8,9},{9,8},{10,11... | collective-permute-start | bytes 147464 | tf_op jit(solution)/shard_map/ppermute | solution.py:707
  78.6 8.1 %collective-permute-start.11 = (f32[12,8,128]{2,1,0:T(8,128)S(1)}, f32[12,8,128]{2,1,0:T(8,128)S(1)}, u32[]{:S(2)}, u32[]{:S(2)}) collective-permute-start(f32[12,8,128]{2,1,0:T(8,128)S(1)} %get-tuple-element.62), channel_id=1, source_target_pairs={{1,2},{3,4},{5,6},{7,8},{9,10},{11,12},{13,14},{2,1},{4,3},{6,5},{... | collective-permute-start | bytes 147464 | tf_op jit(solution)/shard_map/ppermute | solution.py:707
  91.2 6.4 %collective-permute-start.13 = (f32[34,8,128]{2,1,0:T(8,128)S(1)}, f32[34,8,128]{2,1,0:T(8,128)S(1)}, u32[]{:S(2)}, u32[]{:S(2)}) collective-permute-start(f32[34,8,128]{2,1,0:T(8,128)S(1)} %get-tuple-element.68), channel_id=1, source_target_pairs={{16,32},{48,64},{80,96},{32,16},{64,48},{96,80},{17,33},{49,65},{8... | collective-permute-start | bytes 417800 | tf_op jit(solution)/shard_map/ppermute | solution.py:707
  93.1 4.4 %collective-permute-start.12 = (f32[34,8,128]{2,1,0:T(8,128)S(1)}, f32[34,8,128]{2,1,0:T(8,128)S(1)}, u32[]{:S(2)}, u32[]{:S(2)}) collective-permute-start(f32[34,8,128]{2,1,0:T(8,128)S(1)} %get-tuple-element.67.refs_0_), channel_id=1, source_target_pairs={{0,16},{16,0},{32,48},{48,32},{64,80},{80,64},{96,112},{112,96},{1... | collective-permute-start | bytes 417800 | tf_op jit(solution)/shard_map/ppermute | solution.py:707
  98.2 5.0 %collective-permute-start.14 = (f32[12,8,128]{2,1,0:T(8,128)S(1)}, f32[12,8,128]{2,1,0:T(8,128)S(1)}, u32[]{:S(2)}, u32[]{:S(2)}) collective-permute-start(f32[12,8,128]{2,1,0:T(8,128)S(1)} %get-tuple-element.71), channel_id=1, source_target_pairs={{0,1},{1,0},{2,3},{3,2},{4,5},{5,4},{6,7},{7,6},{8,9},{9,8},{10,11... | collective-permute-start | bytes 147464 | tf_op jit(solution)/shard_map/ppermute | solution.py:707
  98.3 8.1 %collective-permute-start.15 = (f32[12,8,128]{2,1,0:T(8,128)S(1)}, f32[12,8,128]{2,1,0:T(8,128)S(1)}, u32[]{:S(2)}, u32[]{:S(2)}) collective-permute-start(f32[12,8,128]{2,1,0:T(8,128)S(1)} %get-tuple-element.72), channel_id=1, source_target_pairs={{1,2},{3,4},{5,6},{7,8},{9,10},{11,12},{13,14},{2,1},{4,3},{6,5},{... | collective-permute-start | bytes 147464 | tf_op jit(solution)/shard_map/ppermute | solution.py:707
  (15 other events, 86.9 us)

commit v2 on v1

--- a/solution.py
+++ b/solution.py
@@ -11,10 +11,11 @@
 WIDE = COLS + 4
 PLACES = (ROWS + 4) * WIDE
 F32, BF16 = jnp.float32, jnp.bfloat16
-VMEM_BYTES = 16 * 1024 * 1024
+VMEM_BYTES, VMEM_MOST = 16 * 1024 * 1024, 63 * 1000 * 1000
 NODE, WIDTH = 64, 512
 FIELD, ADDEND, SUM0, SUM1, SUM2, SUM3, COEF = (i * OWN for i in range(7))
-PX_BASE, PY_BASE = COLS * NODE, (ROWS + 2) * NODE
+PX_BASE, PY_BASE = COLS * NODE, 2 * NODE
+KNOWN, ROOM = COEF + 4 * ROWS, 12288
 
 
 def place(row, col):
@@ -47,6 +48,10 @@
 def joined(pair):
     pair = pair.astype(F32)
     return pair[:8] + pair[8:]
+
+
+def parity():
+    return lax.axis_index("px") % 2, lax.axis_index("py") % 2
 
 
 def sides(par_ref, axis, near, far):
@@ -68,6 +73,9 @@
         for ref in refs:
             for made in self.coming.pop(id(ref), ()):
                 made.wait()
+
+    def fetch(self, source, target):
+        self.coming[id(target)] = [self.copy(source, target)]
 
     def send(self, source, target):
         self.going.append(self.copy(source, target))
@@ -80,7 +88,7 @@
             made.wait()
 
 
-def call(kernel, outs, inputs, scratch=(), copies=0):
+def call(kernel, outs, inputs, scratch=(), copies=0, vmem=VMEM_BYTES):
     spaces = {"s": pltpu.SMEM, "v": pltpu.VMEM, "h": pltpu.HBM, "b": pltpu.HBM}
     arrays = [array for array, _ in inputs]
     fetched = [i for i, (_, kind) in enumerate(inputs) if kind == "h"]
@@ -103,7 +111,7 @@
         in_specs=[pl.BlockSpec(memory_space=spaces[kind]) for _, kind in inputs],
         out_specs=[pl.BlockSpec(memory_space=spaces[kind]) for _, _, kind in outs],
         scratch_shapes=list(scratch) + buffers + [pltpu.SemaphoreType.DMA((max(total, 1),))],
-        compiler_params=pltpu.CompilerParams(vmem_limit_bytes=VMEM_BYTES),
+        compiler_params=pltpu.CompilerParams(vmem_limit_bytes=vmem),
     )(*arrays)
 
 
@@ -194,19 +202,30 @@
 
 
 def start_kernel(
-    flow, par, field, memory, charge, offsets, stiffness, m_even, m_odd, n_even, n_odd, lines, plain, addend, scratch
+    flow, steps, observed, part, node, offsets, field, memory, charge, stiffness,
+    m_even_out, m_odd_out, both_out, d_even_out, d_odd_out, lines, sent,
+    plain, addend, scratch, slots_of, m_even, m_odd, both, d_even, d_odd,
 ):
+    par = parity()
     for out, edge in zip((m_even, m_odd), sides(par, 0, ROWS - 1, 0)):
-        for y in range(COLS):
-            flow.send(stiffness.at[edge, y], out.at[pl.ds(y * NODE, NODE), :])
-    for out, edge in zip((n_even, n_odd), sides(par, 1, COLS - 1, 0)):
-        for x in range(ROWS):
-            flow.send(stiffness.at[x, edge], out.at[pl.ds(x * NODE, NODE), :])
+        flow.coming[id(out)] = [
+            flow.copy(stiffness.at[edge, y], out.at[pl.ds(y * NODE, NODE), :]) for y in range(COLS)
+        ]
+    for out, edge in zip((d_even, d_odd), sides(par, 1, COLS - 1, 0)):
+        flow.coming[id(out)] = [flow.copy(stiffness.at[x, edge], out.at[x]) for x in range(ROWS)]
+    flow.wait(steps, observed, part, node)
+    owner_slots(steps, observed, part, node, slots_of)
+    flow.send(slots_of, sent)
     flow.wait(offsets)
     found = shift_lines(offsets)
     lines[...] = found
     px_tiles = [Tiles(m_even, PX_BASE), Tiles(m_odd, PX_BASE)]
-    py_tiles = [Tiles(n_even, PY_BASE), Tiles(n_odd, PY_BASE)]
+    py_tiles = [Tiles(both.at[0], PY_BASE), Tiles(both.at[1], PY_BASE)]
+    flow.wait(m_even, m_odd, d_even, d_odd)
+    for source, out in ((m_even, m_even_out), (m_odd, m_odd_out)):
+        flow.send(source.at[pl.ds(0, PX_BASE), :], out.at[pl.ds(0, PX_BASE), :])
+    flow.send(d_even, d_even_out)
+    flow.send(d_odd, d_odd_out)
     for out, edge in zip(px_tiles, sides(par, 0, ROWS - 1, 0)):
         line = jnp.where(edge == 0, found[0:1], found[ROWS - 1 : ROWS])
         out[16] = jnp.broadcast_to(line, (16, 128)).astype(BF16)
@@ -225,26 +244,31 @@
     to_plain(total, scratch, addend)
     get, add = (lambda at: plain[at]), (lambda at: addend[at])
     px_message(par, get, add, px_tiles)
+    for source, out in ((m_even, m_even_out), (m_odd, m_odd_out)):
+        flow.send(source.at[pl.ds(PX_BASE, 80), :], out.at[pl.ds(PX_BASE, 80), :])
     py_message(par, get, add, py_tiles)
-
-
-def first_py_kernel(flow, par, r_even, r_odd, in_even, in_odd, n_even, n_odd):
-    n_even[...] = in_even[...]
-    n_odd[...] = in_odd[...]
+    flow.send(both.at[:, pl.ds(PY_BASE, 64), :], both_out.at[:, pl.ds(PY_BASE, 64), :])
+
+
+def first_py_kernel(flow, r_even, r_odd, given, n_even, n_odd):
+    par = parity()
+    n_even[...] = given[0]
+    n_odd[...] = given[1]
     tiles = [Tiles(r_even, PX_BASE), Tiles(r_odd, PX_BASE)]
     outs = [Tiles(n_even, PY_BASE), Tiles(n_odd, PY_BASE)]
     py_fill(par, tiles[0], tiles[1], outs)
     row = lax.broadcasted_iota(jnp.int32, (16, 128), 0)
-    for out, source, edge in zip((n_even, n_odd), (in_even, in_odd), sides(par, 1, COLS - 1, 0)):
+    for out, edge in zip((n_even, n_odd), sides(par, 1, COLS - 1, 0)):
         for k, got in enumerate((r_even, r_odd)):
-            out[pl.ds((ROWS + k) * NODE, NODE), :] = got[pl.ds(edge * NODE, NODE), :]
-    for out, source in zip(outs, (Tiles(in_even, PY_BASE), Tiles(in_odd, PY_BASE))):
+            out[pl.ds(k * NODE, NODE), :] = got[pl.ds(edge * NODE, NODE), :]
+    for out in outs:
         even, odd = tiles[0][16].astype(F32), tiles[1][16].astype(F32)
-        own = source[14].astype(F32)
+        own = out[14].astype(F32)
         out[14] = jnp.where(row == ROWS, even, jnp.where(row == ROWS + 1, odd, own)).astype(BF16)
 
 
-def second_py_kernel(flow, par, r_even, r_odd, in_even, in_odd, n_even, n_odd):
+def second_py_kernel(flow, r_even, r_odd, in_even, in_odd, n_even, n_odd):
+    par = parity()
     n_even[...] = in_even[...]
     n_odd[...] = in_odd[...]
     py_fill(par, Tiles(r_even), Tiles(r_odd), (Tiles(n_even), Tiles(n_odd)))
@@ -288,7 +312,7 @@
             return acc
 
         to_plain(part, scratch, region(base))
-    flow.send(full, out)
+    flow.send(full, out.at[pl.ds(0, KNOWN)])
 
 
 class Coefs:
@@ -312,14 +336,16 @@
 
 
 def weight_of(blocks, item):
-    own, r_even, r_odd, n_even, n_odd = blocks
+    own, r_even, r_odd, n_even, n_odd, d_even, d_odd = blocks
     if item < OWN:
         return own[item // COLS, item % COLS]
     item -= OWN
-    for array, count in ((r_even, COLS), (r_odd, COLS), (n_even, ROWS + 2), (n_odd, ROWS + 2)):
-        if item < count:
-            return array[pl.ds(item * NODE, NODE), :]
-        item -= count
+    if item < 2 * COLS:
+        return (r_even, r_odd)[item // COLS][pl.ds(item % COLS * NODE, NODE), :]
+    side, j = (item - 2 * COLS) // (ROWS + 2), (item - 2 * COLS) % (ROWS + 2)
+    if j < ROWS:
+        return (d_even, d_odd)[side][j]
+    return (n_even, n_odd)[side][pl.ds((j - ROWS) * NODE, NODE), :]
 
 
 def targets_of(table, par):
@@ -330,7 +356,7 @@
             return table[item // COLS, (item % COLS) * 8 + k]
         item -= OWN + 2 * COLS
         side, j = item // (ROWS + 2), item % (ROWS + 2)
-        return table[8 * (side + 1) + j, columns[side] * 8 + k]
+        return table[8 + j, columns[side] * 8 + k + 64 * side]
 
     return target
 
@@ -344,8 +370,10 @@
     odd = Tiles(r_odd, PX_BASE)[16].astype(F32)[:8]
     first = jnp.where(row == ROWS, even, jnp.where(row == ROWS + 1, odd, lines))
     parts = [first.astype(jnp.int32) + place(line, lane // 8)]
+    ends = []
     for msg, col in zip((n_even, n_odd), sides(par, 1, COLS, -1)):
-        parts.append(Tiles(msg, PY_BASE)[14].astype(F32)[:8].astype(jnp.int32) + place(line, col))
+        ends.append(Tiles(msg, PY_BASE)[14].astype(F32)[:8].astype(jnp.int32) + place(line, col))
+    parts.append(jnp.where(lane < 64, ends[0], pltpu.roll(ends[1], 64, 1)))
     return jnp.concatenate(parts, 0)
 
 
@@ -397,25 +425,28 @@
 
 
 def forward_one(
-    flow, par, lines, own, r_even, r_odd, n_even, n_odd, known, past, now, m_even, m_odd, p_even, p_odd, table_out,
-    field, middle, table, codes, older,
+    flow, lines, own, r_even, r_odd, n_even, n_odd, d_even, d_odd, stored, past, now, m_even, m_odd, p_even, p_odd, table_out,
+    field, middle, table, known,
 ):
+    par = parity()
+    begun = flow.copy(stored.at[pl.ds(0, 2 * OWN)], known.at[pl.ds(0, 2 * OWN)])
+    rest = flow.copy(stored.at[pl.ds(2 * OWN, KNOWN - 2 * OWN)], known.at[pl.ds(2 * OWN, KNOWN - 2 * OWN)])
     table_out[...] = table_lines(par, lines[...], r_even, r_odd, n_even, n_odd)
     looked = flow.copy(table_out, table)
     coef = Coefs(known.at[pl.ds(COEF, 4 * ROWS)])
 
     def ready():
         looked.wait()
-        flow.wait(known)
+        begun.wait()
 
     def first(block, out):
+        if block == 0:
+            rest.wait()
         got = out + known[ADDEND + block]
-        older[block] = got
+        past[block] = got
         full = known[SUM2 + block] + coef(1, block) * got
-        older[OWN + block] = full
+        past[OWN + block] = full
         now[OWN + block] = -coef(0, block) * full
-        if block == OWN - 1:
-            flow.send(older, past)
         return got
 
     def second(block, out):
@@ -423,21 +454,23 @@
 
     received = (Tiles(r_even, PX_BASE), Tiles(r_odd, PX_BASE), Tiles(n_even, PY_BASE), Tiles(n_odd, PY_BASE))
     forward_pair(
-        par, targets_of(table, par), ready, (own, r_even, r_odd, n_even, n_odd), lambda block: known[FIELD + block],
+        par, targets_of(table, par), ready, (own, r_even, r_odd, n_even, n_odd, d_even, d_odd), lambda block: known[FIELD + block],
         received, field, middle, first, second,
     )
     get, add = (lambda at: now[at]), (lambda at: now[OWN + at])
     px_message(par, get, add, (Tiles(m_even), Tiles(m_odd)))
     py_message(par, get, add, (Tiles(p_even), Tiles(p_odd)))
     for block in range(OWN):
-        now[2 * OWN + block] = known[SUM3 + block] + coef(2, block) * older[block] + coef(1, block) * now[block]
+        now[2 * OWN + block] = known[SUM3 + block] + coef(2, block) * past[block] + coef(1, block) * now[block]
 
 
 def turn_kernel(
-    flow, par, table, tally, own, r_even, r_odd, n_even, n_odd, e_even, e_odd, s_even, s_odd, now, coefs, spread, counted,
-    adjoint4, first_out, second_out, m_even, m_odd, field, middle, sums_one, sums_two, field3, field4, start_out,
+    flow, table, own, r_even, r_odd, n_even, n_odd, d_even, d_odd, e_even, e_odd, s_even, s_odd, now, stored, spread, counted,
+    adjoint4, first_out, second_out, m_even, m_odd, field, middle, sums_one, sums_two, field3, field4, coefs,
 ):
-    blocks = (own, r_even, r_odd, n_even, n_odd)
+    par = parity()
+    flow.fetch(stored.at[pl.ds(COEF, 4 * ROWS)], coefs)
+    blocks = (own, r_even, r_odd, n_even, n_odd, d_even, d_odd)
     target = targets_of(table, par)
     coef = Coefs(coefs)
 
@@ -447,28 +480,26 @@
         return got
 
     def second(block, out):
+        if block == 0:
+            flow.wait(coefs)
         field4[block] = out - coef(0, block) * now[2 * OWN + block]
 
     received = (Tiles(e_even), Tiles(e_odd), Tiles(s_even), Tiles(s_odd))
     clear(sums_one, sums_two)
     forward_pair(
-        par, target, lambda: flow.wait(coefs), blocks, lambda block: now[block], received, field, middle, first, second
-    )
-    flow.wait(spread, counted)
-
+        par, target, lambda: None, blocks, lambda block: now[block], received, field, middle, first, second
+    )
     def start(block):
-        value = injected(tally, 4, counted, field4[block], spread, block)
-        start_out[block] = value
-        if block == OWN - 1:
-            flow.send(start_out, adjoint4)
+        value = injected(4, counted, field4[block], spread, block)
+        adjoint4[block] = value
         return value
 
     def add_first(block):
-        return injected(tally, 3, counted, field3[block], spread, block)
+        return injected(3, counted, field3[block], spread, block)
 
     def add_second(block):
-        memory = coef(0, block) * coef(1, block) * start_out[block]
-        return injected(tally, 2, counted, now[block], spread, block) - memory
+        memory = coef(0, block) * coef(1, block) * adjoint4[block]
+        return injected(2, counted, now[block], spread, block) - memory
 
     adjoint_pair(
         par, target, blocks, start, add_first, add_second, (first_out, second_out, m_even, m_odd), sums_one, sums_two
@@ -513,8 +544,8 @@
         value = both(middle, at)
         push(last, OWN + number, value[:, :64].astype(BF16))
     for out, row in zip((m_even, m_odd), rows_at):
-        for j in range(COLS + 2):
-            out[j] = plain_of(both(middle, place(row, j - 1)))
+        for j in range(0, COLS + 2, 2):
+            out[j // 2] = paired(plain_of(both(middle, place(row, j + i - 1))) for i in range(2))
     for x in range(ROWS):
         for j in range(COLS + 2):
             value = plain_of(both(middle, place(x, j - 1)))
@@ -525,8 +556,9 @@
             first_out[x * (COLS + 2) + j] = value
     for out, base in zip((m_even, m_odd), sides(par, 0, ROWS, -2)):
         for k in range(2):
-            for j in range(WIDE):
-                out[COLS + 2 + k * WIDE + j] = plain_of(both(last, place(base + k, j - 2)))
+            for j in range(0, WIDE, 2):
+                at = COLS // 2 + 1 + (k * WIDE + j) // 2
+                out[at] = paired(plain_of(both(last, place(base + k, j + i - 2))) for i in range(2))
     for x in range(ROWS):
         for j in range(WIDE):
             value = plain_of(both(last, place(x, j - 2)))
@@ -535,20 +567,31 @@
             second_out[x * WIDE + j] = value
 
 
-def adjoint_py_kernel(flow, par, first, second, r_even, r_odd, first_own, second_own, n_even, n_odd, one, two):
+def paired(blocks):
+    return jnp.concatenate(list(blocks), 0).astype(BF16)
+
+
+def add_pair(target, at, pair):
+    both = pair.astype(F32)
+    target[at] += both[:8]
+    target[at + 1] += both[8:]
+
+
+def adjoint_py_kernel(flow, first, second, r_even, r_odd, first_own, second_own, n_even, n_odd, one, two):
+    par = parity()
     one[...] = first[...]
     two[...] = second[...]
     for msg, row, base in zip((r_even, r_odd), sides(par, 0, 3, 0), sides(par, 0, 2, 0)):
-        for j in range(COLS + 2):
-            one[row * (COLS + 2) + j] += msg[j]
+        for j in range(0, COLS + 2, 2):
+            add_pair(one, row * (COLS + 2) + j, msg[j // 2])
         for k in range(2):
-            for j in range(WIDE):
-                two[(base + k) * WIDE + j] += msg[COLS + 2 + k * WIDE + j]
+            for j in range(0, WIDE, 2):
+                add_pair(two, (base + k) * WIDE + j, msg[COLS // 2 + 1 + (k * WIDE + j) // 2])
     for out, col, base in zip((n_even, n_odd), sides(par, 1, COLS + 1, 0), sides(par, 1, COLS + 2, 0)):
         for x in range(ROWS):
-            out[x] = one[x * (COLS + 2) + col]
-            for k in range(2):
-                out[ROWS + 2 * x + k] = two[x * WIDE + base + k]
+            out[2 + x] = paired(two[x * WIDE + base + k] for k in range(2))
+        for h in range(2):
+            out[h] = paired(one[(2 * h + i) * (COLS + 2) + col] for i in range(2))
     for x in range(ROWS):
         for y in range(COLS):
             first_own[x * COLS + y] = one[x * (COLS + 2) + 1 + y]
@@ -560,43 +603,47 @@
     second[...] = second_own[...]
     for msg, col, base in zip((n_even, n_odd), sides(par, 1, 7, 0), sides(par, 1, 6, 0)):
         for x in range(ROWS):
-            first[x * COLS + col] += msg[x]
-            for k in range(2):
-                second[x * COLS + base + k] += msg[ROWS + 2 * x + k]
-
-
-def injected(tally, moment, counted, field, spread, block):
-    return tally[moment] * counted[block] * field - spread[moment - 1, block]
+            add_pair(second, x * COLS + base, msg[2 + x])
+        for h in range(2):
+            both = msg[h].astype(F32)
+            first[2 * h * COLS + col] += both[:8]
+            first[(2 * h + 1) * COLS + col] += both[8:]
+
+
+def injected(moment, counted, field, spread, block):
+    return counted[moment - 1, block] * field - spread[moment - 1, block]
 
 
 def adjoint_two(
-    flow, par, table, tally, own, r_even, r_odd, n_even, n_odd, first_own, second_own, e_even, e_odd, adjoint4, past, coefs,
-    spread, counted, later, first_out, second_out, m_even, m_odd, sums_one, sums_two, adjoint3, adjoint2,
+    flow, table, own, r_even, r_odd, n_even, n_odd, d_even, d_odd, first_own, second_own, e_even, e_odd, adjoint4, past, stored,
+    spread, counted, later, first_out, second_out, m_even, m_odd, sums_one, sums_two, coefs,
 ):
+    par = parity()
+    flow.fetch(stored.at[pl.ds(COEF, 4 * ROWS)], coefs)
     clear(sums_one, sums_two)
+    adjoint3, adjoint2 = later.at[pl.ds(0, OWN)], later.at[pl.ds(OWN, OWN)]
     settle(par, first_own, second_own, e_even, e_odd, adjoint3, adjoint2)
-    flow.send(adjoint3, later.at[pl.ds(0, OWN)])
-    flow.send(adjoint2, later.at[pl.ds(OWN, OWN)])
     coef = Coefs(coefs)
 
     def add_first(block):
         if block == 0:
-            flow.wait(adjoint4, past, coefs, spread, counted)
+            flow.wait(coefs)
         memory = coef(2, block) * adjoint4[block] + coef(1, block) * adjoint3[block]
-        return injected(tally, 1, counted, past[block], spread, block) - coef(0, block) * memory
+        return injected(1, counted, past[block], spread, block) - coef(0, block) * memory
 
     def add_second(block):
         memory = coef(3, block) * adjoint4[block] + coef(2, block) * adjoint3[block] + coef(1, block) * adjoint2[block]
         return -coef(0, block) * memory
 
     adjoint_pair(
-        par, targets_of(table, par), (own, r_even, r_odd, n_even, n_odd), lambda block: adjoint2[block], add_first,
+        par, targets_of(table, par), (own, r_even, r_odd, n_even, n_odd, d_even, d_odd), lambda block: adjoint2[block], add_first,
         add_second, (first_out, second_out, m_even, m_odd), sums_one, sums_two,
     )
 
 
-def gradient_kernel(flow, after, adjoint4, later, known, past, now, out):
-    flow.wait(adjoint4, later, known, past, now)
+def gradient_kernel(flow, after, adjoint4, later, stored, past, now, out, known):
+    flow.fetch(stored.at[pl.ds(0, KNOWN)], known)
+    flow.wait(known)
     for block in range(OWN):
         out[block] = (
             adjoint4[block] * now[2 * OWN + block] + later[block] * past[OWN + block]
@@ -606,8 +653,9 @@
 
 
 def finish_kernel(
-    flow, par, first_own, second_own, n_even, n_odd, before, result, gradient, adjoint1, adjoint0, scratch
+    flow, first_own, second_own, n_even, n_odd, before, result, gradient, adjoint1, adjoint0, scratch
 ):
+    par = parity()
     settle(par, first_own, second_own, n_even, n_odd, adjoint1, adjoint0)
     for x in range(ROWS):
         parts = []
@@ -627,10 +675,9 @@
     return high, (value - high.astype(F32)).astype(BF16)
 
 
-def owner_kernel(flow, steps, after, observed, part, node, out, slots_of):
-    flow.wait(observed, part, node)
+def owner_slots(steps, observed, part, node, slots_of):
     owned = observed.shape[0]
-    slots = out.shape[0]
+    slots = slots_of.shape[0]
     devices = slots // CAP
     row = lax.broadcasted_iota(jnp.int32, (128, 128), 0)
     col = lax.broadcasted_iota(jnp.int32, (128, 128), 1)
@@ -638,7 +685,7 @@
     source = row % 16
     step = jnp.zeros((128, 128), jnp.int32)
     for g in range(8):
-        step = jnp.where(gate == g, steps[g], step)
+        step = jnp.where(gate == g, jnp.broadcast_to(steps[0:1, g : g + 1], (128, 128)), step)
     wanted = 2 * (col % 8) + (col // 8) % 2
     chosen = ((step == col // 16 + 1) & (source == wanted) & (col < 64)).astype(F32).astype(BF16)
     high, low = split(observed[...])
@@ -661,11 +708,16 @@
     high, low = split(sums)
     turned = lambda a, b: lax.dot_general(a, b, (((1,), (1,)), ((), ())), preferred_element_type=F32)
     slots_of[...] = dot(where, high) + dot(where, low) + turned(where, marks.astype(F32).astype(BF16))
-    flow.send(slots_of, out)
-
-
-def holder_kernel(flow, slots, spread_out, counted_out, spread, counted):
+
+
+def holder_kernel(flow, steps, slots, after, spread, counted):
     flow.wait(slots)
+    tally = []
+    for n in range(4):
+        total = jnp.zeros((), F32)
+        for g in range(8):
+            total = total + jnp.where(steps[g] == n + 1, 1.0, 0.0)
+        tally.append(total)
     values = slots[...]
     count = values.shape[0]
     lane = lax.broadcasted_iota(jnp.int32, (count, 128), 1)
@@ -688,10 +740,9 @@
                 spread[n, first + 1] = jnp.where(low8, pltpu.roll(even, 64, 1), odd)
             many = jnp.broadcast_to(out[66:67, j * 128 : (j + 1) * 128], (8, 128))
             other = pltpu.roll(many, 64, 1)
-            counted[first] = jnp.where(low8, many, other)
-            counted[first + 1] = jnp.where(low8, other, many)
-    flow.send(spread, spread_out)
-    flow.send(counted, counted_out)
+            for n in range(4):
+                counted[n, first] = jnp.where(low8, many, other) * tally[n]
+                counted[n, first + 1] = jnp.where(low8, other, many) * tally[n]
 
 
 def swap_even(axis):
@@ -721,8 +772,8 @@
 ):
     devices = lax.axis_size(("px", "py"))
     slots = devices * CAP
-    par = jnp.stack([lax.axis_index("px") % 2, lax.axis_index("py") % 2]).astype(jnp.int32)
     turn = pltpu.VMEM((256, 128), F32)
+    lookup = pltpu.SMEM((16, 128), jnp.int32)
     places = pltpu.VMEM((PLACES, 16, 128), BF16)
     sums = pltpu.VMEM((PLACES, 16, 128), F32)
     blocks = pltpu.VMEM((OWN, 8, 128), F32)
@@ -730,93 +781,98 @@
     py_first = ((PY_BASE + 64, WIDTH), BF16, "v")
     px_shape = ((16, 16, 128), BF16, "v")
     py_shape = ((14, 16, 128), BF16, "v")
-    m_even, m_odd, p_even, p_odd, lines = call(
-        start_kernel, [px_first, px_first, py_first, py_first, ((8, 128), F32, "v")],
+    down = ((ROWS, NODE, WIDTH), BF16, "v")
+    two = (2,) + py_first[0]
+    m_even, m_odd, both, d_even, d_odd, lines, sent = call(
+        start_kernel,
         [
-            (par, "s"), (checkpoint_field, "h"), (checkpoint_memory, "h"), (chargeability, "h"), (block_offsets, "h"),
-            (stiffness, "b"),
+            px_first[:2] + ("h",), px_first[:2] + ("h",), (two, BF16, "h"), down[:2] + ("h",), down[:2] + ("h",),
+            ((8, 128), F32, "v"), ((slots, 128), F32, "h"),
         ],
-        [blocks, blocks, turn], copies=2 * COLS + 2 * ROWS,
+        [
+            (gate_step.reshape(1, -1), "h"), (observed, "h"), (receiver_part.reshape(1, -1), "h"),
+            (receiver_node.reshape(1, -1), "h"), (block_offsets, "h"), (checkpoint_field, "h"),
+            (checkpoint_memory, "h"), (chargeability, "h"), (stiffness, "b"),
+        ],
+        [blocks, blocks, turn, pltpu.VMEM((slots, 128), F32)]
+        + [pltpu.VMEM(shape, BF16) for shape in (px_first[0], px_first[0], two, down[0], down[0])],
+        copies=2 * COLS + 2 * ROWS + 8, vmem=65 * 1000 * 1000,
     )
     r_even, r_odd = exchange("px", m_even, m_odd)
-    (known,) = call(
-        decay_kernel, [((COEF + 4 * ROWS, 8, 128), F32, "h")],
-        [(lines, "v"), (checkpoint_field, "h"), (checkpoint_memory, "h"), (chargeability, "h"), (relaxation, "h")],
-        [pltpu.VMEM((COEF + 4 * ROWS, 8, 128), F32), turn], copies=1,
-    )
-    (sent,) = call(
-        owner_kernel, [((slots, 128), F32, "h")],
-        [
-            (gate_step, "s"), (r_even, "v"), (observed, "h"), (receiver_part.reshape(1, -1), "h"),
-            (receiver_node.reshape(1, -1), "h"),
-        ],
-        [pltpu.VMEM((slots, 128), F32)], copies=1,
-    )
+    d_even, d_odd = exchange("py", d_even, d_odd)
+    sent, r_even = lax.optimization_barrier((sent, r_even))
     held = lax.all_to_all(
         sent.reshape(devices, CAP, 128), ("px", "py"), split_axis=0, concat_axis=0, tiled=True
     ).reshape(slots, 128)
     n_even, n_odd = call(
         first_py_kernel, [py_first, py_first],
-        [(par, "s"), (r_even, "v"), (r_odd, "v"), (p_even, "v"), (p_odd, "v")],
+        [(r_even, "v"), (r_odd, "v"), (both, "v")],
+    )
+    (known,) = call(
+        decay_kernel, [((ROOM, 8, 128), F32, "h")],
+        [(n_even, "v"), (checkpoint_field, "h"), (checkpoint_memory, "h"), (chargeability, "h"), (relaxation, "h")],
+        [pltpu.VMEM((KNOWN, 8, 128), F32), turn], copies=1, vmem=VMEM_MOST,
     )
     n_even, n_odd = exchange("py", n_even, n_odd)
-    tally = jnp.sum(gate_step[None, :] == jnp.arange(5, dtype=jnp.int32)[:, None], axis=1).astype(F32)
-    weights = [(a, "v") for a in (stiffness, r_even, r_odd, n_even, n_odd)]
+    held, n_even = lax.optimization_barrier((held, n_even))
+    weights = [(a, "v") for a in (stiffness, r_even, r_odd, n_even, n_odd, d_even, d_odd)]
     past, now, m_even, m_odd, p_even, p_odd, table = call(
         forward_one,
         [
-            ((2 * OWN, 8, 128), F32, "h"), ((3 * OWN, 8, 128), F32, "v"), px_shape, px_shape, py_shape, py_shape,
-            ((24, 128), jnp.int32, "v"),
+            ((2 * OWN, 8, 128), F32, "v"), ((3 * OWN, 8, 128), F32, "v"), px_shape, px_shape, py_shape, py_shape,
+            ((16, 128), jnp.int32, "v"),
         ],
-        [(par, "s"), (lines, "v")] + weights + [(known, "h")],
-        [places, places, pltpu.SMEM((24, 128), jnp.int32), pltpu.VMEM((8, 128), F32), pltpu.VMEM((2 * OWN, 8, 128), F32)],
-        copies=2,
+        [(lines, "v")] + weights + [(known, "b")],
+        [places, places, lookup, pltpu.VMEM((KNOWN, 8, 128), F32)], copies=3,
     )
     r_even, r_odd = exchange("px", m_even, m_odd)
     n_even, n_odd = call(
         second_py_kernel, [py_shape, py_shape],
-        [(par, "s"), (r_even, "v"), (r_odd, "v"), (p_even, "v"), (p_odd, "v")],
+        [(r_even, "v"), (r_odd, "v"), (p_even, "v"), (p_odd, "v")],
     )
     n_even, n_odd = exchange("py", n_even, n_odd)
     spread, counted = call(
-        holder_kernel, [((4, OWN, 8, 128), F32, "h"), ((OWN, 8, 128), F32, "h")], [(held, "h")],
-        [pltpu.VMEM((4, OWN, 8, 128), F32), blocks], copies=2,
-    )
-    coefs = known[COEF:]
+        holder_kernel, [((4, OWN, 8, 128), F32, "v"), ((4, OWN, 8, 128), F32, "v")],
+        [(gate_step, "s"), (held, "h"), (m_even, "v")],
+    )
+    coefs = pltpu.VMEM((4 * ROWS, 8, 128), F32)
+    rim = ((COLS // 2 + 1 + WIDE, 16, 128), BF16, "v")
+    rim_py = ((6, 16, 128), BF16, "v")
     pair_out = [
         ((ROWS * (COLS + 2), 8, 128), F32, "v"), ((ROWS * WIDE, 8, 128), F32, "v"),
-        ((COLS + 2 + 2 * WIDE, 8, 128), F32, "v"), ((COLS + 2 + 2 * WIDE, 8, 128), F32, "v"),
+        rim, rim,
     ]
     adjoint4, *rest = call(
-        turn_kernel, [((OWN, 8, 128), F32, "h")] + pair_out,
-        [(par, "s"), (table, "s"), (tally, "s")] + weights
-        + [(r_even, "v"), (r_odd, "v"), (n_even, "v"), (n_odd, "v"), (now, "v"), (coefs, "h"), (spread, "h"), (counted, "h")],
-        [places, places, sums, sums, blocks, blocks, blocks], copies=1,
+        turn_kernel, [PLAIN] + pair_out,
+        [(table, "s")] + weights
+        + [(r_even, "v"), (r_odd, "v"), (n_even, "v"), (n_odd, "v"), (now, "v"), (known, "b"), (spread, "v"), (counted, "v")],
+        [places, places, sums, sums, blocks, blocks, coefs], copies=1,
     )
 
     def gathered(first, second, m_even, m_odd):
         r_even, r_odd = exchange("px", m_even, m_odd)
         own_first, own_second, n_even, n_odd = call(
-            adjoint_py_kernel, [PLAIN, PLAIN, ((12, 8, 128), F32, "v"), ((12, 8, 128), F32, "v")],
-            [(par, "s"), (first, "v"), (second, "v"), (r_even, "v"), (r_odd, "v")],
+            adjoint_py_kernel, [PLAIN, PLAIN, rim_py, rim_py],
+            [(first, "v"), (second, "v"), (r_even, "v"), (r_odd, "v")],
             [pltpu.VMEM(first.shape, F32), pltpu.VMEM(second.shape, F32)],
         )
         n_even, n_odd = exchange("py", n_even, n_odd)
         return [(a, "v") for a in (own_first, own_second, n_even, n_odd)]
 
     later, *rest = call(
-        adjoint_two, [((2 * OWN, 8, 128), F32, "h")] + pair_out,
-        [(par, "s"), (table, "s"), (tally, "s")] + weights + gathered(*rest)
-        + [(adjoint4, "h"), (past, "h"), (coefs, "h"), (spread, "h"), (counted, "h")],
-        [sums, sums, blocks, blocks], copies=2,
+        adjoint_two, [((2 * OWN, 8, 128), F32, "v")] + pair_out,
+        [(table, "s")] + weights + gathered(*rest)
+        + [(adjoint4, "v"), (past, "v"), (known, "b"), (spread, "v"), (counted, "v")],
+        [sums, sums, coefs], copies=1,
     )
     (before,) = call(
         gradient_kernel, [((2 * OWN, 8, 128), F32, "v")],
-        [(rest[2], "v"), (adjoint4, "h"), (later, "h"), (known, "h"), (past, "h"), (now, "h")],
+        [(a, "b" if a is known else "v") for a in (rest[2], adjoint4, later, known, past, now)],
+        [pltpu.VMEM((KNOWN, 8, 128), F32)], copies=1,
     )
     field_out, gradient = call(
         finish_kernel, [(checkpoint_field.shape, F32, "v"), (chargeability.shape, F32, "v")],
-        [(par, "s")] + gathered(*rest) + [(before, "v")], [blocks, blocks, turn],
+        [] + gathered(*rest) + [(before, "v")], [blocks, blocks, turn],
     )
     return field_out, gradient
 

time: 109 us -> 96.3 us (0.88)
  local copies, waits for them, and re-layouts: 9.28 us -> 1.01 us
  waiting for transfers between devices: 27.1 us -> 22.1 us
  starting transfers between devices: 40.2 us -> 43.1 us
  Pallas kernels: 29.9 us -> 28.3 us
    unnamed x44 -> x10, local copies, waits for them, and re-layouts: 9.28 us -> 1.01 us
    ppermute x8 -> x9, waiting for transfers between devices: 27.1 us -> 19.1 us  [exchange(): lax.ppermute(for_odd, axis, swap_odd(axis))]
    all_to_all x1, starting transfers between devices: 8.08 us -> 11.5 us  [body(): lax.all_to_all(sent.reshape(devices, CAP, 128), ('px', 'py'), split_axis=...]
    ppermute x8 -> x9, waiting for transfers between devices: 0.02 us -> 2.94 us  [exchange(): lax.ppermute(for_even, axis, swap_even(axis))]
    pallas_call x13 -> x12, Pallas kernels: 29.9 us -> 28.3 us  [call(): pl.pallas_call(wrapped, out_shape=[jax.ShapeDtypeStruct(shape, dtype) for...]
    ppermute x8 -> x9, starting transfers between devices: 5.98 us -> 5.61 us  [exchange(): lax.ppermute(for_even, axis, swap_even(axis))]
    ppermute x8 -> x9, starting transfers between devices: 26.1 us -> 26 us  [exchange(): lax.ppermute(for_odd, axis, swap_odd(axis))]
  transfers between devices with their start and end apart: 17 -> 19, of which waited for: 7 -> 9; matrix products, arithmetic and copies ran while one was open for 0% -> 0% of each run, Pallas kernels for 11% -> 9%
where the time goes in v2:
time: 96.3 us; the launch traced here: 95.6 us
  starting transfers between devices  43.1 us (45%)
  Pallas kernels  28.3 us (29%)
  waiting for transfers between devices  22.1 us (23%)
  between operations  1.08 us (1%)
  local copies, waits for them, and re-layouts  1.01 us (1%)
    pallas_call x12, Pallas kernels, call(): pl.pallas_call(wrapped, out_shape=[jax.ShapeDtypeStruct(shape, dtype) for...  28.3 us
    ppermute x9, starting transfers between devices, exchange(): lax.ppermute(for_odd, axis, swap_odd(axis))  26 us
    ppermute x9, waiting for transfers between devices, exchange(): lax.ppermute(for_odd, axis, swap_odd(axis))  19.1 us
    all_to_all x1, starting transfers between devices, body(): lax.all_to_all(sent.reshape(devices, CAP, 128), ('px', 'py'), split_axis=...  11.5 us
    ppermute x9, starting transfers between devices, exchange(): lax.ppermute(for_even, axis, swap_even(axis))  5.61 us
    ppermute x9, waiting for transfers between devices, exchange(): lax.ppermute(for_even, axis, swap_even(axis))  2.94 us
  transfers between devices with their start and end apart: 19, of which 9 were waited for; matrix products, arithmetic and copies ran while one was open for 0% of the time, Pallas kernels for 9%

profile of v2, /device:TPU:10, one launch (start us, length us, event | category | flops | bytes accessed | tf_op | source)
XLA Modules:
  0.0 95.6 jit_solution(7798792167102867036)
XLA Ops:
  0.6 4.2 %shard_map.113 = (bf16[592,512]{1,0:T(8,128)(2,1)}, bf16[592,512]{1,0:T(8,128)(2,1)}, bf16[2,192,512]{2,1,0:T(8,128)(2,1)}, bf16[4,64,512]{2,1,0:T(8,128)(2,1)},...) custom-call(s32[1,8]{1,0:T(1,128)} %bitcast.5, f32[256,128]{1,0:T(8,128)} %refs_1_.5, ...), custom_call_target="tpu_custom_call" | custom-call | tf_op jit(solution)/shard_map/pallas_call | solution.py:108
  4.9 2.4 %collective-permute-start.1 = (bf16[592,512]{1,0:T(8,128)(2,1)}, bf16[592,512]{1,0:T(8,128)(2,1)S(1)}, u32[]{:S(2)}, u32[]{:S(2)}) collective-permute-start(bf16[592,512]{1,0:T(8,128)(2,1)} %get-tuple-element.48), channel_id=1, source_target_pairs={{16,32},{48,64},{80,96},{32,16},{64,48},{96,80},{17,33},{49,65},{8... | collective-permute-start | bytes 1818632 | tf_op jit(solution)/shard_map/ppermute | solution.py:758
  7.4 11.5 %all-to-all-start = ((f32[128,8,128]{2,1,0:T(8,128)}), f32[128,8,128]{2,1,0:T(8,128)}, u32[]{:S(2)}, u32[]{:S(2)}) async-start(f32[128,8,128]{2,1,0:T(8,128)} %bitcast.6), calls=%async_computation | async-start | bytes 1048576 | tf_op jit(solution)/shard_map/all_to_all | solution.py:804
  18.9 1.7 %collective-permute-start.4 = (bf16[4,64,512]{2,1,0:T(8,128)(2,1)}, bf16[4,64,512]{2,1,0:T(8,128)(2,1)}, u32[]{:S(2)}, u32[]{:S(2)}) collective-permute-start(bf16[4,64,512]{2,1,0:T(8,128)(2,1)} %get-tuple-element.54), channel_id=1, source_target_pairs={{0,1},{1,0},{2,3},{3,2},{4,5},{5,4},{6,7},{7,6},{8,9},{9,8},{10,11... | collective-permute-start | bytes 786440 | tf_op jit(solution)/shard_map/ppermute | solution.py:758
  20.6 4.2 %collective-permute-start.5 = (bf16[4,64,512]{2,1,0:T(8,128)(2,1)}, bf16[4,64,512]{2,1,0:T(8,128)(2,1)}, u32[]{:S(2)}, u32[]{:S(2)}) collective-permute-start(bf16[4,64,512]{2,1,0:T(8,128)(2,1)} %get-tuple-element.55), channel_id=1, source_target_pairs={{1,2},{3,4},{5,6},{7,8},{9,10},{11,12},{13,14},{2,1},{4,3},{6,5},{... | collective-permute-start | bytes 786440 | tf_op jit(solution)/shard_map/ppermute | solution.py:758
  27.5 2.9 %collective-permute-start.3 = (bf16[192,512]{1,0:T(8,128)(2,1)}, bf16[192,512]{1,0:T(8,128)(2,1)}, u32[]{:S(2)}, u32[]{:S(2)}) collective-permute-start(bf16[192,512]{1,0:T(8,128)(2,1)} %get-tuple-element.53), channel_id=1, source_target_pairs={{1,2},{3,4},{5,6},{7,8},{9,10},{11,12},{13,14},{2,1},{4,3},{6,5},{... | collective-permute-start | bytes 589832 | tf_op jit(solution)/shard_map/ppermute | solution.py:758
  30.4 3.3 %shard_map.115.refs_8_.refs_13_.refs_14_.refs_3_ = f32[12288,8,128]{2,1,0:T(8,128)} custom-call(bf16[192,512]{1,0:T(8,128)(2,1)} %copy-done.2, f32[4,8,1024]{2,1,0:T(8,128)} %refs_1_.6, f32[4,4,8,1024]{3,2,1,0:T(8,128)} %refs_2_.1, f32[4,8,64]{2,1,0:T(8,128)} %refs_3_.1, f32[4,4,8,64]{3,2,1,0:T(8,128)} %refs_4_.3), custom_call_target="tpu_custom_call" | custom-call | tf_op jit(solution)/shard_map/pallas_call | solution.py:108
  33.7 2.7 %collective-permute-done.2.refs_4_ = bf16[192,512]{1,0:T(8,128)(2,1)S(1)} collective-permute-done((bf16[192,512]{1,0:T(8,128)(2,1)S(1)}, bf16[192,512]{1,0:T(8,128)(2,1)S(1)}, u32[]{:S(2)}, u32[]{:S(2)}) %collective-permute-start.2) | collective-permute-done | bytes 196640 | tf_op jit(solution)/shard_map/ppermute | solution.py:758
  36.5 2.2 %collective-permute-done.3.refs_5_ = bf16[192,512]{1,0:T(8,128)(2,1)} collective-permute-done((bf16[192,512]{1,0:T(8,128)(2,1)}, bf16[192,512]{1,0:T(8,128)(2,1)}, u32[]{:S(2)}, u32[]{:S(2)}) %collective-permute-start.3) | collective-permute-done | bytes 196640 | tf_op jit(solution)/shard_map/ppermute | solution.py:758
  38.7 4.5 %shard_map.116 = (f32[64,8,128]{2,1,0:T(8,128)S(1)}, f32[96,8,128]{2,1,0:T(8,128)S(1)}, bf16[16,16,128]{2,1,0:T(8,128)(2,1)S(1)}, bf16[16,16,128]{2,1,0:T(8,128)...) custom-call(f32[8,128]{1,0:T(8,128)S(1)} %copy-done.3, ...), custom_call_target="tpu_custom_call" | custom-call | tf_op jit(solution)/shard_map/pallas_call | solution.py:108
  43.2 2.1 %collective-permute-start.7 = (bf16[16,16,128]{2,1,0:T(8,128)(2,1)S(1)}, bf16[16,16,128]{2,1,0:T(8,128)(2,1)S(1)}, u32[]{:S(2)}, u32[]{:S(2)}) collective-permute-start(bf16[16,16,128]{2,1,0:T(8,128)(2,1)S(1)} %get-tuple-element.58), channel_id=1, source_target_pairs={{16,32},{48,64},{80,96},{32,16},{64,48},{96,80},{17,33},{49,65},{8... | collective-permute-start | bytes 196616 | tf_op jit(solution)/shard_map/ppermute | solution.py:758
  46.3 2.5 %collective-permute-done.7.refs_1_.refs_9_ = bf16[16,16,128]{2,1,0:T(8,128)(2,1)S(1)} collective-permute-done((bf16[16,16,128]{2,1,0:T(8,128)(2,1)S(1)}, bf16[16,16,128]{2,1,0:T(8,128)(2,1)S(1)}, u32[]{:S(2)}, u32[]{:S(2)}) %collective-permute-start.7) | collective-permute-done | bytes 65568 | tf_op jit(solution)/shard_map/ppermute | solution.py:758
  49.1 3.5 %collective-permute-start.9 = (bf16[14,16,128]{2,1,0:T(8,128)(2,1)S(1)}, bf16[14,16,128]{2,1,0:T(8,128)(2,1)S(1)}, u32[]{:S(2)}, u32[]{:S(2)}) collective-permute-start(bf16[14,16,128]{2,1,0:T(8,128)(2,1)S(1)} %get-tuple-element.62), channel_id=1, source_target_pairs={{1,2},{3,4},{5,6},{7,8},{9,10},{11,12},{13,14},{2,1},{4,3},{6,5},{... | collective-permute-start | bytes 172040 | tf_op jit(solution)/shard_map/ppermute | solution.py:758
  52.5 3.4 %shard_map.118 = (f32[4,32,8,128]{3,2,1,0:T(8,128)S(1)}, f32[4,32,8,128]{3,2,1,0:T(8,128)S(1)}) custom-call(s32[8]{0:T(128)S(1)} %copy-done.4, f32[1024,128]{1,0:T(8,128)} %bitcast.4.refs_1_, bf16[16,16,128]{2,1,0:T(8,128)(2,1)S(1)} %get-tuple-element.57.refs_2_), custom_call_target="tpu_custom_call" | custom-call | tf_op jit(solution)/shard_map/pallas_call | solution.py:108
  57.2 5.8 %shard_map.119 = (f32[32,8,128]{2,1,0:T(8,128)S(1)}, f32[40,8,128]{2,1,0:T(8,128)S(1)}, f32[48,8,128]{2,1,0:T(8,128)S(1)}, bf16[17,16,128]{2,1,0:T(8,128)(2,1)S(1)}, bf16[17,16,128]{2,1,0:T(8,128)(2,1)S(1)}) custom-call(s32[16,128]{1,0:T(8,128)S(1)} %get-tuple-element.56.refs_0_, bf16[4,8,64,512]{3,2,1,0:T(8,128)(2,1)S(1)} %copy-done, ...), custom_call_target="tpu_custom_call" | custom-call | tf_op jit(solution)/shard_map/pallas_call | solution.py:108
  63.2 1.9 %collective-permute-start.11 = (bf16[17,16,128]{2,1,0:T(8,128)(2,1)S(1)}, bf16[17,16,128]{2,1,0:T(8,128)(2,1)S(1)}, u32[]{:S(2)}, u32[]{:S(2)}) collective-permute-start(bf16[17,16,128]{2,1,0:T(8,128)(2,1)S(1)} %get-tuple-element.70), channel_id=1, source_target_pairs={{16,32},{48,64},{80,96},{32,16},{64,48},{96,80},{17,33},{49,65},{8... | collective-permute-start | bytes 208904 | tf_op jit(solution)/shard_map/ppermute | solution.py:758
  65.1 3.7 %collective-permute-done.11.refs_3_ = bf16[17,16,128]{2,1,0:T(8,128)(2,1)S(1)} collective-permute-done((bf16[17,16,128]{2,1,0:T(8,128)(2,1)S(1)}, bf16[17,16,128]{2,1,0:T(8,128)(2,1)S(1)}, u32[]{:S(2)}, u32[]{:S(2)}) %collective-permute-start.11) | collective-permute-done | bytes 69664 | tf_op jit(solution)/shard_map/ppermute | solution.py:758
  69.0 3.6 %collective-permute-start.13 = (bf16[6,16,128]{2,1,0:T(8,128)(2,1)S(1)}, bf16[6,16,128]{2,1,0:T(8,128)(2,1)S(1)}, u32[]{:S(2)}, u32[]{:S(2)}) collective-permute-start(bf16[6,16,128]{2,1,0:T(8,128)(2,1)S(1)} %get-tuple-element.74), channel_id=1, source_target_pairs={{1,2},{3,4},{5,6},{7,8},{9,10},{11,12},{13,14},{2,1},{4,3},{6,5},{... | collective-permute-start | bytes 73736 | tf_op jit(solution)/shard_map/ppermute | solution.py:758
  72.8 4.0 %collective-permute-done.13.refs_11_ = bf16[6,16,128]{2,1,0:T(8,128)(2,1)S(1)} collective-permute-done((bf16[6,16,128]{2,1,0:T(8,128)(2,1)S(1)}, bf16[6,16,128]{2,1,0:T(8,128)(2,1)S(1)}, u32[]{:S(2)}, u32[]{:S(2)}) %collective-permute-start.13) | collective-permute-done | bytes 24608 | tf_op jit(solution)/shard_map/ppermute | solution.py:758
  76.8 4.2 %shard_map.121 = (f32[64,8,128]{2,1,0:T(8,128)S(1)}, f32[40,8,128]{2,1,0:T(8,128)S(1)}, f32[48,8,128]{2,1,0:T(8,128)S(1)}, bf16[17,16,128]{2,1,0:T(8,128)(2,1)S(1)}, bf16[17,16,128]{2,1,0:T(8,128)(2,1)S(1)}) custom-call(s32[16,128]{1,0:T(8,128)S(1)} %get-tuple-element.56.refs_0_, bf16[4,8,64,512]{3,2,1,0:T(8,128)(2,1)S(1)} %copy-done, ...), custom_call_target="tpu_custom_call" | custom-call | tf_op jit(solution)/shard_map/pallas_call | solution.py:108
  81.0 1.9 %collective-permute-start.15 = (bf16[17,16,128]{2,1,0:T(8,128)(2,1)S(1)}, bf16[17,16,128]{2,1,0:T(8,128)(2,1)S(1)}, u32[]{:S(2)}, u32[]{:S(2)}) collective-permute-start(bf16[17,16,128]{2,1,0:T(8,128)(2,1)S(1)} %get-tuple-element.80), channel_id=1, source_target_pairs={{16,32},{48,64},{80,96},{32,16},{64,48},{96,80},{17,33},{49,65},{8... | collective-permute-start | bytes 208904 | tf_op jit(solution)/shard_map/ppermute | solution.py:758
  84.2 2.4 %collective-permute-done.15.refs_3_ = bf16[17,16,128]{2,1,0:T(8,128)(2,1)S(1)} collective-permute-done((bf16[17,16,128]{2,1,0:T(8,128)(2,1)S(1)}, bf16[17,16,128]{2,1,0:T(8,128)(2,1)S(1)}, u32[]{:S(2)}, u32[]{:S(2)}) %collective-permute-start.15) | collective-permute-done | bytes 69664 | tf_op jit(solution)/shard_map/ppermute | solution.py:758
  86.8 3.4 %collective-permute-start.17 = (bf16[6,16,128]{2,1,0:T(8,128)(2,1)S(1)}, bf16[6,16,128]{2,1,0:T(8,128)(2,1)S(1)}, u32[]{:S(2)}, u32[]{:S(2)}) collective-permute-start(bf16[6,16,128]{2,1,0:T(8,128)(2,1)S(1)} %get-tuple-element.84), channel_id=1, source_target_pairs={{1,2},{3,4},{5,6},{7,8},{9,10},{11,12},{13,14},{2,1},{4,3},{6,5},{... | collective-permute-start | bytes 73736 | tf_op jit(solution)/shard_map/ppermute | solution.py:758
  91.5 3.1 %collective-permute-done.17.refs_3_ = bf16[6,16,128]{2,1,0:T(8,128)(2,1)S(1)} collective-permute-done((bf16[6,16,128]{2,1,0:T(8,128)(2,1)S(1)}, bf16[6,16,128]{2,1,0:T(8,128)(2,1)S(1)}, u32[]{:S(2)}, u32[]{:S(2)}) %collective-permute-start.17) | collective-permute-done | bytes 24608 | tf_op jit(solution)/shard_map/ppermute | solution.py:758
  (36 shorter events, 9.3 us)
Async XLA Ops:
  4.8 33.9 %copy-start = (bf16[4,8,64,512]{3,2,1,0:T(8,128)(2,1)S(1)}, bf16[4,8,64,512]{3,2,1,0:T(8,128)(2,1)}, u32[]{:S(2)}) copy-start(bf16[4,8,64,512]{3,2,1,0:T(8,128)(2,1)} %refs_1_.9) | copy-start | bytes 6291460
  4.8 2.6 %collective-permute-start = (bf16[592,512]{1,0:T(8,128)(2,1)}, bf16[592,512]{1,0:T(8,128)(2,1)S(1)}, u32[]{:S(2)}, u32[]{:S(2)}) collective-permute-start(bf16[592,512]{1,0:T(8,128)(2,1)} %get-tuple-element.46), channel_id=1, source_target_pairs={{0,16},{16,0},{32,48},{48,32},{64,80},{80,64},{96,112},{112,96},{1... | collective-permute-start | bytes 1818632 | tf_op jit(solution)/shard_map/ppermute | solution.py:758
  4.9 19.9 %collective-permute-start.1 = (bf16[592,512]{1,0:T(8,128)(2,1)}, bf16[592,512]{1,0:T(8,128)(2,1)S(1)}, u32[]{:S(2)}, u32[]{:S(2)}) collective-permute-start(bf16[592,512]{1,0:T(8,128)(2,1)} %get-tuple-element.48), channel_id=1, source_target_pairs={{16,32},{48,64},{80,96},{32,16},{64,48},{96,80},{17,33},{49,65},{8... | collective-permute-start | bytes 1818632 | tf_op jit(solution)/shard_map/ppermute | solution.py:758
  7.4 29.1 %all-to-all-start = ((f32[128,8,128]{2,1,0:T(8,128)}), f32[128,8,128]{2,1,0:T(8,128)}, u32[]{:S(2)}, u32[]{:S(2)}) async-start(f32[128,8,128]{2,1,0:T(8,128)} %bitcast.6), calls=%async_computation | async-start | bytes 1048576 | tf_op jit(solution)/shard_map/all_to_all | solution.py:804
  18.9 17.6 %collective-permute-start.4 = (bf16[4,64,512]{2,1,0:T(8,128)(2,1)}, bf16[4,64,512]{2,1,0:T(8,128)(2,1)}, u32[]{:S(2)}, u32[]{:S(2)}) collective-permute-start(bf16[4,64,512]{2,1,0:T(8,128)(2,1)} %get-tuple-element.54), channel_id=1, source_target_pairs={{0,1},{1,0},{2,3},{3,2},{4,5},{5,4},{6,7},{7,6},{8,9},{9,8},{10,11... | collective-permute-start | bytes 786440 | tf_op jit(solution)/shard_map/ppermute | solution.py:758
  20.6 15.9 %collective-permute-start.5 = (bf16[4,64,512]{2,1,0:T(8,128)(2,1)}, bf16[4,64,512]{2,1,0:T(8,128)(2,1)}, u32[]{:S(2)}, u32[]{:S(2)}) collective-permute-start(bf16[4,64,512]{2,1,0:T(8,128)(2,1)} %get-tuple-element.55), channel_id=1, source_target_pairs={{1,2},{3,4},{5,6},{7,8},{9,10},{11,12},{13,14},{2,1},{4,3},{6,5},{... | collective-permute-start | bytes 786440 | tf_op jit(solution)/shard_map/ppermute | solution.py:758
  24.9 1.0 %copy-start.1 = (bf16[2,192,512]{2,1,0:T(8,128)(2,1)S(1)}, bf16[2,192,512]{2,1,0:T(8,128)(2,1)}, u32[]{:S(2)}) copy-start(bf16[2,192,512]{2,1,0:T(8,128)(2,1)} %get-tuple-element.50.refs_2_) | copy-start | bytes 1179652
  25.8 12.8 %copy-start.3 = (f32[8,128]{1,0:T(8,128)S(1)}, f32[8,128]{1,0:T(8,128)}, u32[]{:S(2)}) copy-start(f32[8,128]{1,0:T(8,128)} %get-tuple-element.44.refs_0_) | copy-start | bytes 12292
  26.6 3.8 %copy-start.2 = (bf16[192,512]{1,0:T(8,128)(2,1)}, bf16[192,512]{1,0:T(8,128)(2,1)S(1)}, u32[]{:S(2)}) copy-start(bf16[192,512]{1,0:T(8,128)(2,1)S(1)} %get-tuple-element.51.refs_0_) | copy-start | bytes 589828
  26.6 9.9 %collective-permute-start.2 = (bf16[192,512]{1,0:T(8,128)(2,1)S(1)}, bf16[192,512]{1,0:T(8,128)(2,1)S(1)}, u32[]{:S(2)}, u32[]{:S(2)}) collective-permute-start(bf16[192,512]{1,0:T(8,128)(2,1)S(1)} %get-tuple-element.51.refs_0_), channel_id=1, source_target_pairs={{0,1},{1,0},{2,3},{3,2},{4,5},{5,4},{6,7},{7,6},{8,9},{9,8},{10,11... | collective-permute-start | bytes 589832 | tf_op jit(solution)/shard_map/ppermute | solution.py:758
  27.5 25.0 %copy-start.4 = (s32[8]{0:T(128)S(1)}, s32[8]{0:T(128)}, u32[]{:S(2)}) copy-start(s32[8]{0:T(128)} %refs_0_.1) | copy-start | bytes 100
  27.5 11.2 %collective-permute-start.3 = (bf16[192,512]{1,0:T(8,128)(2,1)}, bf16[192,512]{1,0:T(8,128)(2,1)}, u32[]{:S(2)}, u32[]{:S(2)}) collective-permute-start(bf16[192,512]{1,0:T(8,128)(2,1)} %get-tuple-element.53), channel_id=1, source_target_pairs={{1,2},{3,4},{5,6},{7,8},{9,10},{11,12},{13,14},{2,1},{4,3},{6,5},{... | collective-permute-start | bytes 589832 | tf_op jit(solution)/shard_map/ppermute | solution.py:758
  43.2 5.6 %collective-permute-start.7 = (bf16[16,16,128]{2,1,0:T(8,128)(2,1)S(1)}, bf16[16,16,128]{2,1,0:T(8,128)(2,1)S(1)}, u32[]{:S(2)}, u32[]{:S(2)}) collective-permute-start(bf16[16,16,128]{2,1,0:T(8,128)(2,1)S(1)} %get-tuple-element.58), channel_id=1, source_target_pairs={{16,32},{48,64},{80,96},{32,16},{64,48},{96,80},{17,33},{49,65},{8... | collective-permute-start | bytes 196616 | tf_op jit(solution)/shard_map/ppermute | solution.py:758
  45.3 3.5 %collective-permute-start.6 = (bf16[16,16,128]{2,1,0:T(8,128)(2,1)S(1)}, bf16[16,16,128]{2,1,0:T(8,128)(2,1)S(1)}, u32[]{:S(2)}, u32[]{:S(2)}) collective-permute-start(bf16[16,16,128]{2,1,0:T(8,128)(2,1)S(1)} %get-tuple-element.57.refs_2_), channel_id=1, source_target_pairs={{0,16},{16,0},{32,48},{48,32},{64,80},{80,64},{96,112},{112,96},{1... | collective-permute-start | bytes 196616 | tf_op jit(solution)/shard_map/ppermute | solution.py:758
  48.8 7.1 %collective-permute-start.8 = (bf16[14,16,128]{2,1,0:T(8,128)(2,1)S(1)}, bf16[14,16,128]{2,1,0:T(8,128)(2,1)S(1)}, u32[]{:S(2)}, u32[]{:S(2)}) collective-permute-start(bf16[14,16,128]{2,1,0:T(8,128)(2,1)S(1)} %get-tuple-element.61), channel_id=1, source_target_pairs={{0,1},{1,0},{2,3},{3,2},{4,5},{5,4},{6,7},{7,6},{8,9},{9,8},{10,11... | collective-permute-start | bytes 172040 | tf_op jit(solution)/shard_map/ppermute | solution.py:758
  49.1 8.2 %collective-permute-start.9 = (bf16[14,16,128]{2,1,0:T(8,128)(2,1)S(1)}, bf16[14,16,128]{2,1,0:T(8,128)(2,1)S(1)}, u32[]{:S(2)}, u32[]{:S(2)}) collective-permute-start(bf16[14,16,128]{2,1,0:T(8,128)(2,1)S(1)} %get-tuple-element.62), channel_id=1, source_target_pairs={{1,2},{3,4},{5,6},{7,8},{9,10},{11,12},{13,14},{2,1},{4,3},{6,5},{... | collective-permute-start | bytes 172040 | tf_op jit(solution)/shard_map/ppermute | solution.py:758
  63.1 2.0 %collective-permute-start.10 = (bf16[17,16,128]{2,1,0:T(8,128)(2,1)S(1)}, bf16[17,16,128]{2,1,0:T(8,128)(2,1)S(1)}, u32[]{:S(2)}, u32[]{:S(2)}) collective-permute-start(bf16[17,16,128]{2,1,0:T(8,128)(2,1)S(1)} %get-tuple-element.69), channel_id=1, source_target_pairs={{0,16},{16,0},{32,48},{48,32},{64,80},{80,64},{96,112},{112,96},{1... | collective-permute-start | bytes 208904 | tf_op jit(solution)/shard_map/ppermute | solution.py:758
  63.2 5.6 %collective-permute-start.11 = (bf16[17,16,128]{2,1,0:T(8,128)(2,1)S(1)}, bf16[17,16,128]{2,1,0:T(8,128)(2,1)S(1)}, u32[]{:S(2)}, u32[]{:S(2)}) collective-permute-start(bf16[17,16,128]{2,1,0:T(8,128)(2,1)S(1)} %get-tuple-element.70), channel_id=1, source_target_pairs={{16,32},{48,64},{80,96},{32,16},{64,48},{96,80},{17,33},{49,65},{8... | collective-permute-start | bytes 208904 | tf_op jit(solution)/shard_map/ppermute | solution.py:758
  68.9 3.9 %collective-permute-start.12 = (bf16[6,16,128]{2,1,0:T(8,128)(2,1)S(1)}, bf16[6,16,128]{2,1,0:T(8,128)(2,1)S(1)}, u32[]{:S(2)}, u32[]{:S(2)}) collective-permute-start(bf16[6,16,128]{2,1,0:T(8,128)(2,1)S(1)} %get-tuple-element.73), channel_id=1, source_target_pairs={{0,1},{1,0},{2,3},{3,2},{4,5},{5,4},{6,7},{7,6},{8,9},{9,8},{10,11... | collective-permute-start | bytes 73736 | tf_op jit(solution)/shard_map/ppermute | solution.py:758
  69.0 7.8 %collective-permute-start.13 = (bf16[6,16,128]{2,1,0:T(8,128)(2,1)S(1)}, bf16[6,16,128]{2,1,0:T(8,128)(2,1)S(1)}, u32[]{:S(2)}, u32[]{:S(2)}) collective-permute-start(bf16[6,16,128]{2,1,0:T(8,128)(2,1)S(1)} %get-tuple-element.74), channel_id=1, source_target_pairs={{1,2},{3,4},{5,6},{7,8},{9,10},{11,12},{13,14},{2,1},{4,3},{6,5},{... | collective-permute-start | bytes 73736 | tf_op jit(solution)/shard_map/ppermute | solution.py:758
  81.0 5.6 %collective-permute-start.15 = (bf16[17,16,128]{2,1,0:T(8,128)(2,1)S(1)}, bf16[17,16,128]{2,1,0:T(8,128)(2,1)S(1)}, u32[]{:S(2)}, u32[]{:S(2)}) collective-permute-start(bf16[17,16,128]{2,1,0:T(8,128)(2,1)S(1)} %get-tuple-element.80), channel_id=1, source_target_pairs={{16,32},{48,64},{80,96},{32,16},{64,48},{96,80},{17,33},{49,65},{8... | collective-permute-start | bytes 208904 | tf_op jit(solution)/shard_map/ppermute | solution.py:758
  82.9 3.7 %collective-permute-start.14 = (bf16[17,16,128]{2,1,0:T(8,128)(2,1)S(1)}, bf16[17,16,128]{2,1,0:T(8,128)(2,1)S(1)}, u32[]{:S(2)}, u32[]{:S(2)}) collective-permute-start(bf16[17,16,128]{2,1,0:T(8,128)(2,1)S(1)} %get-tuple-element.79.refs_0_), channel_id=1, source_target_pairs={{0,16},{16,0},{32,48},{48,32},{64,80},{80,64},{96,112},{112,96},{1... | collective-permute-start | bytes 208904 | tf_op jit(solution)/shard_map/ppermute | solution.py:758
  86.7 4.8 %collective-permute-start.16 = (bf16[6,16,128]{2,1,0:T(8,128)(2,1)S(1)}, bf16[6,16,128]{2,1,0:T(8,128)(2,1)S(1)}, u32[]{:S(2)}, u32[]{:S(2)}) collective-permute-start(bf16[6,16,128]{2,1,0:T(8,128)(2,1)S(1)} %get-tuple-element.83), channel_id=1, source_target_pairs={{0,1},{1,0},{2,3},{3,2},{4,5},{5,4},{6,7},{7,6},{8,9},{9,8},{10,11... | collective-permute-start | bytes 73736 | tf_op jit(solution)/shard_map/ppermute | solution.py:758
  86.8 7.8 %collective-permute-start.17 = (bf16[6,16,128]{2,1,0:T(8,128)(2,1)S(1)}, bf16[6,16,128]{2,1,0:T(8,128)(2,1)S(1)}, u32[]{:S(2)}, u32[]{:S(2)}) collective-permute-start(bf16[6,16,128]{2,1,0:T(8,128)(2,1)S(1)} %get-tuple-element.84), channel_id=1, source_target_pairs={{1,2},{3,4},{5,6},{7,8},{9,10},{11,12},{13,14},{2,1},{4,3},{6,5},{... | collective-permute-start | bytes 73736 | tf_op jit(solution)/shard_map/ppermute | solution.py:758

commit v3 on v2

--- a/solution.py
+++ b/solution.py
@@ -426,6 +426,7 @@
 
 def forward_one(
     flow, lines, own, r_even, r_odd, n_even, n_odd, d_even, d_odd, stored, past, now, m_even, m_odd, p_even, p_odd, table_out,
+    coefs_out, n_odd_out, d_even_out, d_odd_out,
     field, middle, table, known,
 ):
     par = parity()
@@ -459,17 +460,20 @@
     )
     get, add = (lambda at: now[at]), (lambda at: now[OWN + at])
     px_message(par, get, add, (Tiles(m_even), Tiles(m_odd)))
+    coefs_out[...] = known[COEF:KNOWN]
+    n_odd_out[...] = n_odd[...]
+    d_even_out[...] = d_even[...]
+    d_odd_out[...] = d_odd[...]
     py_message(par, get, add, (Tiles(p_even), Tiles(p_odd)))
     for block in range(OWN):
         now[2 * OWN + block] = known[SUM3 + block] + coef(2, block) * past[block] + coef(1, block) * now[block]
 
 
 def turn_kernel(
-    flow, table, own, r_even, r_odd, n_even, n_odd, d_even, d_odd, e_even, e_odd, s_even, s_odd, now, stored, spread, counted,
-    adjoint4, first_out, second_out, m_even, m_odd, field, middle, sums_one, sums_two, field3, field4, coefs,
+    flow, table, own, r_even, r_odd, n_even, n_odd, d_even, d_odd, e_even, e_odd, s_even, s_odd, now, coefs, spread, counted,
+    adjoint4, first_out, second_out, m_even, m_odd, field, middle, sums_one, sums_two, field3, field4,
 ):
     par = parity()
-    flow.fetch(stored.at[pl.ds(COEF, 4 * ROWS)], coefs)
     blocks = (own, r_even, r_odd, n_even, n_odd, d_even, d_odd)
     target = targets_of(table, par)
     coef = Coefs(coefs)
@@ -480,8 +484,6 @@
         return got
 
     def second(block, out):
-        if block == 0:
-            flow.wait(coefs)
         field4[block] = out - coef(0, block) * now[2 * OWN + block]
 
     received = (Tiles(e_even), Tiles(e_odd), Tiles(s_even), Tiles(s_odd))
@@ -615,19 +617,16 @@
 
 
 def adjoint_two(
-    flow, table, own, r_even, r_odd, n_even, n_odd, d_even, d_odd, first_own, second_own, e_even, e_odd, adjoint4, past, stored,
-    spread, counted, later, first_out, second_out, m_even, m_odd, sums_one, sums_two, coefs,
+    flow, table, own, r_even, r_odd, n_even, n_odd, d_even, d_odd, first_own, second_own, e_even, e_odd, adjoint4, past, coefs,
+    spread, counted, later, first_out, second_out, m_even, m_odd, sums_one, sums_two,
 ):
     par = parity()
-    flow.fetch(stored.at[pl.ds(COEF, 4 * ROWS)], coefs)
     clear(sums_one, sums_two)
     adjoint3, adjoint2 = later.at[pl.ds(0, OWN)], later.at[pl.ds(OWN, OWN)]
     settle(par, first_own, second_own, e_even, e_odd, adjoint3, adjoint2)
     coef = Coefs(coefs)
 
     def add_first(block):
-        if block == 0:
-            flow.wait(coefs)
         memory = coef(2, block) * adjoint4[block] + coef(1, block) * adjoint3[block]
         return injected(1, counted, past[block], spread, block) - coef(0, block) * memory
 
@@ -816,15 +815,16 @@
     n_even, n_odd = exchange("py", n_even, n_odd)
     held, n_even = lax.optimization_barrier((held, n_even))
     weights = [(a, "v") for a in (stiffness, r_even, r_odd, n_even, n_odd, d_even, d_odd)]
-    past, now, m_even, m_odd, p_even, p_odd, table = call(
+    past, now, m_even, m_odd, p_even, p_odd, table, coefs, *late = call(
         forward_one,
         [
             ((2 * OWN, 8, 128), F32, "v"), ((3 * OWN, 8, 128), F32, "v"), px_shape, px_shape, py_shape, py_shape,
-            ((16, 128), jnp.int32, "v"),
+            ((16, 128), jnp.int32, "v"), ((4 * ROWS, 8, 128), F32, "v"), py_first, down, down,
         ],
         [(lines, "v")] + weights + [(known, "b")],
         [places, places, lookup, pltpu.VMEM((KNOWN, 8, 128), F32)], copies=3,
     )
+    weights = weights[:4] + [(a, "v") for a in late]
     r_even, r_odd = exchange("px", m_even, m_odd)
     n_even, n_odd = call(
         second_py_kernel, [py_shape, py_shape],
@@ -835,7 +835,6 @@
         holder_kernel, [((4, OWN, 8, 128), F32, "v"), ((4, OWN, 8, 128), F32, "v")],
         [(gate_step, "s"), (held, "h"), (m_even, "v")],
     )
-    coefs = pltpu.VMEM((4 * ROWS, 8, 128), F32)
     rim = ((COLS // 2 + 1 + WIDE, 16, 128), BF16, "v")
     rim_py = ((6, 16, 128), BF16, "v")
     pair_out = [
@@ -845,8 +844,8 @@
     adjoint4, *rest = call(
         turn_kernel, [PLAIN] + pair_out,
         [(table, "s")] + weights
-        + [(r_even, "v"), (r_odd, "v"), (n_even, "v"), (n_odd, "v"), (now, "v"), (known, "b"), (spread, "v"), (counted, "v")],
-        [places, places, sums, sums, blocks, blocks, coefs], copies=1,
+        + [(r_even, "v"), (r_odd, "v"), (n_even, "v"), (n_odd, "v"), (now, "v"), (coefs, "v"), (spread, "v"), (counted, "v")],
+        [places, places, sums, sums, blocks, blocks],
     )
 
     def gathered(first, second, m_even, m_odd):
@@ -862,8 +861,8 @@
     later, *rest = call(
         adjoint_two, [((2 * OWN, 8, 128), F32, "v")] + pair_out,
         [(table, "s")] + weights + gathered(*rest)
-        + [(adjoint4, "v"), (past, "v"), (known, "b"), (spread, "v"), (counted, "v")],
-        [sums, sums, coefs], copies=1,
+        + [(adjoint4, "v"), (past, "v"), (coefs, "v"), (spread, "v"), (counted, "v")],
+        [sums, sums],
     )
     (before,) = call(
         gradient_kernel, [((2 * OWN, 8, 128), F32, "v")],

time: 96.3 us -> 93.4 us (0.970)
  Pallas kernels: 28.3 us -> 25.5 us
    pallas_call x12, Pallas kernels: 28.3 us -> 25.5 us  [call(): pl.pallas_call(wrapped, out_shape=[jax.ShapeDtypeStruct(shape, dtype) for...]
where the time goes in v3:
time: 93.4 us; the launch traced here: 92.8 us
  starting transfers between devices  43.2 us (46%)
  Pallas kernels  25.5 us (27%)
  waiting for transfers between devices  22 us (24%)
  between operations  1.08 us (1%)
  local copies, waits for them, and re-layouts  1.01 us (1%)
    ppermute x9, starting transfers between devices, exchange(): lax.ppermute(for_odd, axis, swap_odd(axis))  26 us
    pallas_call x12, Pallas kernels, call(): pl.pallas_call(wrapped, out_shape=[jax.ShapeDtypeStruct(shape, dtype) for...  25.5 us
    ppermute x9, waiting for transfers between devices, exchange(): lax.ppermute(for_odd, axis, swap_odd(axis))  19.1 us
    all_to_all x1, starting transfers between devices, body(): lax.all_to_all(sent.reshape(devices, CAP, 128), ('px', 'py'), split_axis=...  11.5 us
    ppermute x9, starting transfers between devices, exchange(): lax.ppermute(for_even, axis, swap_even(axis))  5.65 us
    ppermute x9, waiting for transfers between devices, exchange(): lax.ppermute(for_even, axis, swap_even(axis))  2.93 us
  transfers between devices with their start and end apart: 19, of which 9 were waited for; matrix products, arithmetic and copies ran while one was open for 0% of the time, Pallas kernels for 9%

profile of v3, /device:TPU:10, one launch (start us, length us, event | category | flops | bytes accessed | tf_op | source)
XLA Modules:
  0.0 92.8 jit_solution(16460751852319885108)
XLA Ops:
  0.6 4.2 %shard_map.113 = (bf16[592,512]{1,0:T(8,128)(2,1)}, bf16[592,512]{1,0:T(8,128)(2,1)}, bf16[2,192,512]{2,1,0:T(8,128)(2,1)}, bf16[4,64,512]{2,1,0:T(8,128)(2,1)},...) custom-call(s32[1,8]{1,0:T(1,128)} %bitcast.5, f32[256,128]{1,0:T(8,128)} %refs_1_.5, ...), custom_call_target="tpu_custom_call" | custom-call | tf_op jit(solution)/shard_map/pallas_call | solution.py:108
  4.9 2.4 %collective-permute-start.1 = (bf16[592,512]{1,0:T(8,128)(2,1)}, bf16[592,512]{1,0:T(8,128)(2,1)S(1)}, u32[]{:S(2)}, u32[]{:S(2)}) collective-permute-start(bf16[592,512]{1,0:T(8,128)(2,1)} %get-tuple-element.52), channel_id=1, source_target_pairs={{16,32},{48,64},{80,96},{32,16},{64,48},{96,80},{17,33},{49,65},{8... | collective-permute-start | bytes 1818632 | tf_op jit(solution)/shard_map/ppermute | solution.py:757
  7.4 11.5 %all-to-all-start = ((f32[128,8,128]{2,1,0:T(8,128)}), f32[128,8,128]{2,1,0:T(8,128)}, u32[]{:S(2)}, u32[]{:S(2)}) async-start(f32[128,8,128]{2,1,0:T(8,128)} %bitcast.6), calls=%async_computation | async-start | bytes 1048576 | tf_op jit(solution)/shard_map/all_to_all | solution.py:803
  18.9 1.7 %collective-permute-start.4 = (bf16[4,64,512]{2,1,0:T(8,128)(2,1)}, bf16[4,64,512]{2,1,0:T(8,128)(2,1)}, u32[]{:S(2)}, u32[]{:S(2)}) collective-permute-start(bf16[4,64,512]{2,1,0:T(8,128)(2,1)} %get-tuple-element.58), channel_id=1, source_target_pairs={{0,1},{1,0},{2,3},{3,2},{4,5},{5,4},{6,7},{7,6},{8,9},{9,8},{10,11... | collective-permute-start | bytes 786440 | tf_op jit(solution)/shard_map/ppermute | solution.py:757
  20.6 4.2 %collective-permute-start.5 = (bf16[4,64,512]{2,1,0:T(8,128)(2,1)}, bf16[4,64,512]{2,1,0:T(8,128)(2,1)}, u32[]{:S(2)}, u32[]{:S(2)}) collective-permute-start(bf16[4,64,512]{2,1,0:T(8,128)(2,1)} %get-tuple-element.59), channel_id=1, source_target_pairs={{1,2},{3,4},{5,6},{7,8},{9,10},{11,12},{13,14},{2,1},{4,3},{6,5},{... | collective-permute-start | bytes 786440 | tf_op jit(solution)/shard_map/ppermute | solution.py:757
  27.5 2.9 %collective-permute-start.3 = (bf16[192,512]{1,0:T(8,128)(2,1)}, bf16[192,512]{1,0:T(8,128)(2,1)}, u32[]{:S(2)}, u32[]{:S(2)}) collective-permute-start(bf16[192,512]{1,0:T(8,128)(2,1)} %get-tuple-element.57), channel_id=1, source_target_pairs={{1,2},{3,4},{5,6},{7,8},{9,10},{11,12},{13,14},{2,1},{4,3},{6,5},{... | collective-permute-start | bytes 589832 | tf_op jit(solution)/shard_map/ppermute | solution.py:757
  30.4 3.3 %shard_map.115.refs_8_.refs_3_ = f32[12288,8,128]{2,1,0:T(8,128)} custom-call(bf16[192,512]{1,0:T(8,128)(2,1)} %copy-done.2, f32[4,8,1024]{2,1,0:T(8,128)} %refs_1_.6, f32[4,4,8,1024]{3,2,1,0:T(8,128)} %refs_2_.1, f32[4,8,64]{2,1,0:T(8,128)} %refs_3_.1, f32[4,4,8,64]{3,2,1,0:T(8,128)} %refs_4_.3), custom_call_target="tpu_custom_call" | custom-call | tf_op jit(solution)/shard_map/pallas_call | solution.py:108
  33.7 2.7 %collective-permute-done.2.refs_4_ = bf16[192,512]{1,0:T(8,128)(2,1)S(1)} collective-permute-done((bf16[192,512]{1,0:T(8,128)(2,1)S(1)}, bf16[192,512]{1,0:T(8,128)(2,1)S(1)}, u32[]{:S(2)}, u32[]{:S(2)}) %collective-permute-start.2) | collective-permute-done | bytes 196640 | tf_op jit(solution)/shard_map/ppermute | solution.py:757
  36.5 2.2 %collective-permute-done.3.refs_5_ = bf16[192,512]{1,0:T(8,128)(2,1)} collective-permute-done((bf16[192,512]{1,0:T(8,128)(2,1)}, bf16[192,512]{1,0:T(8,128)(2,1)}, u32[]{:S(2)}, u32[]{:S(2)}) %collective-permute-start.3) | collective-permute-done | bytes 196640 | tf_op jit(solution)/shard_map/ppermute | solution.py:757
  38.7 4.6 %shard_map.116 = (f32[64,8,128]{2,1,0:T(8,128)S(1)}, f32[96,8,128]{2,1,0:T(8,128)S(1)}, bf16[16,16,128]{2,1,0:T(8,128)(2,1)S(1)}, bf16[16,16,128]{2,1,0:T(8,128)...) custom-call(f32[8,128]{1,0:T(8,128)S(1)} %copy-done.3, ...), custom_call_target="tpu_custom_call" | custom-call | tf_op jit(solution)/shard_map/pallas_call | solution.py:108
  43.2 2.1 %collective-permute-start.7 = (bf16[16,16,128]{2,1,0:T(8,128)(2,1)S(1)}, bf16[16,16,128]{2,1,0:T(8,128)(2,1)S(1)}, u32[]{:S(2)}, u32[]{:S(2)}) collective-permute-start(bf16[16,16,128]{2,1,0:T(8,128)(2,1)S(1)} %get-tuple-element.65), channel_id=1, source_target_pairs={{16,32},{48,64},{80,96},{32,16},{64,48},{96,80},{17,33},{49,65},{8... | collective-permute-start | bytes 196616 | tf_op jit(solution)/shard_map/ppermute | solution.py:757
  46.4 2.5 %collective-permute-done.7.refs_1_.refs_9_ = bf16[16,16,128]{2,1,0:T(8,128)(2,1)S(1)} collective-permute-done((bf16[16,16,128]{2,1,0:T(8,128)(2,1)S(1)}, bf16[16,16,128]{2,1,0:T(8,128)(2,1)S(1)}, u32[]{:S(2)}, u32[]{:S(2)}) %collective-permute-start.7) | collective-permute-done | bytes 65568 | tf_op jit(solution)/shard_map/ppermute | solution.py:757
  49.1 3.5 %collective-permute-start.9 = (bf16[14,16,128]{2,1,0:T(8,128)(2,1)S(1)}, bf16[14,16,128]{2,1,0:T(8,128)(2,1)S(1)}, u32[]{:S(2)}, u32[]{:S(2)}) collective-permute-start(bf16[14,16,128]{2,1,0:T(8,128)(2,1)S(1)} %get-tuple-element.69), channel_id=1, source_target_pairs={{1,2},{3,4},{5,6},{7,8},{9,10},{11,12},{13,14},{2,1},{4,3},{6,5},{... | collective-permute-start | bytes 172040 | tf_op jit(solution)/shard_map/ppermute | solution.py:757
  52.6 3.4 %shard_map.118 = (f32[4,32,8,128]{3,2,1,0:T(8,128)S(1)}, f32[4,32,8,128]{3,2,1,0:T(8,128)S(1)}) custom-call(s32[8]{0:T(128)S(1)} %copy-done.4, f32[1024,128]{1,0:T(8,128)} %bitcast.4.refs_1_, bf16[16,16,128]{2,1,0:T(8,128)(2,1)S(1)} %get-tuple-element.64.refs_2_), custom_call_target="tpu_custom_call" | custom-call | tf_op jit(solution)/shard_map/pallas_call | solution.py:108
  57.3 4.5 %shard_map.119 = (f32[32,8,128]{2,1,0:T(8,128)S(1)}, f32[40,8,128]{2,1,0:T(8,128)S(1)}, f32[48,8,128]{2,1,0:T(8,128)S(1)}, bf16[17,16,128]{2,1,0:T(8,128)(2,1)S(1)}, bf16[17,16,128]{2,1,0:T(8,128)(2,1)S(1)}) custom-call(s32[16,128]{1,0:T(8,128)S(1)} %get-tuple-element.60.refs_0_, bf16[4,8,64,512]{3,2,1,0:T(8,128)(2,1)S(1)} %copy-done, ...), custom_call_target="tpu_custom_call" | custom-call | tf_op jit(solution)/shard_map/pallas_call | solution.py:108
  61.9 1.9 %collective-permute-start.11 = (bf16[17,16,128]{2,1,0:T(8,128)(2,1)S(1)}, bf16[17,16,128]{2,1,0:T(8,128)(2,1)S(1)}, u32[]{:S(2)}, u32[]{:S(2)}) collective-permute-start(bf16[17,16,128]{2,1,0:T(8,128)(2,1)S(1)} %get-tuple-element.78), channel_id=1, source_target_pairs={{16,32},{48,64},{80,96},{32,16},{64,48},{96,80},{17,33},{49,65},{8... | collective-permute-start | bytes 208904 | tf_op jit(solution)/shard_map/ppermute | solution.py:757
  63.8 3.7 %collective-permute-done.11.refs_3_ = bf16[17,16,128]{2,1,0:T(8,128)(2,1)S(1)} collective-permute-done((bf16[17,16,128]{2,1,0:T(8,128)(2,1)S(1)}, bf16[17,16,128]{2,1,0:T(8,128)(2,1)S(1)}, u32[]{:S(2)}, u32[]{:S(2)}) %collective-permute-start.11) | collective-permute-done | bytes 69664 | tf_op jit(solution)/shard_map/ppermute | solution.py:757
  67.7 3.6 %collective-permute-start.13 = (bf16[6,16,128]{2,1,0:T(8,128)(2,1)S(1)}, bf16[6,16,128]{2,1,0:T(8,128)(2,1)S(1)}, u32[]{:S(2)}, u32[]{:S(2)}) collective-permute-start(bf16[6,16,128]{2,1,0:T(8,128)(2,1)S(1)} %get-tuple-element.82), channel_id=1, source_target_pairs={{1,2},{3,4},{5,6},{7,8},{9,10},{11,12},{13,14},{2,1},{4,3},{6,5},{... | collective-permute-start | bytes 73736 | tf_op jit(solution)/shard_map/ppermute | solution.py:757
  71.5 4.0 %collective-permute-done.13.refs_11_ = bf16[6,16,128]{2,1,0:T(8,128)(2,1)S(1)} collective-permute-done((bf16[6,16,128]{2,1,0:T(8,128)(2,1)S(1)}, bf16[6,16,128]{2,1,0:T(8,128)(2,1)S(1)}, u32[]{:S(2)}, u32[]{:S(2)}) %collective-permute-start.13) | collective-permute-done | bytes 24608 | tf_op jit(solution)/shard_map/ppermute | solution.py:757
  75.6 2.7 %shard_map.121 = (f32[64,8,128]{2,1,0:T(8,128)S(1)}, f32[40,8,128]{2,1,0:T(8,128)S(1)}, f32[48,8,128]{2,1,0:T(8,128)S(1)}, bf16[17,16,128]{2,1,0:T(8,128)(2,1)S(1)}, bf16[17,16,128]{2,1,0:T(8,128)(2,1)S(1)}) custom-call(s32[16,128]{1,0:T(8,128)S(1)} %get-tuple-element.60.refs_0_, bf16[4,8,64,512]{3,2,1,0:T(8,128)(2,1)S(1)} %copy-done, ...), custom_call_target="tpu_custom_call" | custom-call | tf_op jit(solution)/shard_map/pallas_call | solution.py:108
  78.3 1.9 %collective-permute-start.15 = (bf16[17,16,128]{2,1,0:T(8,128)(2,1)S(1)}, bf16[17,16,128]{2,1,0:T(8,128)(2,1)S(1)}, u32[]{:S(2)}, u32[]{:S(2)}) collective-permute-start(bf16[17,16,128]{2,1,0:T(8,128)(2,1)S(1)} %get-tuple-element.88), channel_id=1, source_target_pairs={{16,32},{48,64},{80,96},{32,16},{64,48},{96,80},{17,33},{49,65},{8... | collective-permute-start | bytes 208904 | tf_op jit(solution)/shard_map/ppermute | solution.py:757
  81.5 2.3 %collective-permute-done.15.refs_3_ = bf16[17,16,128]{2,1,0:T(8,128)(2,1)S(1)} collective-permute-done((bf16[17,16,128]{2,1,0:T(8,128)(2,1)S(1)}, bf16[17,16,128]{2,1,0:T(8,128)(2,1)S(1)}, u32[]{:S(2)}, u32[]{:S(2)}) %collective-permute-start.15) | collective-permute-done | bytes 69664 | tf_op jit(solution)/shard_map/ppermute | solution.py:757
  84.1 3.4 %collective-permute-start.17 = (bf16[6,16,128]{2,1,0:T(8,128)(2,1)S(1)}, bf16[6,16,128]{2,1,0:T(8,128)(2,1)S(1)}, u32[]{:S(2)}, u32[]{:S(2)}) collective-permute-start(bf16[6,16,128]{2,1,0:T(8,128)(2,1)S(1)} %get-tuple-element.92), channel_id=1, source_target_pairs={{1,2},{3,4},{5,6},{7,8},{9,10},{11,12},{13,14},{2,1},{4,3},{6,5},{... | collective-permute-start | bytes 73736 | tf_op jit(solution)/shard_map/ppermute | solution.py:757
  88.8 3.1 %collective-permute-done.17.refs_3_ = bf16[6,16,128]{2,1,0:T(8,128)(2,1)S(1)} collective-permute-done((bf16[6,16,128]{2,1,0:T(8,128)(2,1)S(1)}, bf16[6,16,128]{2,1,0:T(8,128)(2,1)S(1)}, u32[]{:S(2)}, u32[]{:S(2)}) %collective-permute-start.17) | collective-permute-done | bytes 24608 | tf_op jit(solution)/shard_map/ppermute | solution.py:757
  (36 shorter events, 9.3 us)
Async XLA Ops:
  4.8 33.9 %copy-start = (bf16[4,8,64,512]{3,2,1,0:T(8,128)(2,1)S(1)}, bf16[4,8,64,512]{3,2,1,0:T(8,128)(2,1)}, u32[]{:S(2)}) copy-start(bf16[4,8,64,512]{3,2,1,0:T(8,128)(2,1)} %refs_1_.9) | copy-start | bytes 6291460
  4.8 2.6 %collective-permute-start = (bf16[592,512]{1,0:T(8,128)(2,1)}, bf16[592,512]{1,0:T(8,128)(2,1)S(1)}, u32[]{:S(2)}, u32[]{:S(2)}) collective-permute-start(bf16[592,512]{1,0:T(8,128)(2,1)} %get-tuple-element.50), channel_id=1, source_target_pairs={{0,16},{16,0},{32,48},{48,32},{64,80},{80,64},{96,112},{112,96},{1... | collective-permute-start | bytes 1818632 | tf_op jit(solution)/shard_map/ppermute | solution.py:757
  4.9 19.9 %collective-permute-start.1 = (bf16[592,512]{1,0:T(8,128)(2,1)}, bf16[592,512]{1,0:T(8,128)(2,1)S(1)}, u32[]{:S(2)}, u32[]{:S(2)}) collective-permute-start(bf16[592,512]{1,0:T(8,128)(2,1)} %get-tuple-element.52), channel_id=1, source_target_pairs={{16,32},{48,64},{80,96},{32,16},{64,48},{96,80},{17,33},{49,65},{8... | collective-permute-start | bytes 1818632 | tf_op jit(solution)/shard_map/ppermute | solution.py:757
  7.4 29.1 %all-to-all-start = ((f32[128,8,128]{2,1,0:T(8,128)}), f32[128,8,128]{2,1,0:T(8,128)}, u32[]{:S(2)}, u32[]{:S(2)}) async-start(f32[128,8,128]{2,1,0:T(8,128)} %bitcast.6), calls=%async_computation | async-start | bytes 1048576 | tf_op jit(solution)/shard_map/all_to_all | solution.py:803
  18.9 17.6 %collective-permute-start.4 = (bf16[4,64,512]{2,1,0:T(8,128)(2,1)}, bf16[4,64,512]{2,1,0:T(8,128)(2,1)}, u32[]{:S(2)}, u32[]{:S(2)}) collective-permute-start(bf16[4,64,512]{2,1,0:T(8,128)(2,1)} %get-tuple-element.58), channel_id=1, source_target_pairs={{0,1},{1,0},{2,3},{3,2},{4,5},{5,4},{6,7},{7,6},{8,9},{9,8},{10,11... | collective-permute-start | bytes 786440 | tf_op jit(solution)/shard_map/ppermute | solution.py:757
  20.6 15.9 %collective-permute-start.5 = (bf16[4,64,512]{2,1,0:T(8,128)(2,1)}, bf16[4,64,512]{2,1,0:T(8,128)(2,1)}, u32[]{:S(2)}, u32[]{:S(2)}) collective-permute-start(bf16[4,64,512]{2,1,0:T(8,128)(2,1)} %get-tuple-element.59), channel_id=1, source_target_pairs={{1,2},{3,4},{5,6},{7,8},{9,10},{11,12},{13,14},{2,1},{4,3},{6,5},{... | collective-permute-start | bytes 786440 | tf_op jit(solution)/shard_map/ppermute | solution.py:757
  24.9 1.0 %copy-start.1 = (bf16[2,192,512]{2,1,0:T(8,128)(2,1)S(1)}, bf16[2,192,512]{2,1,0:T(8,128)(2,1)}, u32[]{:S(2)}) copy-start(bf16[2,192,512]{2,1,0:T(8,128)(2,1)} %get-tuple-element.54.refs_2_) | copy-start | bytes 1179652
  25.8 12.8 %copy-start.3 = (f32[8,128]{1,0:T(8,128)S(1)}, f32[8,128]{1,0:T(8,128)}, u32[]{:S(2)}) copy-start(f32[8,128]{1,0:T(8,128)} %get-tuple-element.48.refs_0_) | copy-start | bytes 12292
  26.6 3.8 %copy-start.2 = (bf16[192,512]{1,0:T(8,128)(2,1)}, bf16[192,512]{1,0:T(8,128)(2,1)S(1)}, u32[]{:S(2)}) copy-start(bf16[192,512]{1,0:T(8,128)(2,1)S(1)} %get-tuple-element.55.refs_0_) | copy-start | bytes 589828
  26.6 9.9 %collective-permute-start.2 = (bf16[192,512]{1,0:T(8,128)(2,1)S(1)}, bf16[192,512]{1,0:T(8,128)(2,1)S(1)}, u32[]{:S(2)}, u32[]{:S(2)}) collective-permute-start(bf16[192,512]{1,0:T(8,128)(2,1)S(1)} %get-tuple-element.55.refs_0_), channel_id=1, source_target_pairs={{0,1},{1,0},{2,3},{3,2},{4,5},{5,4},{6,7},{7,6},{8,9},{9,8},{10,11... | collective-permute-start | bytes 589832 | tf_op jit(solution)/shard_map/ppermute | solution.py:757
  27.5 25.1 %copy-start.4 = (s32[8]{0:T(128)S(1)}, s32[8]{0:T(128)}, u32[]{:S(2)}) copy-start(s32[8]{0:T(128)} %refs_0_.1) | copy-start | bytes 100
  27.5 11.2 %collective-permute-start.3 = (bf16[192,512]{1,0:T(8,128)(2,1)}, bf16[192,512]{1,0:T(8,128)(2,1)}, u32[]{:S(2)}, u32[]{:S(2)}) collective-permute-start(bf16[192,512]{1,0:T(8,128)(2,1)} %get-tuple-element.57), channel_id=1, source_target_pairs={{1,2},{3,4},{5,6},{7,8},{9,10},{11,12},{13,14},{2,1},{4,3},{6,5},{... | collective-permute-start | bytes 589832 | tf_op jit(solution)/shard_map/ppermute | solution.py:757
  43.2 5.6 %collective-permute-start.7 = (bf16[16,16,128]{2,1,0:T(8,128)(2,1)S(1)}, bf16[16,16,128]{2,1,0:T(8,128)(2,1)S(1)}, u32[]{:S(2)}, u32[]{:S(2)}) collective-permute-start(bf16[16,16,128]{2,1,0:T(8,128)(2,1)S(1)} %get-tuple-element.65), channel_id=1, source_target_pairs={{16,32},{48,64},{80,96},{32,16},{64,48},{96,80},{17,33},{49,65},{8... | collective-permute-start | bytes 196616 | tf_op jit(solution)/shard_map/ppermute | solution.py:757
  45.4 3.5 %collective-permute-start.6 = (bf16[16,16,128]{2,1,0:T(8,128)(2,1)S(1)}, bf16[16,16,128]{2,1,0:T(8,128)(2,1)S(1)}, u32[]{:S(2)}, u32[]{:S(2)}) collective-permute-start(bf16[16,16,128]{2,1,0:T(8,128)(2,1)S(1)} %get-tuple-element.64.refs_2_), channel_id=1, source_target_pairs={{0,16},{16,0},{32,48},{48,32},{64,80},{80,64},{96,112},{112,96},{1... | collective-permute-start | bytes 196616 | tf_op jit(solution)/shard_map/ppermute | solution.py:757
  48.9 7.1 %collective-permute-start.8 = (bf16[14,16,128]{2,1,0:T(8,128)(2,1)S(1)}, bf16[14,16,128]{2,1,0:T(8,128)(2,1)S(1)}, u32[]{:S(2)}, u32[]{:S(2)}) collective-permute-start(bf16[14,16,128]{2,1,0:T(8,128)(2,1)S(1)} %get-tuple-element.68), channel_id=1, source_target_pairs={{0,1},{1,0},{2,3},{3,2},{4,5},{5,4},{6,7},{7,6},{8,9},{9,8},{10,11... | collective-permute-start | bytes 172040 | tf_op jit(solution)/shard_map/ppermute | solution.py:757
  49.1 8.2 %collective-permute-start.9 = (bf16[14,16,128]{2,1,0:T(8,128)(2,1)S(1)}, bf16[14,16,128]{2,1,0:T(8,128)(2,1)S(1)}, u32[]{:S(2)}, u32[]{:S(2)}) collective-permute-start(bf16[14,16,128]{2,1,0:T(8,128)(2,1)S(1)} %get-tuple-element.69), channel_id=1, source_target_pairs={{1,2},{3,4},{5,6},{7,8},{9,10},{11,12},{13,14},{2,1},{4,3},{6,5},{... | collective-permute-start | bytes 172040 | tf_op jit(solution)/shard_map/ppermute | solution.py:757
  61.8 2.0 %collective-permute-start.10 = (bf16[17,16,128]{2,1,0:T(8,128)(2,1)S(1)}, bf16[17,16,128]{2,1,0:T(8,128)(2,1)S(1)}, u32[]{:S(2)}, u32[]{:S(2)}) collective-permute-start(bf16[17,16,128]{2,1,0:T(8,128)(2,1)S(1)} %get-tuple-element.77), channel_id=1, source_target_pairs={{0,16},{16,0},{32,48},{48,32},{64,80},{80,64},{96,112},{112,96},{1... | collective-permute-start | bytes 208904 | tf_op jit(solution)/shard_map/ppermute | solution.py:757
  61.9 5.6 %collective-permute-start.11 = (bf16[17,16,128]{2,1,0:T(8,128)(2,1)S(1)}, bf16[17,16,128]{2,1,0:T(8,128)(2,1)S(1)}, u32[]{:S(2)}, u32[]{:S(2)}) collective-permute-start(bf16[17,16,128]{2,1,0:T(8,128)(2,1)S(1)} %get-tuple-element.78), channel_id=1, source_target_pairs={{16,32},{48,64},{80,96},{32,16},{64,48},{96,80},{17,33},{49,65},{8... | collective-permute-start | bytes 208904 | tf_op jit(solution)/shard_map/ppermute | solution.py:757
  67.6 3.9 %collective-permute-start.12 = (bf16[6,16,128]{2,1,0:T(8,128)(2,1)S(1)}, bf16[6,16,128]{2,1,0:T(8,128)(2,1)S(1)}, u32[]{:S(2)}, u32[]{:S(2)}) collective-permute-start(bf16[6,16,128]{2,1,0:T(8,128)(2,1)S(1)} %get-tuple-element.81), channel_id=1, source_target_pairs={{0,1},{1,0},{2,3},{3,2},{4,5},{5,4},{6,7},{7,6},{8,9},{9,8},{10,11... | collective-permute-start | bytes 73736 | tf_op jit(solution)/shard_map/ppermute | solution.py:757
  67.7 7.8 %collective-permute-start.13 = (bf16[6,16,128]{2,1,0:T(8,128)(2,1)S(1)}, bf16[6,16,128]{2,1,0:T(8,128)(2,1)S(1)}, u32[]{:S(2)}, u32[]{:S(2)}) collective-permute-start(bf16[6,16,128]{2,1,0:T(8,128)(2,1)S(1)} %get-tuple-element.82), channel_id=1, source_target_pairs={{1,2},{3,4},{5,6},{7,8},{9,10},{11,12},{13,14},{2,1},{4,3},{6,5},{... | collective-permute-start | bytes 73736 | tf_op jit(solution)/shard_map/ppermute | solution.py:757
  78.3 5.6 %collective-permute-start.15 = (bf16[17,16,128]{2,1,0:T(8,128)(2,1)S(1)}, bf16[17,16,128]{2,1,0:T(8,128)(2,1)S(1)}, u32[]{:S(2)}, u32[]{:S(2)}) collective-permute-start(bf16[17,16,128]{2,1,0:T(8,128)(2,1)S(1)} %get-tuple-element.88), channel_id=1, source_target_pairs={{16,32},{48,64},{80,96},{32,16},{64,48},{96,80},{17,33},{49,65},{8... | collective-permute-start | bytes 208904 | tf_op jit(solution)/shard_map/ppermute | solution.py:757
  80.2 3.7 %collective-permute-start.14 = (bf16[17,16,128]{2,1,0:T(8,128)(2,1)S(1)}, bf16[17,16,128]{2,1,0:T(8,128)(2,1)S(1)}, u32[]{:S(2)}, u32[]{:S(2)}) collective-permute-start(bf16[17,16,128]{2,1,0:T(8,128)(2,1)S(1)} %get-tuple-element.87.refs_0_), channel_id=1, source_target_pairs={{0,16},{16,0},{32,48},{48,32},{64,80},{80,64},{96,112},{112,96},{1... | collective-permute-start | bytes 208904 | tf_op jit(solution)/shard_map/ppermute | solution.py:757
  84.0 4.8 %collective-permute-start.16 = (bf16[6,16,128]{2,1,0:T(8,128)(2,1)S(1)}, bf16[6,16,128]{2,1,0:T(8,128)(2,1)S(1)}, u32[]{:S(2)}, u32[]{:S(2)}) collective-permute-start(bf16[6,16,128]{2,1,0:T(8,128)(2,1)S(1)} %get-tuple-element.91), channel_id=1, source_target_pairs={{0,1},{1,0},{2,3},{3,2},{4,5},{5,4},{6,7},{7,6},{8,9},{9,8},{10,11... | collective-permute-start | bytes 73736 | tf_op jit(solution)/shard_map/ppermute | solution.py:757
  84.1 7.8 %collective-permute-start.17 = (bf16[6,16,128]{2,1,0:T(8,128)(2,1)S(1)}, bf16[6,16,128]{2,1,0:T(8,128)(2,1)S(1)}, u32[]{:S(2)}, u32[]{:S(2)}) collective-permute-start(bf16[6,16,128]{2,1,0:T(8,128)(2,1)S(1)} %get-tuple-element.92), channel_id=1, source_target_pairs={{1,2},{3,4},{5,6},{7,8},{9,10},{11,12},{13,14},{2,1},{4,3},{6,5},{... | collective-permute-start | bytes 73736 | tf_op jit(solution)/shard_map/ppermute | solution.py:757

commit v4 on v3

--- a/solution.py
+++ b/solution.py
@@ -15,7 +15,7 @@
 NODE, WIDTH = 64, 512
 FIELD, ADDEND, SUM0, SUM1, SUM2, SUM3, COEF = (i * OWN for i in range(7))
 PX_BASE, PY_BASE = COLS * NODE, 2 * NODE
-KNOWN, ROOM = COEF + 4 * ROWS, 12288
+KNOWN, ROOM, PAGES = COEF + 4 * ROWS, 12288, 96
 
 
 def place(row, col):
@@ -247,20 +247,22 @@
     for source, out in ((m_even, m_even_out), (m_odd, m_odd_out)):
         flow.send(source.at[pl.ds(PX_BASE, 80), :], out.at[pl.ds(PX_BASE, 80), :])
     py_message(par, get, add, py_tiles)
-    flow.send(both.at[:, pl.ds(PY_BASE, 64), :], both_out.at[:, pl.ds(PY_BASE, 64), :])
+    flow.send(both.at[:, pl.ds(PY_BASE, 64), :], both_out.at[pl.ds(0, 2), pl.ds(PY_BASE, 64), :])
 
 
 def first_py_kernel(flow, r_even, r_odd, given, n_even, n_odd):
     par = parity()
-    n_even[...] = given[0]
-    n_odd[...] = given[1]
+    part = pl.ds(PY_BASE, 64)
+    own = [flow.copy(given.at[i, part, :], out.at[part, :]) for i, out in enumerate((n_even, n_odd))]
     tiles = [Tiles(r_even, PX_BASE), Tiles(r_odd, PX_BASE)]
     outs = [Tiles(n_even, PY_BASE), Tiles(n_odd, PY_BASE)]
-    py_fill(par, tiles[0], tiles[1], outs)
     row = lax.broadcasted_iota(jnp.int32, (16, 128), 0)
     for out, edge in zip((n_even, n_odd), sides(par, 1, COLS - 1, 0)):
         for k, got in enumerate((r_even, r_odd)):
             out[pl.ds(k * NODE, NODE), :] = got[pl.ds(edge * NODE, NODE), :]
+    for copied in own:
+        copied.wait()
+    py_fill(par, tiles[0], tiles[1], outs)
     for out in outs:
         even, odd = tiles[0][16].astype(F32), tiles[1][16].astype(F32)
         own = out[14].astype(F32)
@@ -377,7 +379,7 @@
     return jnp.concatenate(parts, 0)
 
 
-def forward_pair(par, target, ready, blocks, plain, received, field, middle, store_first, store_second):
+def forward_pair(par, target, arrive, ready, arrived, blocks, plain, received, field, middle, store_first, store_second):
     low = low_lanes(16)
     r_even, r_odd, n_even, n_odd = received
 
@@ -393,6 +395,7 @@
             for p in range(4):
                 at = place(base + k, 2 * p)
                 spread(msg[k * 4 + p], at, at + 1)
+    arrive()
     rows = [0, 1, 2, 3, row_bases[0], row_bases[0] + 1, row_bases[1], row_bases[1] + 1]
     for msg, base in zip((n_even, n_odd), col_bases):
         for j, row in enumerate(rows):
@@ -414,6 +417,7 @@
         )
         return unpacked(out)
 
+    arrived()
     for number, (array, index, at) in enumerate(outer_places(par)):
         got = product(field, OWN + number) + joined(received[array][8 + index])
         middle[at] = doubled(got).astype(BF16)
@@ -432,13 +436,18 @@
     par = parity()
     begun = flow.copy(stored.at[pl.ds(0, 2 * OWN)], known.at[pl.ds(0, 2 * OWN)])
     rest = flow.copy(stored.at[pl.ds(2 * OWN, KNOWN - 2 * OWN)], known.at[pl.ds(2 * OWN, KNOWN - 2 * OWN)])
-    table_out[...] = table_lines(par, lines[...], r_even, r_odd, n_even, n_odd)
-    looked = flow.copy(table_out, table)
+    looked = []
+
+    def arrive():
+        flow.wait(n_odd)
+        table_out[...] = table_lines(par, lines[...], r_even, r_odd, n_even, n_odd)
+        looked.append(flow.copy(table_out, table))
+
     coef = Coefs(known.at[pl.ds(COEF, 4 * ROWS)])
 
     def ready():
-        looked.wait()
         begun.wait()
+        looked[0].wait()
 
     def first(block, out):
         if block == 0:
@@ -455,7 +464,7 @@
 
     received = (Tiles(r_even, PX_BASE), Tiles(r_odd, PX_BASE), Tiles(n_even, PY_BASE), Tiles(n_odd, PY_BASE))
     forward_pair(
-        par, targets_of(table, par), ready, (own, r_even, r_odd, n_even, n_odd, d_even, d_odd), lambda block: known[FIELD + block],
+        par, targets_of(table, par), arrive, ready, lambda: flow.wait(d_even, d_odd), (own, r_even, r_odd, n_even, n_odd, d_even, d_odd), lambda block: known[FIELD + block],
         received, field, middle, first, second,
     )
     get, add = (lambda at: now[at]), (lambda at: now[OWN + at])
@@ -489,7 +498,7 @@
     received = (Tiles(e_even), Tiles(e_odd), Tiles(s_even), Tiles(s_odd))
     clear(sums_one, sums_two)
     forward_pair(
-        par, target, lambda: None, blocks, lambda block: now[block], received, field, middle, first, second
+        par, target, lambda: None, lambda: None, lambda: None, blocks, lambda block: now[block], received, field, middle, first, second
     )
     def start(block):
         value = injected(4, counted, field4[block], spread, block)
@@ -785,7 +794,7 @@
     m_even, m_odd, both, d_even, d_odd, lines, sent = call(
         start_kernel,
         [
-            px_first[:2] + ("h",), px_first[:2] + ("h",), (two, BF16, "h"), down[:2] + ("h",), down[:2] + ("h",),
+            px_first[:2] + ("h",), px_first[:2] + ("h",), ((PAGES,) + py_first[0], BF16, "h"), down[:2] + ("h",), down[:2] + ("h",),
             ((8, 128), F32, "v"), ((slots, 128), F32, "h"),
         ],
         [
@@ -805,7 +814,8 @@
     ).reshape(slots, 128)
     n_even, n_odd = call(
         first_py_kernel, [py_first, py_first],
-        [(r_even, "v"), (r_odd, "v"), (both, "v")],
+        [(r_even, "v"), (r_odd, "v"), (both, "b")],
+        copies=2, vmem=50 * 1000 * 1000,
     )
     (known,) = call(
         decay_kernel, [((ROOM, 8, 128), F32, "h")],
@@ -821,7 +831,7 @@
             ((2 * OWN, 8, 128), F32, "v"), ((3 * OWN, 8, 128), F32, "v"), px_shape, px_shape, py_shape, py_shape,
             ((16, 128), jnp.int32, "v"), ((4 * ROWS, 8, 128), F32, "v"), py_first, down, down,
         ],
-        [(lines, "v")] + weights + [(known, "b")],
+        [(lines, "v")] + weights[:4] + [(a, "h") for a, _ in weights[4:]] + [(known, "b")],
         [places, places, lookup, pltpu.VMEM((KNOWN, 8, 128), F32)], copies=3,
     )
     weights = weights[:4] + [(a, "v") for a in late]

time: 93.4 us -> 92.9 us (level)
  local copies, waits for them, and re-layouts: 1.01 us -> 0.02 us
    unnamed x10 -> x8, local copies, waits for them, and re-layouts: 1.01 us -> 0.02 us
  transfers between devices with their start and end apart: 19 -> 19, of which waited for: 9 -> 9; matrix products, arithmetic and copies ran while one was open for 0% -> 0% of each run, Pallas kernels for 9% -> 10%
where the time goes in v4:
time: 92.9 us; the launch traced here: 92.3 us
  starting transfers between devices  43.3 us (47%)
  Pallas kernels  26 us (28%)
  waiting for transfers between devices  21.8 us (23%)
  between operations  1.07 us (1%)
    ppermute x9, starting transfers between devices, exchange(): lax.ppermute(for_odd, axis, swap_odd(axis))  26.3 us
    pallas_call x12, Pallas kernels, call(): pl.pallas_call(wrapped, out_shape=[jax.ShapeDtypeStruct(shape, dtype) for...  26 us
    ppermute x9, waiting for transfers between devices, exchange(): lax.ppermute(for_odd, axis, swap_odd(axis))  19 us
    all_to_all x1, starting transfers between devices, body(): lax.all_to_all(sent.reshape(devices, CAP, 128), ('px', 'py'), split_axis=...  11.3 us
    ppermute x9, starting transfers between devices, exchange(): lax.ppermute(for_even, axis, swap_even(axis))  5.66 us
    ppermute x9, waiting for transfers between devices, exchange(): lax.ppermute(for_even, axis, swap_even(axis))  2.84 us
  transfers between devices with their start and end apart: 19, of which 9 were waited for; matrix products, arithmetic and copies ran while one was open for 0% of the time, Pallas kernels for 10%

profile of v4, /device:TPU:10, one launch (start us, length us, event | category | flops | bytes accessed | tf_op | source)
XLA Modules:
  0.0 92.3 jit_solution(711873978374967423)
XLA Ops:
  0.6 4.2 %shard_map.113 = (bf16[592,512]{1,0:T(8,128)(2,1)}, bf16[592,512]{1,0:T(8,128)(2,1)}, bf16[96,192,512]{2,1,0:T(8,128)(2,1)}, bf16[4,64,512]{2,1,0:T(8,128)(2,1)}...) custom-call(s32[1,8]{1,0:T(1,128)} %bitcast.5, f32[256,128]{1,0:T(8,128)} %refs_1_.5, ...), custom_call_target="tpu_custom_call" | custom-call | tf_op jit(solution)/shard_map/pallas_call | solution.py:108
  4.9 2.4 %collective-permute-start.1 = (bf16[592,512]{1,0:T(8,128)(2,1)}, bf16[592,512]{1,0:T(8,128)(2,1)S(1)}, u32[]{:S(2)}, u32[]{:S(2)}) collective-permute-start(bf16[592,512]{1,0:T(8,128)(2,1)} %get-tuple-element.52), channel_id=1, source_target_pairs={{16,32},{48,64},{80,96},{32,16},{64,48},{96,80},{17,33},{49,65},{8... | collective-permute-start | bytes 1818632 | tf_op jit(solution)/shard_map/ppermute | solution.py:766
  7.4 11.3 %all-to-all-start = ((f32[128,8,128]{2,1,0:T(8,128)}), f32[128,8,128]{2,1,0:T(8,128)}, u32[]{:S(2)}, u32[]{:S(2)}) async-start(f32[128,8,128]{2,1,0:T(8,128)} %bitcast.6), calls=%async_computation | async-start | bytes 1048576 | tf_op jit(solution)/shard_map/all_to_all | solution.py:812
  18.7 1.7 %collective-permute-start.4 = (bf16[4,64,512]{2,1,0:T(8,128)(2,1)}, bf16[4,64,512]{2,1,0:T(8,128)(2,1)}, u32[]{:S(2)}, u32[]{:S(2)}) collective-permute-start(bf16[4,64,512]{2,1,0:T(8,128)(2,1)} %get-tuple-element.58), channel_id=1, source_target_pairs={{0,1},{1,0},{2,3},{3,2},{4,5},{5,4},{6,7},{7,6},{8,9},{9,8},{10,11... | collective-permute-start | bytes 786440 | tf_op jit(solution)/shard_map/ppermute | solution.py:766
  20.5 4.2 %collective-permute-start.5 = (bf16[4,64,512]{2,1,0:T(8,128)(2,1)}, bf16[4,64,512]{2,1,0:T(8,128)(2,1)}, u32[]{:S(2)}, u32[]{:S(2)}) collective-permute-start(bf16[4,64,512]{2,1,0:T(8,128)(2,1)} %get-tuple-element.59), channel_id=1, source_target_pairs={{1,2},{3,4},{5,6},{7,8},{9,10},{11,12},{13,14},{2,1},{4,3},{6,5},{... | collective-permute-start | bytes 786440 | tf_op jit(solution)/shard_map/ppermute | solution.py:766
  27.3 3.0 %collective-permute-start.3 = (bf16[192,512]{1,0:T(8,128)(2,1)}, bf16[192,512]{1,0:T(8,128)(2,1)}, u32[]{:S(2)}, u32[]{:S(2)}) collective-permute-start(bf16[192,512]{1,0:T(8,128)(2,1)} %get-tuple-element.57), channel_id=1, source_target_pairs={{1,2},{3,4},{5,6},{7,8},{9,10},{11,12},{13,14},{2,1},{4,3},{6,5},{... | collective-permute-start | bytes 589832 | tf_op jit(solution)/shard_map/ppermute | solution.py:766
  30.3 3.3 %shard_map.115.refs_8_.refs_3_ = f32[12288,8,128]{2,1,0:T(8,128)} custom-call(bf16[192,512]{1,0:T(8,128)(2,1)} %copy-done.1, f32[4,8,1024]{2,1,0:T(8,128)} %refs_1_.6, f32[4,4,8,1024]{3,2,1,0:T(8,128)} %refs_2_.1, f32[4,8,64]{2,1,0:T(8,128)} %refs_3_.1, f32[4,4,8,64]{3,2,1,0:T(8,128)} %refs_4_.3), custom_call_target="tpu_custom_call" | custom-call | tf_op jit(solution)/shard_map/pallas_call | solution.py:108
  33.6 2.7 %collective-permute-done.2.refs_4_ = bf16[192,512]{1,0:T(8,128)(2,1)S(1)} collective-permute-done((bf16[192,512]{1,0:T(8,128)(2,1)S(1)}, bf16[192,512]{1,0:T(8,128)(2,1)S(1)}, u32[]{:S(2)}, u32[]{:S(2)}) %collective-permute-start.2) | collective-permute-done | bytes 196640 | tf_op jit(solution)/shard_map/ppermute | solution.py:766
  36.3 2.2 %collective-permute-done.3.refs_5_ = bf16[192,512]{1,0:T(8,128)(2,1)} collective-permute-done((bf16[192,512]{1,0:T(8,128)(2,1)}, bf16[192,512]{1,0:T(8,128)(2,1)}, u32[]{:S(2)}, u32[]{:S(2)}) %collective-permute-start.3) | collective-permute-done | bytes 196640 | tf_op jit(solution)/shard_map/ppermute | solution.py:766
  38.5 4.2 %shard_map.116 = (f32[64,8,128]{2,1,0:T(8,128)S(1)}, f32[96,8,128]{2,1,0:T(8,128)S(1)}, bf16[16,16,128]{2,1,0:T(8,128)(2,1)S(1)}, bf16[16,16,128]{2,1,0:T(8,128)...) custom-call(f32[8,128]{1,0:T(8,128)S(1)} %copy-done.2, ...), custom_call_target="tpu_custom_call" | custom-call | tf_op jit(solution)/shard_map/pallas_call | solution.py:108
  42.7 2.1 %collective-permute-start.7 = (bf16[16,16,128]{2,1,0:T(8,128)(2,1)S(1)}, bf16[16,16,128]{2,1,0:T(8,128)(2,1)S(1)}, u32[]{:S(2)}, u32[]{:S(2)}) collective-permute-start(bf16[16,16,128]{2,1,0:T(8,128)(2,1)S(1)} %get-tuple-element.65), channel_id=1, source_target_pairs={{16,32},{48,64},{80,96},{32,16},{64,48},{96,80},{17,33},{49,65},{8... | collective-permute-start | bytes 196616 | tf_op jit(solution)/shard_map/ppermute | solution.py:766
  45.9 2.5 %collective-permute-done.7.refs_1_.refs_9_ = bf16[16,16,128]{2,1,0:T(8,128)(2,1)S(1)} collective-permute-done((bf16[16,16,128]{2,1,0:T(8,128)(2,1)S(1)}, bf16[16,16,128]{2,1,0:T(8,128)(2,1)S(1)}, u32[]{:S(2)}, u32[]{:S(2)}) %collective-permute-start.7) | collective-permute-done | bytes 65568 | tf_op jit(solution)/shard_map/ppermute | solution.py:766
  48.6 3.5 %collective-permute-start.9 = (bf16[14,16,128]{2,1,0:T(8,128)(2,1)S(1)}, bf16[14,16,128]{2,1,0:T(8,128)(2,1)S(1)}, u32[]{:S(2)}, u32[]{:S(2)}) collective-permute-start(bf16[14,16,128]{2,1,0:T(8,128)(2,1)S(1)} %get-tuple-element.69), channel_id=1, source_target_pairs={{1,2},{3,4},{5,6},{7,8},{9,10},{11,12},{13,14},{2,1},{4,3},{6,5},{... | collective-permute-start | bytes 172040 | tf_op jit(solution)/shard_map/ppermute | solution.py:766
  52.1 3.4 %shard_map.118 = (f32[4,32,8,128]{3,2,1,0:T(8,128)S(1)}, f32[4,32,8,128]{3,2,1,0:T(8,128)S(1)}) custom-call(s32[8]{0:T(128)S(1)} %copy-done.3, f32[1024,128]{1,0:T(8,128)} %bitcast.4.refs_1_, bf16[16,16,128]{2,1,0:T(8,128)(2,1)S(1)} %get-tuple-element.64.refs_2_), custom_call_target="tpu_custom_call" | custom-call | tf_op jit(solution)/shard_map/pallas_call | solution.py:108
  56.8 4.5 %shard_map.119 = (f32[32,8,128]{2,1,0:T(8,128)S(1)}, f32[40,8,128]{2,1,0:T(8,128)S(1)}, f32[48,8,128]{2,1,0:T(8,128)S(1)}, bf16[17,16,128]{2,1,0:T(8,128)(2,1)S(1)}, bf16[17,16,128]{2,1,0:T(8,128)(2,1)S(1)}) custom-call(s32[16,128]{1,0:T(8,128)S(1)} %get-tuple-element.60.refs_0_, bf16[4,8,64,512]{3,2,1,0:T(8,128)(2,1)S(1)} %copy-done, ...), custom_call_target="tpu_custom_call" | custom-call | tf_op jit(solution)/shard_map/pallas_call | solution.py:108
  61.4 1.9 %collective-permute-start.11 = (bf16[17,16,128]{2,1,0:T(8,128)(2,1)S(1)}, bf16[17,16,128]{2,1,0:T(8,128)(2,1)S(1)}, u32[]{:S(2)}, u32[]{:S(2)}) collective-permute-start(bf16[17,16,128]{2,1,0:T(8,128)(2,1)S(1)} %get-tuple-element.78), channel_id=1, source_target_pairs={{16,32},{48,64},{80,96},{32,16},{64,48},{96,80},{17,33},{49,65},{8... | collective-permute-start | bytes 208904 | tf_op jit(solution)/shard_map/ppermute | solution.py:766
  63.3 3.7 %collective-permute-done.11.refs_3_ = bf16[17,16,128]{2,1,0:T(8,128)(2,1)S(1)} collective-permute-done((bf16[17,16,128]{2,1,0:T(8,128)(2,1)S(1)}, bf16[17,16,128]{2,1,0:T(8,128)(2,1)S(1)}, u32[]{:S(2)}, u32[]{:S(2)}) %collective-permute-start.11) | collective-permute-done | bytes 69664 | tf_op jit(solution)/shard_map/ppermute | solution.py:766
  67.2 3.7 %collective-permute-start.13 = (bf16[6,16,128]{2,1,0:T(8,128)(2,1)S(1)}, bf16[6,16,128]{2,1,0:T(8,128)(2,1)S(1)}, u32[]{:S(2)}, u32[]{:S(2)}) collective-permute-start(bf16[6,16,128]{2,1,0:T(8,128)(2,1)S(1)} %get-tuple-element.82), channel_id=1, source_target_pairs={{1,2},{3,4},{5,6},{7,8},{9,10},{11,12},{13,14},{2,1},{4,3},{6,5},{... | collective-permute-start | bytes 73736 | tf_op jit(solution)/shard_map/ppermute | solution.py:766
  71.0 4.0 %collective-permute-done.13.refs_11_ = bf16[6,16,128]{2,1,0:T(8,128)(2,1)S(1)} collective-permute-done((bf16[6,16,128]{2,1,0:T(8,128)(2,1)S(1)}, bf16[6,16,128]{2,1,0:T(8,128)(2,1)S(1)}, u32[]{:S(2)}, u32[]{:S(2)}) %collective-permute-start.13) | collective-permute-done | bytes 24608 | tf_op jit(solution)/shard_map/ppermute | solution.py:766
  75.0 2.7 %shard_map.121 = (f32[64,8,128]{2,1,0:T(8,128)S(1)}, f32[40,8,128]{2,1,0:T(8,128)S(1)}, f32[48,8,128]{2,1,0:T(8,128)S(1)}, bf16[17,16,128]{2,1,0:T(8,128)(2,1)S(1)}, bf16[17,16,128]{2,1,0:T(8,128)(2,1)S(1)}) custom-call(s32[16,128]{1,0:T(8,128)S(1)} %get-tuple-element.60.refs_0_, bf16[4,8,64,512]{3,2,1,0:T(8,128)(2,1)S(1)} %copy-done, ...), custom_call_target="tpu_custom_call" | custom-call | tf_op jit(solution)/shard_map/pallas_call | solution.py:108
  77.7 1.9 %collective-permute-start.15 = (bf16[17,16,128]{2,1,0:T(8,128)(2,1)S(1)}, bf16[17,16,128]{2,1,0:T(8,128)(2,1)S(1)}, u32[]{:S(2)}, u32[]{:S(2)}) collective-permute-start(bf16[17,16,128]{2,1,0:T(8,128)(2,1)S(1)} %get-tuple-element.88), channel_id=1, source_target_pairs={{16,32},{48,64},{80,96},{32,16},{64,48},{96,80},{17,33},{49,65},{8... | collective-permute-start | bytes 208904 | tf_op jit(solution)/shard_map/ppermute | solution.py:766
  81.0 2.3 %collective-permute-done.15.refs_3_ = bf16[17,16,128]{2,1,0:T(8,128)(2,1)S(1)} collective-permute-done((bf16[17,16,128]{2,1,0:T(8,128)(2,1)S(1)}, bf16[17,16,128]{2,1,0:T(8,128)(2,1)S(1)}, u32[]{:S(2)}, u32[]{:S(2)}) %collective-permute-start.15) | collective-permute-done | bytes 69664 | tf_op jit(solution)/shard_map/ppermute | solution.py:766
  83.5 3.5 %collective-permute-start.17 = (bf16[6,16,128]{2,1,0:T(8,128)(2,1)S(1)}, bf16[6,16,128]{2,1,0:T(8,128)(2,1)S(1)}, u32[]{:S(2)}, u32[]{:S(2)}) collective-permute-start(bf16[6,16,128]{2,1,0:T(8,128)(2,1)S(1)} %get-tuple-element.92), channel_id=1, source_target_pairs={{1,2},{3,4},{5,6},{7,8},{9,10},{11,12},{13,14},{2,1},{4,3},{6,5},{... | collective-permute-start | bytes 73736 | tf_op jit(solution)/shard_map/ppermute | solution.py:766
  88.3 3.0 %collective-permute-done.17.refs_3_ = bf16[6,16,128]{2,1,0:T(8,128)(2,1)S(1)} collective-permute-done((bf16[6,16,128]{2,1,0:T(8,128)(2,1)S(1)}, bf16[6,16,128]{2,1,0:T(8,128)(2,1)S(1)}, u32[]{:S(2)}, u32[]{:S(2)}) %collective-permute-start.17) | collective-permute-done | bytes 24608 | tf_op jit(solution)/shard_map/ppermute | solution.py:766
  (34 shorter events, 9.2 us)
Async XLA Ops:
  4.8 2.6 %collective-permute-start = (bf16[592,512]{1,0:T(8,128)(2,1)}, bf16[592,512]{1,0:T(8,128)(2,1)S(1)}, u32[]{:S(2)}, u32[]{:S(2)}) collective-permute-start(bf16[592,512]{1,0:T(8,128)(2,1)} %get-tuple-element.50), channel_id=1, source_target_pairs={{0,16},{16,0},{32,48},{48,32},{64,80},{80,64},{96,112},{112,96},{1... | collective-permute-start | bytes 1818632 | tf_op jit(solution)/shard_map/ppermute | solution.py:766
  4.9 19.8 %collective-permute-start.1 = (bf16[592,512]{1,0:T(8,128)(2,1)}, bf16[592,512]{1,0:T(8,128)(2,1)S(1)}, u32[]{:S(2)}, u32[]{:S(2)}) collective-permute-start(bf16[592,512]{1,0:T(8,128)(2,1)} %get-tuple-element.52), channel_id=1, source_target_pairs={{16,32},{48,64},{80,96},{32,16},{64,48},{96,80},{17,33},{49,65},{8... | collective-permute-start | bytes 1818632 | tf_op jit(solution)/shard_map/ppermute | solution.py:766
  7.4 29.0 %all-to-all-start = ((f32[128,8,128]{2,1,0:T(8,128)}), f32[128,8,128]{2,1,0:T(8,128)}, u32[]{:S(2)}, u32[]{:S(2)}) async-start(f32[128,8,128]{2,1,0:T(8,128)} %bitcast.6), calls=%async_computation | async-start | bytes 1048576 | tf_op jit(solution)/shard_map/all_to_all | solution.py:812
  18.7 17.6 %collective-permute-start.4 = (bf16[4,64,512]{2,1,0:T(8,128)(2,1)}, bf16[4,64,512]{2,1,0:T(8,128)(2,1)}, u32[]{:S(2)}, u32[]{:S(2)}) collective-permute-start(bf16[4,64,512]{2,1,0:T(8,128)(2,1)} %get-tuple-element.58), channel_id=1, source_target_pairs={{0,1},{1,0},{2,3},{3,2},{4,5},{5,4},{6,7},{7,6},{8,9},{9,8},{10,11... | collective-permute-start | bytes 786440 | tf_op jit(solution)/shard_map/ppermute | solution.py:766
  20.5 15.9 %collective-permute-start.5 = (bf16[4,64,512]{2,1,0:T(8,128)(2,1)}, bf16[4,64,512]{2,1,0:T(8,128)(2,1)}, u32[]{:S(2)}, u32[]{:S(2)}) collective-permute-start(bf16[4,64,512]{2,1,0:T(8,128)(2,1)} %get-tuple-element.59), channel_id=1, source_target_pairs={{1,2},{3,4},{5,6},{7,8},{9,10},{11,12},{13,14},{2,1},{4,3},{6,5},{... | collective-permute-start | bytes 786440 | tf_op jit(solution)/shard_map/ppermute | solution.py:766
  26.3 4.0 %copy-start.1 = (bf16[192,512]{1,0:T(8,128)(2,1)}, bf16[192,512]{1,0:T(8,128)(2,1)S(1)}, u32[]{:S(2)}) copy-start(bf16[192,512]{1,0:T(8,128)(2,1)S(1)} %get-tuple-element.55.refs_0_) | copy-start | bytes 589828
  26.3 10.0 %collective-permute-start.2 = (bf16[192,512]{1,0:T(8,128)(2,1)S(1)}, bf16[192,512]{1,0:T(8,128)(2,1)S(1)}, u32[]{:S(2)}, u32[]{:S(2)}) collective-permute-start(bf16[192,512]{1,0:T(8,128)(2,1)S(1)} %get-tuple-element.55.refs_0_), channel_id=1, source_target_pairs={{0,1},{1,0},{2,3},{3,2},{4,5},{5,4},{6,7},{7,6},{8,9},{9,8},{10,11... | collective-permute-start | bytes 589832 | tf_op jit(solution)/shard_map/ppermute | solution.py:766
  27.3 11.3 %copy-start = (bf16[4,8,64,512]{3,2,1,0:T(8,128)(2,1)S(1)}, bf16[4,8,64,512]{3,2,1,0:T(8,128)(2,1)}, u32[]{:S(2)}) copy-start(bf16[4,8,64,512]{3,2,1,0:T(8,128)(2,1)} %refs_1_.9) | copy-start | bytes 6291460
  27.3 11.3 %copy-start.2 = (f32[8,128]{1,0:T(8,128)S(1)}, f32[8,128]{1,0:T(8,128)}, u32[]{:S(2)}) copy-start(f32[8,128]{1,0:T(8,128)} %get-tuple-element.48.refs_0_) | copy-start | bytes 12292
  27.3 11.3 %collective-permute-start.3 = (bf16[192,512]{1,0:T(8,128)(2,1)}, bf16[192,512]{1,0:T(8,128)(2,1)}, u32[]{:S(2)}, u32[]{:S(2)}) collective-permute-start(bf16[192,512]{1,0:T(8,128)(2,1)} %get-tuple-element.57), channel_id=1, source_target_pairs={{1,2},{3,4},{5,6},{7,8},{9,10},{11,12},{13,14},{2,1},{4,3},{6,5},{... | collective-permute-start | bytes 589832 | tf_op jit(solution)/shard_map/ppermute | solution.py:766
  38.5 13.5 %copy-start.3 = (s32[8]{0:T(128)S(1)}, s32[8]{0:T(128)}, u32[]{:S(2)}) copy-start(s32[8]{0:T(128)} %refs_0_.1) | copy-start | bytes 100
  42.7 5.6 %collective-permute-start.7 = (bf16[16,16,128]{2,1,0:T(8,128)(2,1)S(1)}, bf16[16,16,128]{2,1,0:T(8,128)(2,1)S(1)}, u32[]{:S(2)}, u32[]{:S(2)}) collective-permute-start(bf16[16,16,128]{2,1,0:T(8,128)(2,1)S(1)} %get-tuple-element.65), channel_id=1, source_target_pairs={{16,32},{48,64},{80,96},{32,16},{64,48},{96,80},{17,33},{49,65},{8... | collective-permute-start | bytes 196616 | tf_op jit(solution)/shard_map/ppermute | solution.py:766
  44.8 3.5 %collective-permute-start.6 = (bf16[16,16,128]{2,1,0:T(8,128)(2,1)S(1)}, bf16[16,16,128]{2,1,0:T(8,128)(2,1)S(1)}, u32[]{:S(2)}, u32[]{:S(2)}) collective-permute-start(bf16[16,16,128]{2,1,0:T(8,128)(2,1)S(1)} %get-tuple-element.64.refs_2_), channel_id=1, source_target_pairs={{0,16},{16,0},{32,48},{48,32},{64,80},{80,64},{96,112},{112,96},{1... | collective-permute-start | bytes 196616 | tf_op jit(solution)/shard_map/ppermute | solution.py:766
  48.4 7.1 %collective-permute-start.8 = (bf16[14,16,128]{2,1,0:T(8,128)(2,1)S(1)}, bf16[14,16,128]{2,1,0:T(8,128)(2,1)S(1)}, u32[]{:S(2)}, u32[]{:S(2)}) collective-permute-start(bf16[14,16,128]{2,1,0:T(8,128)(2,1)S(1)} %get-tuple-element.68), channel_id=1, source_target_pairs={{0,1},{1,0},{2,3},{3,2},{4,5},{5,4},{6,7},{7,6},{8,9},{9,8},{10,11... | collective-permute-start | bytes 172040 | tf_op jit(solution)/shard_map/ppermute | solution.py:766
  48.6 8.2 %collective-permute-start.9 = (bf16[14,16,128]{2,1,0:T(8,128)(2,1)S(1)}, bf16[14,16,128]{2,1,0:T(8,128)(2,1)S(1)}, u32[]{:S(2)}, u32[]{:S(2)}) collective-permute-start(bf16[14,16,128]{2,1,0:T(8,128)(2,1)S(1)} %get-tuple-element.69), channel_id=1, source_target_pairs={{1,2},{3,4},{5,6},{7,8},{9,10},{11,12},{13,14},{2,1},{4,3},{6,5},{... | collective-permute-start | bytes 172040 | tf_op jit(solution)/shard_map/ppermute | solution.py:766
  61.3 2.0 %collective-permute-start.10 = (bf16[17,16,128]{2,1,0:T(8,128)(2,1)S(1)}, bf16[17,16,128]{2,1,0:T(8,128)(2,1)S(1)}, u32[]{:S(2)}, u32[]{:S(2)}) collective-permute-start(bf16[17,16,128]{2,1,0:T(8,128)(2,1)S(1)} %get-tuple-element.77), channel_id=1, source_target_pairs={{0,16},{16,0},{32,48},{48,32},{64,80},{80,64},{96,112},{112,96},{1... | collective-permute-start | bytes 208904 | tf_op jit(solution)/shard_map/ppermute | solution.py:766
  61.4 5.6 %collective-permute-start.11 = (bf16[17,16,128]{2,1,0:T(8,128)(2,1)S(1)}, bf16[17,16,128]{2,1,0:T(8,128)(2,1)S(1)}, u32[]{:S(2)}, u32[]{:S(2)}) collective-permute-start(bf16[17,16,128]{2,1,0:T(8,128)(2,1)S(1)} %get-tuple-element.78), channel_id=1, source_target_pairs={{16,32},{48,64},{80,96},{32,16},{64,48},{96,80},{17,33},{49,65},{8... | collective-permute-start | bytes 208904 | tf_op jit(solution)/shard_map/ppermute | solution.py:766
  67.1 3.9 %collective-permute-start.12 = (bf16[6,16,128]{2,1,0:T(8,128)(2,1)S(1)}, bf16[6,16,128]{2,1,0:T(8,128)(2,1)S(1)}, u32[]{:S(2)}, u32[]{:S(2)}) collective-permute-start(bf16[6,16,128]{2,1,0:T(8,128)(2,1)S(1)} %get-tuple-element.81), channel_id=1, source_target_pairs={{0,1},{1,0},{2,3},{3,2},{4,5},{5,4},{6,7},{7,6},{8,9},{9,8},{10,11... | collective-permute-start | bytes 73736 | tf_op jit(solution)/shard_map/ppermute | solution.py:766
  67.2 7.8 %collective-permute-start.13 = (bf16[6,16,128]{2,1,0:T(8,128)(2,1)S(1)}, bf16[6,16,128]{2,1,0:T(8,128)(2,1)S(1)}, u32[]{:S(2)}, u32[]{:S(2)}) collective-permute-start(bf16[6,16,128]{2,1,0:T(8,128)(2,1)S(1)} %get-tuple-element.82), channel_id=1, source_target_pairs={{1,2},{3,4},{5,6},{7,8},{9,10},{11,12},{13,14},{2,1},{4,3},{6,5},{... | collective-permute-start | bytes 73736 | tf_op jit(solution)/shard_map/ppermute | solution.py:766
  77.7 5.6 %collective-permute-start.15 = (bf16[17,16,128]{2,1,0:T(8,128)(2,1)S(1)}, bf16[17,16,128]{2,1,0:T(8,128)(2,1)S(1)}, u32[]{:S(2)}, u32[]{:S(2)}) collective-permute-start(bf16[17,16,128]{2,1,0:T(8,128)(2,1)S(1)} %get-tuple-element.88), channel_id=1, source_target_pairs={{16,32},{48,64},{80,96},{32,16},{64,48},{96,80},{17,33},{49,65},{8... | collective-permute-start | bytes 208904 | tf_op jit(solution)/shard_map/ppermute | solution.py:766
  79.6 3.7 %collective-permute-start.14 = (bf16[17,16,128]{2,1,0:T(8,128)(2,1)S(1)}, bf16[17,16,128]{2,1,0:T(8,128)(2,1)S(1)}, u32[]{:S(2)}, u32[]{:S(2)}) collective-permute-start(bf16[17,16,128]{2,1,0:T(8,128)(2,1)S(1)} %get-tuple-element.87.refs_0_), channel_id=1, source_target_pairs={{0,16},{16,0},{32,48},{48,32},{64,80},{80,64},{96,112},{112,96},{1... | collective-permute-start | bytes 208904 | tf_op jit(solution)/shard_map/ppermute | solution.py:766
  83.4 4.9 %collective-permute-start.16 = (bf16[6,16,128]{2,1,0:T(8,128)(2,1)S(1)}, bf16[6,16,128]{2,1,0:T(8,128)(2,1)S(1)}, u32[]{:S(2)}, u32[]{:S(2)}) collective-permute-start(bf16[6,16,128]{2,1,0:T(8,128)(2,1)S(1)} %get-tuple-element.91), channel_id=1, source_target_pairs={{0,1},{1,0},{2,3},{3,2},{4,5},{5,4},{6,7},{7,6},{8,9},{9,8},{10,11... | collective-permute-start | bytes 73736 | tf_op jit(solution)/shard_map/ppermute | solution.py:766
  83.5 7.8 %collective-permute-start.17 = (bf16[6,16,128]{2,1,0:T(8,128)(2,1)S(1)}, bf16[6,16,128]{2,1,0:T(8,128)(2,1)S(1)}, u32[]{:S(2)}, u32[]{:S(2)}) collective-permute-start(bf16[6,16,128]{2,1,0:T(8,128)(2,1)S(1)} %get-tuple-element.92), channel_id=1, source_target_pairs={{1,2},{3,4},{5,6},{7,8},{9,10},{11,12},{13,14},{2,1},{4,3},{6,5},{... | collective-permute-start | bytes 73736 | tf_op jit(solution)/shard_map/ppermute | solution.py:766

commit v5 on v4

--- a/solution.py
+++ b/solution.py
@@ -317,6 +317,10 @@
     flow.send(full, out.at[pl.ds(0, KNOWN)])
 
 
+def load_kernel(flow, after, stored, out):
+    flow.send(stored.at[pl.ds(0, KNOWN)], out)
+
+
 class Coefs:
     def __init__(self, ref):
         self.ref = ref
@@ -363,7 +367,7 @@
     return target
 
 
-def table_lines(par, lines, r_even, r_odd, n_even, n_odd):
+def first_lines(par, lines, r_even, r_odd):
     row = lax.broadcasted_iota(jnp.int32, (8, 128), 0)
     lane = lax.broadcasted_iota(jnp.int32, (8, 128), 1)
     row_even, row_odd = sides(par, 0, ROWS, -1)
@@ -371,12 +375,18 @@
     even = Tiles(r_even, PX_BASE)[16].astype(F32)[:8]
     odd = Tiles(r_odd, PX_BASE)[16].astype(F32)[:8]
     first = jnp.where(row == ROWS, even, jnp.where(row == ROWS + 1, odd, lines))
-    parts = [first.astype(jnp.int32) + place(line, lane // 8)]
+    return first.astype(jnp.int32) + place(line, lane // 8)
+
+
+def last_lines(par, n_even, n_odd):
+    row = lax.broadcasted_iota(jnp.int32, (8, 128), 0)
+    lane = lax.broadcasted_iota(jnp.int32, (8, 128), 1)
+    row_even, row_odd = sides(par, 0, ROWS, -1)
+    line = jnp.where(row == ROWS, row_even, jnp.where(row == ROWS + 1, row_odd, row))
     ends = []
     for msg, col in zip((n_even, n_odd), sides(par, 1, COLS, -1)):
         ends.append(Tiles(msg, PY_BASE)[14].astype(F32)[:8].astype(jnp.int32) + place(line, col))
-    parts.append(jnp.where(lane < 64, ends[0], pltpu.roll(ends[1], 64, 1)))
-    return jnp.concatenate(parts, 0)
+    return jnp.where(lane < 64, ends[0], pltpu.roll(ends[1], 64, 1))
 
 
 def forward_pair(par, target, arrive, ready, arrived, blocks, plain, received, field, middle, store_first, store_second):
@@ -417,41 +427,48 @@
         )
         return unpacked(out)
 
-    arrived()
-    for number, (array, index, at) in enumerate(outer_places(par)):
-        got = product(field, OWN + number) + joined(received[array][8 + index])
-        middle[at] = doubled(got).astype(BF16)
+    outer = list(enumerate(outer_places(par)))
+
+    def rim(listed):
+        for number, (array, index, at) in listed:
+            got = product(field, OWN + number) + joined(received[array][8 + index])
+            middle[at] = doubled(got).astype(BF16)
+
+    rim(outer[: 2 * COLS])
     for block in range(OWN):
         got = store_first(block, product(field, block))
         middle[place(block // COLS, block % COLS)] = doubled(got).astype(BF16)
+    arrived()
+    rim(outer[2 * COLS :])
     for block in range(OWN):
         store_second(block, product(middle, block))
 
 
 def forward_one(
-    flow, lines, own, r_even, r_odd, n_even, n_odd, d_even, d_odd, stored, past, now, m_even, m_odd, p_even, p_odd, table_out,
+    flow, lines, own, r_even, r_odd, n_even, n_odd, d_even, d_odd, known, past, now, m_even, m_odd, p_even, p_odd, table_out,
     coefs_out, n_odd_out, d_even_out, d_odd_out,
-    field, middle, table, known,
+    field, middle, table,
 ):
     par = parity()
-    begun = flow.copy(stored.at[pl.ds(0, 2 * OWN)], known.at[pl.ds(0, 2 * OWN)])
-    rest = flow.copy(stored.at[pl.ds(2 * OWN, KNOWN - 2 * OWN)], known.at[pl.ds(2 * OWN, KNOWN - 2 * OWN)])
-    looked = []
+    halves_of = [pl.ds(0, 8), pl.ds(8, 8)]
+    table_out[halves_of[0], :] = first_lines(par, lines[...], r_even, r_odd)
+    looked = [flow.copy(table_out.at[halves_of[0], :], table.at[halves_of[0], :])]
 
     def arrive():
         flow.wait(n_odd)
-        table_out[...] = table_lines(par, lines[...], r_even, r_odd, n_even, n_odd)
-        looked.append(flow.copy(table_out, table))
+        table_out[halves_of[1], :] = last_lines(par, n_even, n_odd)
+        looked.append(flow.copy(table_out.at[halves_of[1], :], table.at[halves_of[1], :]))
+
+    def arrived():
+        looked[1].wait()
+        flow.wait(d_even, d_odd)
 
     coef = Coefs(known.at[pl.ds(COEF, 4 * ROWS)])
 
     def ready():
-        begun.wait()
         looked[0].wait()
 
     def first(block, out):
-        if block == 0:
-            rest.wait()
         got = out + known[ADDEND + block]
         past[block] = got
         full = known[SUM2 + block] + coef(1, block) * got
@@ -464,7 +481,7 @@
 
     received = (Tiles(r_even, PX_BASE), Tiles(r_odd, PX_BASE), Tiles(n_even, PY_BASE), Tiles(n_odd, PY_BASE))
     forward_pair(
-        par, targets_of(table, par), arrive, ready, lambda: flow.wait(d_even, d_odd), (own, r_even, r_odd, n_even, n_odd, d_even, d_odd), lambda block: known[FIELD + block],
+        par, targets_of(table, par), arrive, ready, arrived, (own, r_even, r_odd, n_even, n_odd, d_even, d_odd), lambda block: known[FIELD + block],
         received, field, middle, first, second,
     )
     get, add = (lambda at: now[at]), (lambda at: now[OWN + at])
@@ -824,6 +841,9 @@
     )
     n_even, n_odd = exchange("py", n_even, n_odd)
     held, n_even = lax.optimization_barrier((held, n_even))
+    (near,) = call(
+        load_kernel, [((KNOWN, 8, 128), F32, "v")], [(n_even, "v"), (known, "b")], copies=1,
+    )
     weights = [(a, "v") for a in (stiffness, r_even, r_odd, n_even, n_odd, d_even, d_odd)]
     past, now, m_even, m_odd, p_even, p_odd, table, coefs, *late = call(
         forward_one,
@@ -831,8 +851,8 @@
             ((2 * OWN, 8, 128), F32, "v"), ((3 * OWN, 8, 128), F32, "v"), px_shape, px_shape, py_shape, py_shape,
             ((16, 128), jnp.int32, "v"), ((4 * ROWS, 8, 128), F32, "v"), py_first, down, down,
         ],
-        [(lines, "v")] + weights[:4] + [(a, "h") for a, _ in weights[4:]] + [(known, "b")],
-        [places, places, lookup, pltpu.VMEM((KNOWN, 8, 128), F32)], copies=3,
+        [(lines, "v")] + weights[:4] + [(a, "h") for a, _ in weights[4:]] + [(near, "v")],
+        [places, places, lookup], copies=2,
     )
     weights = weights[:4] + [(a, "v") for a in late]
     r_even, r_odd = exchange("px", m_even, m_odd)

time: 92.9 us -> 92.5 us (level)
  starting transfers between devices: 43.3 us -> 47.4 us
  waiting for transfers between devices: 21.8 us -> 18.5 us
  Pallas kernels: 26 us -> 25 us
    ppermute x9, waiting for transfers between devices: 19 us -> 14.5 us  [exchange(): lax.ppermute(for_odd, axis, swap_odd(axis))]
    ppermute x9, starting transfers between devices: 26.3 us -> 30.7 us  [exchange(): lax.ppermute(for_odd, axis, swap_odd(axis))]
    ppermute x9, waiting for transfers between devices: 2.84 us -> 3.91 us  [exchange(): lax.ppermute(for_even, axis, swap_even(axis))]
    pallas_call x12 -> x13, Pallas kernels: 26 us -> 25 us  [call(): pl.pallas_call(wrapped, out_shape=[jax.ShapeDtypeStruct(shape, dtype) for...]
  transfers between devices with their start and end apart: 19 -> 19, of which waited for: 9 -> 8; matrix products, arithmetic and copies ran while one was open for 0% -> 0% of each run, Pallas kernels for 10% -> 10%
where the time goes in v5:
time: 92.5 us; the launch traced here: 91.9 us
  starting transfers between devices  47.4 us (51%)
  Pallas kernels  25 us (27%)
  waiting for transfers between devices  18.5 us (20%)
  between operations  1.09 us (1%)
    ppermute x9, starting transfers between devices, exchange(): lax.ppermute(for_odd, axis, swap_odd(axis))  30.7 us
    pallas_call x13, Pallas kernels, call(): pl.pallas_call(wrapped, out_shape=[jax.ShapeDtypeStruct(shape, dtype) for...  25 us
    ppermute x9, waiting for transfers between devices, exchange(): lax.ppermute(for_odd, axis, swap_odd(axis))  14.5 us
    all_to_all x1, starting transfers between devices, body(): lax.all_to_all(sent.reshape(devices, CAP, 128), ('px', 'py'), split_axis=...  10.9 us
    ppermute x9, starting transfers between devices, exchange(): lax.ppermute(for_even, axis, swap_even(axis))  5.82 us
    ppermute x9, waiting for transfers between devices, exchange(): lax.ppermute(for_even, axis, swap_even(axis))  3.91 us
  transfers between devices with their start and end apart: 19, of which 8 were waited for; matrix products, arithmetic and copies ran while one was open for 0% of the time, Pallas kernels for 10%

profile of v5, /device:TPU:10, one launch (start us, length us, event | category | flops | bytes accessed | tf_op | source)
XLA Modules:
  0.0 91.9 jit_solution(8015247042687449860)
XLA Ops:
  0.6 4.2 %shard_map.113 = (bf16[592,512]{1,0:T(8,128)(2,1)}, bf16[592,512]{1,0:T(8,128)(2,1)}, bf16[96,192,512]{2,1,0:T(8,128)(2,1)}, bf16[4,64,512]{2,1,0:T(8,128)(2,1)}...) custom-call(s32[1,8]{1,0:T(1,128)} %bitcast.6, f32[256,128]{1,0:T(8,128)} %refs_1_.5, ...), custom_call_target="tpu_custom_call" | custom-call | tf_op jit(solution)/shard_map/pallas_call | solution.py:108
  5.0 2.4 %collective-permute-start.1 = (bf16[592,512]{1,0:T(8,128)(2,1)}, bf16[592,512]{1,0:T(8,128)(2,1)S(1)}, u32[]{:S(2)}, u32[]{:S(2)}) collective-permute-start(bf16[592,512]{1,0:T(8,128)(2,1)} %get-tuple-element.52), channel_id=1, source_target_pairs={{16,32},{48,64},{80,96},{32,16},{64,48},{96,80},{17,33},{49,65},{8... | collective-permute-start | bytes 1818632 | tf_op jit(solution)/shard_map/ppermute | solution.py:783
  7.4 10.9 %all-to-all-start = ((f32[128,8,128]{2,1,0:T(8,128)}), f32[128,8,128]{2,1,0:T(8,128)S(1)}, u32[]{:S(2)}, u32[]{:S(2)}) async-start(f32[128,8,128]{2,1,0:T(8,128)} %bitcast.7), calls=%async_computation | async-start | bytes 1048576 | tf_op jit(solution)/shard_map/all_to_all | solution.py:829
  18.3 1.7 %collective-permute-start.4 = (bf16[4,64,512]{2,1,0:T(8,128)(2,1)}, bf16[4,64,512]{2,1,0:T(8,128)(2,1)S(1)}, u32[]{:S(2)}, u32[]{:S(2)}) collective-permute-start(bf16[4,64,512]{2,1,0:T(8,128)(2,1)} %get-tuple-element.58), channel_id=1, source_target_pairs={{0,1},{1,0},{2,3},{3,2},{4,5},{5,4},{6,7},{7,6},{8,9},{9,8},{10,11... | collective-permute-start | bytes 786440 | tf_op jit(solution)/shard_map/ppermute | solution.py:783
  20.1 4.2 %collective-permute-start.5 = (bf16[4,64,512]{2,1,0:T(8,128)(2,1)}, bf16[4,64,512]{2,1,0:T(8,128)(2,1)S(1)}, u32[]{:S(2)}, u32[]{:S(2)}) collective-permute-start(bf16[4,64,512]{2,1,0:T(8,128)(2,1)} %get-tuple-element.59), channel_id=1, source_target_pairs={{1,2},{3,4},{5,6},{7,8},{9,10},{11,12},{13,14},{2,1},{4,3},{6,5},{... | collective-permute-start | bytes 786440 | tf_op jit(solution)/shard_map/ppermute | solution.py:783
  26.1 2.9 %collective-permute-start.3 = (bf16[192,512]{1,0:T(8,128)(2,1)S(1)}, bf16[192,512]{1,0:T(8,128)(2,1)S(1)}, u32[]{:S(2)}, u32[]{:S(2)}) collective-permute-start(bf16[192,512]{1,0:T(8,128)(2,1)S(1)} %get-tuple-element.57), channel_id=1, source_target_pairs={{1,2},{3,4},{5,6},{7,8},{9,10},{11,12},{13,14},{2,1},{4,3},{6,5},{... | collective-permute-start | bytes 589832 | tf_op jit(solution)/shard_map/ppermute | solution.py:783
  29.1 3.3 %shard_map.115.refs_1_.refs_3_ = f32[12288,8,128]{2,1,0:T(8,128)} custom-call(bf16[192,512]{1,0:T(8,128)(2,1)} %copy-done.1, f32[4,8,1024]{2,1,0:T(8,128)} %refs_1_.6, f32[4,4,8,1024]{3,2,1,0:T(8,128)} %refs_2_.1, f32[4,8,64]{2,1,0:T(8,128)} %refs_3_.1, f32[4,4,8,64]{3,2,1,0:T(8,128)} %refs_4_.3), custom_call_target="tpu_custom_call" | custom-call | tf_op jit(solution)/shard_map/pallas_call | solution.py:108
  32.4 3.9 %collective-permute-done.2.refs_0_.refs_4_ = bf16[192,512]{1,0:T(8,128)(2,1)S(1)} collective-permute-done((bf16[192,512]{1,0:T(8,128)(2,1)S(1)}, bf16[192,512]{1,0:T(8,128)(2,1)S(1)}, u32[]{:S(2)}, u32[]{:S(2)}) %collective-permute-start.2) | collective-permute-done | bytes 196640 | tf_op jit(solution)/shard_map/ppermute | solution.py:783
  36.3 1.3 %shard_map.116.refs_8_ = f32[208,8,128]{2,1,0:T(8,128)S(1)} custom-call(bf16[192,512]{1,0:T(8,128)(2,1)S(1)} %collective-permute-done.2.refs_0_.refs_4_, f32[12288,8,128]{2,1,0:T(8,128)} %shard_map.115.refs_1_.refs_3_), custom_call_target="tpu_custom_call" | custom-call | tf_op jit(solution)/shard_map/pallas_call | solution.py:108
  38.5 3.4 %shard_map.117 = (f32[64,8,128]{2,1,0:T(8,128)S(1)}, f32[96,8,128]{2,1,0:T(8,128)S(1)}, bf16[16,16,128]{2,1,0:T(8,128)(2,1)S(1)}, bf16[16,16,128]{2,1,0:T(8,128)...) custom-call(f32[8,128]{1,0:T(8,128)S(1)} %copy-done.2, ...), custom_call_target="tpu_custom_call" | custom-call | tf_op jit(solution)/shard_map/pallas_call | solution.py:108
  41.9 2.3 %collective-permute-start.7 = (bf16[16,16,128]{2,1,0:T(8,128)(2,1)S(1)}, bf16[16,16,128]{2,1,0:T(8,128)(2,1)S(1)}, u32[]{:S(2)}, u32[]{:S(2)}) collective-permute-start(bf16[16,16,128]{2,1,0:T(8,128)(2,1)S(1)} %get-tuple-element.65), channel_id=1, source_target_pairs={{16,32},{48,64},{80,96},{32,16},{64,48},{96,80},{17,33},{49,65},{8... | collective-permute-start | bytes 196616 | tf_op jit(solution)/shard_map/ppermute | solution.py:783
  45.0 2.4 %collective-permute-done.7.refs_1_.refs_9_ = bf16[16,16,128]{2,1,0:T(8,128)(2,1)S(1)} collective-permute-done((bf16[16,16,128]{2,1,0:T(8,128)(2,1)S(1)}, bf16[16,16,128]{2,1,0:T(8,128)(2,1)S(1)}, u32[]{:S(2)}, u32[]{:S(2)}) %collective-permute-start.7) | collective-permute-done | bytes 65568 | tf_op jit(solution)/shard_map/ppermute | solution.py:783
  47.7 5.1 %collective-permute-start.9 = (bf16[14,16,128]{2,1,0:T(8,128)(2,1)S(1)}, bf16[14,16,128]{2,1,0:T(8,128)(2,1)S(1)}, u32[]{:S(2)}, u32[]{:S(2)}) collective-permute-start(bf16[14,16,128]{2,1,0:T(8,128)(2,1)S(1)} %get-tuple-element.69), channel_id=1, source_target_pairs={{1,2},{3,4},{5,6},{7,8},{9,10},{11,12},{13,14},{2,1},{4,3},{6,5},{... | collective-permute-start | bytes 172040 | tf_op jit(solution)/shard_map/ppermute | solution.py:783
  52.8 2.4 %shard_map.119 = (f32[4,32,8,128]{3,2,1,0:T(8,128)S(1)}, f32[4,32,8,128]{3,2,1,0:T(8,128)S(1)}) custom-call(s32[8]{0:T(128)S(1)} %copy-done.3, f32[1024,128]{1,0:T(8,128)S(1)} %bitcast.5, bf16[16,16,128]{2,1,0:T(8,128)(2,1)S(1)} %get-tuple-element.64.refs_2_), custom_call_target="tpu_custom_call" | custom-call | tf_op jit(solution)/shard_map/pallas_call | solution.py:108
  55.9 4.5 %shard_map.120 = (f32[32,8,128]{2,1,0:T(8,128)S(1)}, f32[40,8,128]{2,1,0:T(8,128)S(1)}, f32[48,8,128]{2,1,0:T(8,128)S(1)}, bf16[17,16,128]{2,1,0:T(8,128)(2,1)S(1)}, bf16[17,16,128]{2,1,0:T(8,128)(2,1)S(1)}) custom-call(s32[16,128]{1,0:T(8,128)S(1)} %get-tuple-element.60.refs_0_, bf16[4,8,64,512]{3,2,1,0:T(8,128)(2,1)S(1)} %copy-done, ...), custom_call_target="tpu_custom_call" | custom-call | tf_op jit(solution)/shard_map/pallas_call | solution.py:108
  60.5 1.9 %collective-permute-start.11 = (bf16[17,16,128]{2,1,0:T(8,128)(2,1)S(1)}, bf16[17,16,128]{2,1,0:T(8,128)(2,1)S(1)}, u32[]{:S(2)}, u32[]{:S(2)}) collective-permute-start(bf16[17,16,128]{2,1,0:T(8,128)(2,1)S(1)} %get-tuple-element.78), channel_id=1, source_target_pairs={{16,32},{48,64},{80,96},{32,16},{64,48},{96,80},{17,33},{49,65},{8... | collective-permute-start | bytes 208904 | tf_op jit(solution)/shard_map/ppermute | solution.py:783
  62.4 3.7 %collective-permute-done.11.refs_3_ = bf16[17,16,128]{2,1,0:T(8,128)(2,1)S(1)} collective-permute-done((bf16[17,16,128]{2,1,0:T(8,128)(2,1)S(1)}, bf16[17,16,128]{2,1,0:T(8,128)(2,1)S(1)}, u32[]{:S(2)}, u32[]{:S(2)}) %collective-permute-start.11) | collective-permute-done | bytes 69664 | tf_op jit(solution)/shard_map/ppermute | solution.py:783
  66.3 5.3 %collective-permute-start.13 = (bf16[6,16,128]{2,1,0:T(8,128)(2,1)S(1)}, bf16[6,16,128]{2,1,0:T(8,128)(2,1)S(1)}, u32[]{:S(2)}, u32[]{:S(2)}) collective-permute-start(bf16[6,16,128]{2,1,0:T(8,128)(2,1)S(1)} %get-tuple-element.82), channel_id=1, source_target_pairs={{1,2},{3,4},{5,6},{7,8},{9,10},{11,12},{13,14},{2,1},{4,3},{6,5},{... | collective-permute-start | bytes 73736 | tf_op jit(solution)/shard_map/ppermute | solution.py:783
  71.6 2.5 %collective-permute-done.13.refs_11_ = bf16[6,16,128]{2,1,0:T(8,128)(2,1)S(1)} collective-permute-done((bf16[6,16,128]{2,1,0:T(8,128)(2,1)S(1)}, bf16[6,16,128]{2,1,0:T(8,128)(2,1)S(1)}, u32[]{:S(2)}, u32[]{:S(2)}) %collective-permute-start.13) | collective-permute-done | bytes 24608 | tf_op jit(solution)/shard_map/ppermute | solution.py:783
  74.1 2.7 %shard_map.122 = (f32[64,8,128]{2,1,0:T(8,128)S(1)}, f32[40,8,128]{2,1,0:T(8,128)S(1)}, f32[48,8,128]{2,1,0:T(8,128)S(1)}, bf16[17,16,128]{2,1,0:T(8,128)(2,1)S(1)}, bf16[17,16,128]{2,1,0:T(8,128)(2,1)S(1)}) custom-call(s32[16,128]{1,0:T(8,128)S(1)} %get-tuple-element.60.refs_0_, bf16[4,8,64,512]{3,2,1,0:T(8,128)(2,1)S(1)} %copy-done, ...), custom_call_target="tpu_custom_call" | custom-call | tf_op jit(solution)/shard_map/pallas_call | solution.py:108
  76.9 1.9 %collective-permute-start.15 = (bf16[17,16,128]{2,1,0:T(8,128)(2,1)S(1)}, bf16[17,16,128]{2,1,0:T(8,128)(2,1)S(1)}, u32[]{:S(2)}, u32[]{:S(2)}) collective-permute-start(bf16[17,16,128]{2,1,0:T(8,128)(2,1)S(1)} %get-tuple-element.88), channel_id=1, source_target_pairs={{16,32},{48,64},{80,96},{32,16},{64,48},{96,80},{17,33},{49,65},{8... | collective-permute-start | bytes 208904 | tf_op jit(solution)/shard_map/ppermute | solution.py:783
  80.0 2.5 %collective-permute-done.15.refs_3_ = bf16[17,16,128]{2,1,0:T(8,128)(2,1)S(1)} collective-permute-done((bf16[17,16,128]{2,1,0:T(8,128)(2,1)S(1)}, bf16[17,16,128]{2,1,0:T(8,128)(2,1)S(1)}, u32[]{:S(2)}, u32[]{:S(2)}) %collective-permute-start.15) | collective-permute-done | bytes 69664 | tf_op jit(solution)/shard_map/ppermute | solution.py:783
  83.2 4.6 %collective-permute-start.17 = (bf16[6,16,128]{2,1,0:T(8,128)(2,1)S(1)}, bf16[6,16,128]{2,1,0:T(8,128)(2,1)S(1)}, u32[]{:S(2)}, u32[]{:S(2)}) collective-permute-start(bf16[6,16,128]{2,1,0:T(8,128)(2,1)S(1)} %get-tuple-element.92), channel_id=1, source_target_pairs={{1,2},{3,4},{5,6},{7,8},{9,10},{11,12},{13,14},{2,1},{4,3},{6,5},{... | collective-permute-start | bytes 73736 | tf_op jit(solution)/shard_map/ppermute | solution.py:783
  89.0 2.0 %collective-permute-done.17.refs_3_ = bf16[6,16,128]{2,1,0:T(8,128)(2,1)S(1)} collective-permute-done((bf16[6,16,128]{2,1,0:T(8,128)(2,1)S(1)}, bf16[6,16,128]{2,1,0:T(8,128)(2,1)S(1)}, u32[]{:S(2)}, u32[]{:S(2)}) %collective-permute-start.17) | collective-permute-done | bytes 24608 | tf_op jit(solution)/shard_map/ppermute | solution.py:783
  (35 shorter events, 8.7 us)
Async XLA Ops:
  4.9 2.6 %collective-permute-start = (bf16[592,512]{1,0:T(8,128)(2,1)}, bf16[592,512]{1,0:T(8,128)(2,1)S(1)}, u32[]{:S(2)}, u32[]{:S(2)}) collective-permute-start(bf16[592,512]{1,0:T(8,128)(2,1)} %get-tuple-element.50), channel_id=1, source_target_pairs={{0,16},{16,0},{32,48},{48,32},{64,80},{80,64},{96,112},{112,96},{1... | collective-permute-start | bytes 1818632 | tf_op jit(solution)/shard_map/ppermute | solution.py:783
  5.0 19.3 %collective-permute-start.1 = (bf16[592,512]{1,0:T(8,128)(2,1)}, bf16[592,512]{1,0:T(8,128)(2,1)S(1)}, u32[]{:S(2)}, u32[]{:S(2)}) collective-permute-start(bf16[592,512]{1,0:T(8,128)(2,1)} %get-tuple-element.52), channel_id=1, source_target_pairs={{16,32},{48,64},{80,96},{32,16},{64,48},{96,80},{17,33},{49,65},{8... | collective-permute-start | bytes 1818632 | tf_op jit(solution)/shard_map/ppermute | solution.py:783
  7.4 28.8 %all-to-all-start = ((f32[128,8,128]{2,1,0:T(8,128)}), f32[128,8,128]{2,1,0:T(8,128)S(1)}, u32[]{:S(2)}, u32[]{:S(2)}) async-start(f32[128,8,128]{2,1,0:T(8,128)} %bitcast.7), calls=%async_computation | async-start | bytes 1048576 | tf_op jit(solution)/shard_map/all_to_all | solution.py:829
  18.3 19.3 %collective-permute-start.4 = (bf16[4,64,512]{2,1,0:T(8,128)(2,1)}, bf16[4,64,512]{2,1,0:T(8,128)(2,1)S(1)}, u32[]{:S(2)}, u32[]{:S(2)}) collective-permute-start(bf16[4,64,512]{2,1,0:T(8,128)(2,1)} %get-tuple-element.58), channel_id=1, source_target_pairs={{0,1},{1,0},{2,3},{3,2},{4,5},{5,4},{6,7},{7,6},{8,9},{9,8},{10,11... | collective-permute-start | bytes 786440 | tf_op jit(solution)/shard_map/ppermute | solution.py:783
  20.1 17.5 %collective-permute-start.5 = (bf16[4,64,512]{2,1,0:T(8,128)(2,1)}, bf16[4,64,512]{2,1,0:T(8,128)(2,1)S(1)}, u32[]{:S(2)}, u32[]{:S(2)}) collective-permute-start(bf16[4,64,512]{2,1,0:T(8,128)(2,1)} %get-tuple-element.59), channel_id=1, source_target_pairs={{1,2},{3,4},{5,6},{7,8},{9,10},{11,12},{13,14},{2,1},{4,3},{6,5},{... | collective-permute-start | bytes 786440 | tf_op jit(solution)/shard_map/ppermute | solution.py:783
  25.2 3.8 %copy-start.1 = (bf16[192,512]{1,0:T(8,128)(2,1)}, bf16[192,512]{1,0:T(8,128)(2,1)S(1)}, u32[]{:S(2)}) copy-start(bf16[192,512]{1,0:T(8,128)(2,1)S(1)} %get-tuple-element.55.refs_0_) | copy-start | bytes 589828
  25.2 11.0 %collective-permute-start.2 = (bf16[192,512]{1,0:T(8,128)(2,1)S(1)}, bf16[192,512]{1,0:T(8,128)(2,1)S(1)}, u32[]{:S(2)}, u32[]{:S(2)}) collective-permute-start(bf16[192,512]{1,0:T(8,128)(2,1)S(1)} %get-tuple-element.55.refs_0_), channel_id=1, source_target_pairs={{0,1},{1,0},{2,3},{3,2},{4,5},{5,4},{6,7},{7,6},{8,9},{9,8},{10,11... | collective-permute-start | bytes 589832 | tf_op jit(solution)/shard_map/ppermute | solution.py:783
  26.1 12.3 %collective-permute-start.3 = (bf16[192,512]{1,0:T(8,128)(2,1)S(1)}, bf16[192,512]{1,0:T(8,128)(2,1)S(1)}, u32[]{:S(2)}, u32[]{:S(2)}) collective-permute-start(bf16[192,512]{1,0:T(8,128)(2,1)S(1)} %get-tuple-element.57), channel_id=1, source_target_pairs={{1,2},{3,4},{5,6},{7,8},{9,10},{11,12},{13,14},{2,1},{4,3},{6,5},{... | collective-permute-start | bytes 589832 | tf_op jit(solution)/shard_map/ppermute | solution.py:783
  36.3 2.2 %copy-start = (bf16[4,8,64,512]{3,2,1,0:T(8,128)(2,1)S(1)}, bf16[4,8,64,512]{3,2,1,0:T(8,128)(2,1)}, u32[]{:S(2)}) copy-start(bf16[4,8,64,512]{3,2,1,0:T(8,128)(2,1)} %refs_1_.9) | copy-start | bytes 6291460
  36.3 2.2 %copy-start.2 = (f32[8,128]{1,0:T(8,128)S(1)}, f32[8,128]{1,0:T(8,128)}, u32[]{:S(2)}) copy-start(f32[8,128]{1,0:T(8,128)} %get-tuple-element.48.refs_0_) | copy-start | bytes 12292
  36.3 16.6 %copy-start.3 = (s32[8]{0:T(128)S(1)}, s32[8]{0:T(128)}, u32[]{:S(2)}) copy-start(s32[8]{0:T(128)} %refs_0_.1) | copy-start | bytes 100
  41.9 5.6 %collective-permute-start.7 = (bf16[16,16,128]{2,1,0:T(8,128)(2,1)S(1)}, bf16[16,16,128]{2,1,0:T(8,128)(2,1)S(1)}, u32[]{:S(2)}, u32[]{:S(2)}) collective-permute-start(bf16[16,16,128]{2,1,0:T(8,128)(2,1)S(1)} %get-tuple-element.65), channel_id=1, source_target_pairs={{16,32},{48,64},{80,96},{32,16},{64,48},{96,80},{17,33},{49,65},{8... | collective-permute-start | bytes 196616 | tf_op jit(solution)/shard_map/ppermute | solution.py:783
  44.2 3.3 %collective-permute-start.6 = (bf16[16,16,128]{2,1,0:T(8,128)(2,1)S(1)}, bf16[16,16,128]{2,1,0:T(8,128)(2,1)S(1)}, u32[]{:S(2)}, u32[]{:S(2)}) collective-permute-start(bf16[16,16,128]{2,1,0:T(8,128)(2,1)S(1)} %get-tuple-element.64.refs_2_), channel_id=1, source_target_pairs={{0,16},{16,0},{32,48},{48,32},{64,80},{80,64},{96,112},{112,96},{1... | collective-permute-start | bytes 196616 | tf_op jit(solution)/shard_map/ppermute | solution.py:783
  47.5 7.8 %collective-permute-start.8 = (bf16[14,16,128]{2,1,0:T(8,128)(2,1)S(1)}, bf16[14,16,128]{2,1,0:T(8,128)(2,1)S(1)}, u32[]{:S(2)}, u32[]{:S(2)}) collective-permute-start(bf16[14,16,128]{2,1,0:T(8,128)(2,1)S(1)} %get-tuple-element.68), channel_id=1, source_target_pairs={{0,1},{1,0},{2,3},{3,2},{4,5},{5,4},{6,7},{7,6},{8,9},{9,8},{10,11... | collective-permute-start | bytes 172040 | tf_op jit(solution)/shard_map/ppermute | solution.py:783
  47.7 8.2 %collective-permute-start.9 = (bf16[14,16,128]{2,1,0:T(8,128)(2,1)S(1)}, bf16[14,16,128]{2,1,0:T(8,128)(2,1)S(1)}, u32[]{:S(2)}, u32[]{:S(2)}) collective-permute-start(bf16[14,16,128]{2,1,0:T(8,128)(2,1)S(1)} %get-tuple-element.69), channel_id=1, source_target_pairs={{1,2},{3,4},{5,6},{7,8},{9,10},{11,12},{13,14},{2,1},{4,3},{6,5},{... | collective-permute-start | bytes 172040 | tf_op jit(solution)/shard_map/ppermute | solution.py:783
  60.4 2.0 %collective-permute-start.10 = (bf16[17,16,128]{2,1,0:T(8,128)(2,1)S(1)}, bf16[17,16,128]{2,1,0:T(8,128)(2,1)S(1)}, u32[]{:S(2)}, u32[]{:S(2)}) collective-permute-start(bf16[17,16,128]{2,1,0:T(8,128)(2,1)S(1)} %get-tuple-element.77), channel_id=1, source_target_pairs={{0,16},{16,0},{32,48},{48,32},{64,80},{80,64},{96,112},{112,96},{1... | collective-permute-start | bytes 208904 | tf_op jit(solution)/shard_map/ppermute | solution.py:783
  60.5 5.6 %collective-permute-start.11 = (bf16[17,16,128]{2,1,0:T(8,128)(2,1)S(1)}, bf16[17,16,128]{2,1,0:T(8,128)(2,1)S(1)}, u32[]{:S(2)}, u32[]{:S(2)}) collective-permute-start(bf16[17,16,128]{2,1,0:T(8,128)(2,1)S(1)} %get-tuple-element.78), channel_id=1, source_target_pairs={{16,32},{48,64},{80,96},{32,16},{64,48},{96,80},{17,33},{49,65},{8... | collective-permute-start | bytes 208904 | tf_op jit(solution)/shard_map/ppermute | solution.py:783
  66.2 5.4 %collective-permute-start.12 = (bf16[6,16,128]{2,1,0:T(8,128)(2,1)S(1)}, bf16[6,16,128]{2,1,0:T(8,128)(2,1)S(1)}, u32[]{:S(2)}, u32[]{:S(2)}) collective-permute-start(bf16[6,16,128]{2,1,0:T(8,128)(2,1)S(1)} %get-tuple-element.81), channel_id=1, source_target_pairs={{0,1},{1,0},{2,3},{3,2},{4,5},{5,4},{6,7},{7,6},{8,9},{9,8},{10,11... | collective-permute-start | bytes 73736 | tf_op jit(solution)/shard_map/ppermute | solution.py:783
  66.3 7.8 %collective-permute-start.13 = (bf16[6,16,128]{2,1,0:T(8,128)(2,1)S(1)}, bf16[6,16,128]{2,1,0:T(8,128)(2,1)S(1)}, u32[]{:S(2)}, u32[]{:S(2)}) collective-permute-start(bf16[6,16,128]{2,1,0:T(8,128)(2,1)S(1)} %get-tuple-element.82), channel_id=1, source_target_pairs={{1,2},{3,4},{5,6},{7,8},{9,10},{11,12},{13,14},{2,1},{4,3},{6,5},{... | collective-permute-start | bytes 73736 | tf_op jit(solution)/shard_map/ppermute | solution.py:783
  76.9 5.6 %collective-permute-start.15 = (bf16[17,16,128]{2,1,0:T(8,128)(2,1)S(1)}, bf16[17,16,128]{2,1,0:T(8,128)(2,1)S(1)}, u32[]{:S(2)}, u32[]{:S(2)}) collective-permute-start(bf16[17,16,128]{2,1,0:T(8,128)(2,1)S(1)} %get-tuple-element.88), channel_id=1, source_target_pairs={{16,32},{48,64},{80,96},{32,16},{64,48},{96,80},{17,33},{49,65},{8... | collective-permute-start | bytes 208904 | tf_op jit(solution)/shard_map/ppermute | solution.py:783
  78.8 3.7 %collective-permute-start.14 = (bf16[17,16,128]{2,1,0:T(8,128)(2,1)S(1)}, bf16[17,16,128]{2,1,0:T(8,128)(2,1)S(1)}, u32[]{:S(2)}, u32[]{:S(2)}) collective-permute-start(bf16[17,16,128]{2,1,0:T(8,128)(2,1)S(1)} %get-tuple-element.87.refs_0_), channel_id=1, source_target_pairs={{0,16},{16,0},{32,48},{48,32},{64,80},{80,64},{96,112},{112,96},{1... | collective-permute-start | bytes 208904 | tf_op jit(solution)/shard_map/ppermute | solution.py:783
  82.6 6.4 %collective-permute-start.16 = (bf16[6,16,128]{2,1,0:T(8,128)(2,1)S(1)}, bf16[6,16,128]{2,1,0:T(8,128)(2,1)S(1)}, u32[]{:S(2)}, u32[]{:S(2)}) collective-permute-start(bf16[6,16,128]{2,1,0:T(8,128)(2,1)S(1)} %get-tuple-element.91), channel_id=1, source_target_pairs={{0,1},{1,0},{2,3},{3,2},{4,5},{5,4},{6,7},{7,6},{8,9},{9,8},{10,11... | collective-permute-start | bytes 73736 | tf_op jit(solution)/shard_map/ppermute | solution.py:783
  83.2 7.8 %collective-permute-start.17 = (bf16[6,16,128]{2,1,0:T(8,128)(2,1)S(1)}, bf16[6,16,128]{2,1,0:T(8,128)(2,1)S(1)}, u32[]{:S(2)}, u32[]{:S(2)}) collective-permute-start(bf16[6,16,128]{2,1,0:T(8,128)(2,1)S(1)} %get-tuple-element.92), channel_id=1, source_target_pairs={{1,2},{3,4},{5,6},{7,8},{9,10},{11,12},{13,14},{2,1},{4,3},{6,5},{... | collective-permute-start | bytes 73736 | tf_op jit(solution)/shard_map/ppermute | solution.py:783
